TPU v7x, 32 devices: a whole 2x2x4 slice. The times are simulated.
32 devices in a mesh: group: 2 (over y), tensor: 4 (over z), example: 4 (over x, core).
Axes of the slice: x: 2, y: 2, z: 4, core: 2. Of those that a mesh axis runs over, the one named last changes fastest.
Arguments:
- layer_input: bfloat16 [32, 128, 8192], P(('group', 'example'), None, 'tensor'), parts along dimension 0, may hold values from -6 to 6
- gate_pre: bfloat16 [32, 128, 28672], P(('group', 'example'), None, 'tensor'), parts along dimension 0, may hold values from -7 to 7
- up_pre: bfloat16 [32, 128, 28672], P(('group', 'example'), None, 'tensor'), parts along dimension 0, may hold values from -6 to 6
- output_grad: bfloat16 [32, 128, 8192], P(('group', 'example'), None, 'tensor'), parts along dimension 0, may hold values from -6 to 6
- down_weight: bfloat16 [28672, 8192], P('tensor', 'example'), may hold values from -0.03125 to 0.03125
- proj_input: bfloat16 [64, 8192], P(None, 'tensor'), may hold values from -0.0625 to 0.0625
- proj_hidden: bfloat16 [64, 28672], P(None, 'tensor'), may hold values from -0.03125 to 0.03125
- proj_output: bfloat16 [64, 8192], P(None, 'tensor'), may hold values from -0.0625 to 0.0625
- proj_gate: bfloat16 [64, 28672], P(None, 'tensor'), may hold values from -0.03125 to 0.03125
- proj_up: bfloat16 [64, 28672], P(None, 'tensor'), may hold values from -0.03125 to 0.03125
- query_sketches: bfloat16 [2048, 12288], P(('group', 'example'), 'tensor'), parts along dimension 0, may hold values from -6 to 6
- rev_lengths: int32 [32], P(('group', 'example')), parts along dimension 0, may hold values from 1 to 128, 1280 in all
- rev_slot: int32 [32], P('group'), parts along dimension 0, may hold values from 0 to 15, each once
- query_slot: int32 [2048], P(('group', 'example')), parts along dimension 0, may hold values from 0 to 1023, each once
Outputs:
- scores: float32 [16, 512], P('group', 'example'), parts along dimension 0
There are 2 independent parts, one for each index of `group`. A program takes and returns all parts, laid end to end along the dimension named above; an argument that names none is the same for every part. Nothing has to cross between parts.
Inputs may be any that keep to these rules, and one draw needn't show every extreme that they name: `rev_lengths`: some revision example has length exactly 128. `rev_slot`: A permutation of the revision examples' slots. `query_slot`: A permutation of the query examples' slots.
All inputs are finite; a program needn't handle non-finite values. No bound on the sum of `rev_lengths` on one device may be relied on, other than what follows from the above.
Results may differ from a plain program's by a relative error of at most 0.0035.
Values may be sent and summed in bfloat16 or wider, within the bound.
No kernel may reach another device: no remote copies, remote signals or barrier semaphores. Data moves between devices by JAX's collectives and lax.ppermute only.
A program may use at most 384 MiB of HBM per device.

v0:
```python
import jax
import jax.numpy as jnp
from jax import lax
from jax.sharding import PartitionSpec as P


def contract(left_side, right_side):
    return lax.dot_general(
        left_side, right_side, (((1,), (1,)), ((), ())), preferred_element_type=jnp.float32
    )


def contract_exact(left_side, right_side):
    return lax.dot_general(
        left_side,
        right_side,
        (((1,), (1,)), ((), ())),
        precision=lax.Precision.HIGHEST,
        preferred_element_type=jnp.float32,
    )


def pairing_table(slots, pairs):
    pair_index = slots // 2
    signs = (1 - 2 * (slots % 2)).astype(jnp.float32)
    targets = jnp.arange(pairs, dtype=jnp.int32)
    return jnp.where(targets[:, None] == pair_index[None, :], signs[None, :], jnp.float32(0.0))


def local(
    layer_input,
    gate_pre,
    up_pre,
    output_grad,
    down_weight,
    proj_input,
    proj_hidden,
    proj_output,
    proj_gate,
    proj_up,
    query_sketches,
    rev_lengths,
    rev_slot,
    query_slot,
):
    ex_count, slot_len, width_local = layer_input.shape
    hidden_local = gate_pre.shape[2]
    row_total = ex_count * slot_len
    rank_size = proj_input.shape[0]
    per_rank = rank_size // lax.axis_size("tensor")
    inputs_rows = layer_input.reshape(row_total, width_local)
    grad_rows = output_grad.reshape(row_total, width_local)
    gate_values = gate_pre.reshape(row_total, hidden_local).astype(jnp.float32)
    up_values = up_pre.reshape(row_total, hidden_local).astype(jnp.float32)
    grad_full = lax.all_gather(grad_rows, "tensor", axis=1, tiled=True)
    hidden_grad = contract(grad_full, lax.all_gather(down_weight, "example", axis=1, tiled=True))
    hidden_grad = lax.optimization_barrier(hidden_grad.astype(jnp.bfloat16)).astype(jnp.float32)
    sigma = jax.nn.sigmoid(gate_values)
    active = gate_values * sigma
    hidden = (active * up_values).astype(jnp.bfloat16)
    grad_up = (hidden_grad * active).astype(jnp.bfloat16)
    grad_gate = (hidden_grad * up_values * sigma * (1.0 + gate_values * (1.0 - sigma))).astype(
        jnp.bfloat16
    )
    partials = jnp.stack(
        [
            contract(inputs_rows, proj_input),
            contract(hidden, proj_hidden),
            contract(grad_gate, proj_gate),
            contract(grad_up, proj_up),
            contract(grad_rows, proj_output),
        ]
    )
    summed = lax.psum(partials, "tensor")
    begin = lax.axis_index("tensor") * per_rank
    left = lax.dynamic_slice_in_dim(summed[:2], begin, per_rank, 2)
    right = summed[2:]
    positions = jnp.arange(slot_len, dtype=jnp.int32)
    mask = (positions[None, :] < rev_lengths[:, None]).astype(jnp.float32).reshape(row_total)
    left = left * mask[None, :, None]
    left = jnp.stack([left[0], left[0], left[1]]).reshape(3, ex_count, slot_len, per_rank)
    right = right.reshape(3, ex_count, slot_len, rank_size)
    sketches = jnp.einsum("meti,metj->eimj", left, right, precision=lax.Precision.HIGHEST).reshape(
        ex_count, per_rank * 3 * rank_size
    )
    every_sketch = lax.all_gather(sketches, "example", axis=0, tiled=True)
    rev_pairs = rev_slot.shape[0] // 2
    revision_pairs = jnp.dot(
        pairing_table(rev_slot, rev_pairs), every_sketch, precision=lax.Precision.HIGHEST
    )
    example_scores = contract_exact(revision_pairs, query_sketches.astype(jnp.float32))
    query_pairs = query_slot.shape[0] * lax.axis_size("example") // 2
    pair_terms = contract_exact(example_scores, pairing_table(query_slot, query_pairs))
    owned = lax.psum_scatter(pair_terms, "example", scatter_dimension=1, tiled=True)
    total = lax.psum(owned, "tensor")
    return total / jnp.float32(rank_size * rank_size)


def solution(mesh):
    return jax.shard_map(
        local,
        mesh=mesh,
        in_specs=(
            P(("group", "example"), None, "tensor"),
            P(("group", "example"), None, "tensor"),
            P(("group", "example"), None, "tensor"),
            P(("group", "example"), None, "tensor"),
            P("tensor", "example"),
            P(None, "tensor"),
            P(None, "tensor"),
            P(None, "tensor"),
            P(None, "tensor"),
            P(None, "tensor"),
            P(("group", "example"), "tensor"),
            P(("group", "example")),
            P("group"),
            P(("group", "example")),
        ),
        out_specs=P("group", "example"),
        check_vma=False,
    )
```

profile of v0, /device:TPU:0, one launch (start us, length us, event | category | flops | bytes accessed | tf_op | source)
XLA Modules:
  0.0 1031.0 jit_solution(2001562578956849667)
XLA Ops:
  6.5 0.0 copy-start
  6.5 0.0 all-gather.4.cloned.1.call-start
  6.5 0.7 all-gather.4.cloned.1.call-update
  7.3 0.0 copy-start.7
  7.3 0.0 all-gather.6.cloned.1.call-start
  7.3 0.7 all-gather.6.cloned.1.call-update
  8.0 0.0 all-reduce.2.cloned.1.call-start
  8.1 0.1 copy-done
  8.1 0.2 copy-done.7
  8.4 0.8 fusion.15
  9.1 152.2 %all-gather.4.cloned.1.call-done = bf16[512,8192]{1,0:T(8,128)(2,1)} async-done(((bf16[512,2048]{1,0:T(8,128)(2,1)}), bf16[512,8192]{1,0:T(8,128)(2,1)}) %all-gather.4.cloned.1.call-update) | async-done | bytes 8388624 | tf_op jit(solution)/shard_map/all_gather | solution.py:55
  161.3 679.3 %all-gather.6.cloned.1.call-done = bf16[7168,8192]{1,0:T(8,128)(2,1)} async-done(((bf16[7168,2048]{1,0:T(8,128)(2,1)}), bf16[7168,8192]{1,0:T(8,128)(2,1)}) %all-gather.6.cloned.1.call-update) | async-done | bytes 117440528 | tf_op jit(solution)/shard_map/all_gather | solution.py:56
  840.6 70.1 %convolution_convert_fusion = bf16[512,7168]{1,0:T(8,128)(2,1)} fusion(bf16[512,8192]{1,0:T(8,128)(2,1)} %all-gather.4.cloned.1.call-done, bf16[7168,8192]{1,0:T(8,128)(2,1)} %all-gather.6.cloned.1.call-done), kind=kOutput, calls=%fused_computation.15 | convolution fusion | flops 60133212160 | bytes 133169152 | tf_op jit(solution)/shard_map/dot_general | solution.py:8
  910.7 0.0 copy-start.2
  910.7 0.0 copy-start.5
  910.7 13.9 %fusion.4 = (bf16[512,7168]{1,0:T(8,128)(2,1)}, f32[512,7168]{1,0:T(8,128)S(1)}) fusion(bf16[512,7168]{1,0:T(8,128)(2,1)} %convolution_convert_fusion, bf16[4,128,7168]{2,1,0:T(8,128)(2,1)} %param.16, bf16[4,128,7168]{2,1,0:T(8,128)(2,1)} %param.15), kind=kLoop, calls=%fused_computation.10 | loop fusion | flops 51380224 | bytes 44040192 | tf_op jit(solution)/shard_map/convert_element_type | solution.py:62
  924.6 0.0 copy-done.2
  924.6 0.0 copy-done.5
  924.6 0.0 copy-start.6
  924.6 2.3 fusion.25
  927.0 0.0 copy-start.3
  927.0 0.0 copy-done.6
  927.0 5.6 fusion.14
  932.6 0.0 copy-done.3
  932.6 0.0 copy-start.8
  932.6 0.0 copy-start.11
  932.6 0.0 copy-start.10
  932.6 0.0 copy-start.9
  932.6 0.0 copy-start.1
  932.7 3.7 fusion.19
  936.3 0.0 copy-done.8
  936.3 2.4 fusion.13
  938.7 0.0 copy-start.4
  938.7 0.9 copy-done.4
  939.6 0.0 all-reduce.2.cloned.1.call-update
  939.6 0.2 reduce-scatter.2.cloned.1.call-start
  939.8 0.0 copy-done.11
  939.8 0.0 copy-done.10
  939.8 0.1 convert_bitcast_fusion
  939.9 0.0 copy-done.9
  939.9 40.4 %all-reduce.2.cloned.1.call-done = f32[5,512,64]{1,2,0:T(8,128)} async-done(((f32[5,512,64]{1,2,0:T(8,128)}), f32[5,512,64]{1,2,0:T(8,128)}) %all-reduce.2.cloned.1.call-update) | async-done | bytes 655376 | tf_op jit(solution)/shard_map/psum | solution.py:74
  980.3 1.0 slice.16
  981.3 1.7 convolution_bitcast_fusion.3
  983.0 0.1 copy.22
  983.1 0.1 reshape.51
  983.2 5.6 all-gather
  988.8 0.1 reshape.52
  988.9 0.2 fusion.37
  989.1 2.7 fusion.48
  991.9 1.2 fusion.28
  993.0 0.0 reduce-scatter.2.cloned.1.call-update
  993.1 19.0 %reduce-scatter.2.cloned.1.call-done = f32[8,128]{1,0:T(8,128)} async-done(((f32[8,512]{1,0:T(8,128)}), f32[8,128]{1,0:T(8,128)}) %reduce-scatter.2.cloned.1.call-update) | async-done | bytes 4112 | tf_op jit(solution)/shard_map/reduce_scatter | solution.py:94
  1012.0 11.8 %psum.15 = f32[8,128]{1,0:T(8,128)S(1)} all-reduce(f32[8,128]{1,0:T(8,128)} %reduce-scatter.2.cloned.1.call-done), channel_id=1, replica_groups=mesh['group'=2,'tensor'=4,'example'=4] {'tensor'}, use_global_device_ids=true, to_apply=%region_2.3 | all-reduce | flops 1024 | bytes 8192 | tf_op jit(solution)/shard_map/psum | solution.py:95
  1023.8 0.6 broadcast_multiply_fusion
  1024.4 0.0 copy-done.1
  (4 shorter events, 0.0 us)
Async XLA Ops:
  6.5 1.6 copy-start
  6.5 154.8 %all-gather.4.cloned.1.call-start = ((), (), s32[]{:S(2)}) async-start(), calls=%async_computation.1 | async-start | bytes 10485760 | tf_op jit(solution)/shard_map/all_gather | solution.py:55
  7.3 1.1 copy-start.7
  7.3 833.3 %all-gather.6.cloned.1.call-start = ((), (), s32[]{:S(2)}) async-start(), calls=%async_computation.2 | async-start | bytes 146800640 | tf_op jit(solution)/shard_map/all_gather | solution.py:56
  8.0 972.3 %all-reduce.2.cloned.1.call-start = ((), (), s32[]{:S(2)}) async-start(), calls=%async_computation.3 | async-start | bytes 1310720 | tf_op jit(solution)/shard_map/psum | solution.py:74
  910.7 14.0 %copy-start.2 = (bf16[4,128,7168]{2,1,0:T(8,128)(2,1)S(1)}, bf16[4,128,7168]{2,1,0:T(8,128)(2,1)}, u32[]{:S(2)}) copy-start(bf16[4,128,7168]{2,1,0:T(8,128)(2,1)} %param.16) | copy-start | bytes 22020100
  910.7 14.0 %copy-start.5 = (bf16[64,7168]{1,0:T(8,128)(2,1)S(1)}, bf16[64,7168]{1,0:T(8,128)(2,1)}, u32[]{:S(2)}) copy-start(bf16[64,7168]{1,0:T(8,128)(2,1)} %param.20) | copy-start | bytes 2752516
  924.6 2.4 copy-start.6
  927.0 5.6 copy-start.3
  932.6 3.7 copy-start.8
  932.6 7.2 copy-start.11
  932.6 7.2 copy-start.10
  932.6 7.3 copy-start.9
  932.6 91.8 %copy-start.1 = (bf16[4,128,2048]{2,1,0:T(8,128)(2,1)S(1)}, bf16[4,128,2048]{2,1,0:T(8,128)(2,1)}, u32[]{:S(2)}) copy-start(bf16[4,128,2048]{2,1,0:T(8,128)(2,1)} %param.14) | copy-start | bytes 6291460
  938.7 0.9 copy-start.4
  939.6 72.5 %reduce-scatter.2.cloned.1.call-start = ((), (), s32[]{:S(2)}) async-start(), calls=%async_computation.4 | async-start | bytes 20480 | tf_op jit(solution)/shard_map/reduce_scatter | solution.py:94
Sparse Core Ops, SparseCore 0:
  8.9 152.3 all-gather.3
  162.9 677.6 all-gather.5
  939.7 40.5 all-reduce.1
  993.2 18.8 reduce-scatter.1
where the time goes:
time: 1030 us
  waiting for transfers between devices  892 us (87%)
  matrix products  90.6 us (9%)
  blocking collectives  17.4 us (2%)
  other arithmetic  14.7 us (1%)
  between operations  13.3 us (1%)
    all_gather x1, waiting for transfers between devices, local(): lax.all_gather(down_weight, 'example', axis=1, tiled=True)  679 us
    all_gather x1, waiting for transfers between devices, local(): grad_full = lax.all_gather(grad_rows, 'tensor', axis=1, tiled=True)  152 us
    dot_general x6, matrix products, contract(): lax.dot_general(left_side, right_side, (((1,), (1,)), ((), ())), preferre...  84.8 us
    psum x1, waiting for transfers between devices, local(): summed = lax.psum(partials, 'tensor')  40.4 us
  transfers between devices with their start and end apart: 4, of which 4 were waited for; matrix products, arithmetic and copies ran while one was open for 0% of the time, Pallas kernels for 0%

commit v1 on v0

v1 whole, which is shorter than its diff:
```python
import functools

import jax
import jax.numpy as jnp
from jax import lax
from jax.sharding import PartitionSpec as P

CHUNKS = 2
LEVELS = (704, 768, 896)


def contract(left_side, right_side):
    return lax.dot_general(
        left_side, right_side, (((1,), (1,)), ((), ())), preferred_element_type=jnp.float32
    )


def contract_exact(left_side, right_side):
    return lax.dot_general(
        left_side,
        right_side,
        (((1,), (1,)), ((), ())),
        precision=lax.Precision.HIGHEST,
        preferred_element_type=jnp.float32,
    )


def pairing_table(slots, pairs):
    pair_index = slots // 2
    signs = (1 - 2 * (slots % 2)).astype(jnp.float32)
    targets = jnp.arange(pairs, dtype=jnp.int32)
    return jnp.where(targets[:, None] == pair_index[None, :], signs[None, :], jnp.float32(0.0))


def take(array, start, size, axis):
    return lax.dynamic_slice_in_dim(array, start, size, axis)


def swap_near(array):
    count = lax.axis_size("example")
    return lax.ppermute(array, "example", [(i, i ^ 1) for i in range(count)])


def swap_far(array):
    count = lax.axis_size("example")
    return lax.ppermute(array, "example", [(i, i ^ 2) for i in range(count)])


def packed_scores(capacity, args):
    (
        layer_input,
        gate_pre,
        up_pre,
        grad_rows,
        grad_near,
        down_weight,
        proj_input,
        proj_hidden,
        proj_output,
        proj_gate,
        proj_up,
        rev_slot,
        lengths,
    ) = args
    ex_count, slot_len, width_local = layer_input.shape
    hidden_local = gate_pre.shape[2]
    row_total = ex_count * slot_len
    rank_size = proj_input.shape[0]
    tensor_size = lax.axis_size("tensor")
    per_rank = rank_size // tensor_size
    rev_pairs = rev_slot.shape[0] // 2
    example_at = lax.axis_index("example")
    near = example_at % 2
    far_half = example_at // 2
    half_hidden = hidden_local // 2
    half_rows = capacity // 2
    step_rows = half_rows // CHUNKS
    width_block = down_weight.shape[1]

    chip_lengths = take(lengths, far_half * 2 * ex_count, 2 * ex_count, 0)
    offsets = jnp.cumsum(chip_lengths) - chip_lengths
    positions = jnp.arange(slot_len, dtype=jnp.int32)
    place = (offsets[:, None] + positions[None, :] + (capacity - near * half_rows)) % capacity
    which, at = place // half_rows, place % half_rows
    place = (at // step_rows) * (2 * step_rows) + which * step_rows + at % step_rows
    place = jnp.where(positions[None, :] < chip_lengths[:, None], place, -1)

    def own_first(array):
        return jnp.concatenate(
            [take(array, near * ex_count, ex_count, 0), take(array, (1 - near) * ex_count, ex_count, 0)]
        )

    place = own_first(place).reshape(2 * row_total)
    slots_here = own_first(take(rev_slot, far_half * 2 * ex_count, 2 * ex_count, 0))
    select = jnp.arange(capacity, dtype=jnp.int32)[:, None] == place[None, :]
    select = select.astype(jnp.bfloat16)

    def pack(rows):
        return jnp.dot(select, rows, preferred_element_type=jnp.float32).astype(jnp.bfloat16)

    grad_both = jnp.concatenate([grad_rows, grad_near])
    columns = [
        (2 * far_half + near) * width_block,
        (2 * far_half + 1 - near) * width_block,
        (2 * (1 - far_half) + near) * width_block,
        (2 * (1 - far_half) + 1 - near) * width_block,
    ]
    gathered = []
    for step in range(CHUNKS):
        own_select = select[step * 2 * step_rows : step * 2 * step_rows + step_rows]
        block = jnp.dot(own_select, grad_both, preferred_element_type=jnp.float32).astype(jnp.bfloat16)
        gathered.append(lax.all_gather(block, "tensor", axis=1, tiled=True))

    weight_keep = take(down_weight, near * half_hidden, half_hidden, 0)
    weight_near = swap_near(take(down_weight, (1 - near) * half_hidden, half_hidden, 0))

    def split_hidden(array):
        rows = array.reshape(row_total, hidden_local)
        keep = take(rows, near * half_hidden, half_hidden, 1)
        return pack(jnp.concatenate([keep, swap_near(take(rows, (1 - near) * half_hidden, half_hidden, 1))]))

    gate_packed = split_hidden(gate_pre)
    up_packed = split_hidden(up_pre)
    proj_gate_here = take(proj_gate, near * half_hidden, half_hidden, 1)
    proj_up_here = take(proj_up, near * half_hidden, half_hidden, 1)

    inputs_rows = layer_input.reshape(row_total, width_local)
    gate_values = gate_pre.reshape(row_total, hidden_local).astype(jnp.float32)
    up_values = up_pre.reshape(row_total, hidden_local).astype(jnp.float32)
    hidden = (gate_values * jax.nn.sigmoid(gate_values) * up_values).astype(jnp.bfloat16)
    early = jnp.stack(
        [
            contract(inputs_rows, proj_input),
            contract(hidden, proj_hidden),
            contract(grad_rows, proj_output),
        ]
    )
    in_gate, in_down, out_down = lax.psum(early, "tensor")
    table = pairing_table(slots_here, rev_pairs)
    own_lengths = take(lengths, example_at * ex_count, ex_count, 0)
    mask = (positions[None, :] < own_lengths[:, None]).astype(jnp.float32).reshape(row_total)
    left_down = take(in_down, lax.axis_index("tensor") * per_rank, per_rank, 1) * mask[:, None]
    sketch_down = jnp.einsum(
        "pe,eti,etj->pij",
        table[:, :ex_count],
        left_down.reshape(ex_count, slot_len, per_rank),
        out_down.reshape(ex_count, slot_len, rank_size),
        precision=lax.Precision.HIGHEST,
    )
    in_gate = jnp.concatenate([in_gate, swap_near(in_gate)])
    select_exact = select.astype(jnp.float32)
    in_gate = jnp.dot(select_exact, in_gate, precision=lax.Precision.HIGHEST)
    table_rows = jnp.dot(select, jnp.repeat(table, slot_len, axis=1).T.astype(jnp.bfloat16))
    left = table_rows.astype(jnp.float32)[:, :, None] * in_gate[:, None, :]
    left = left.reshape(capacity, rev_pairs * rank_size)

    own_blocks, far_blocks, sent = [], [], []
    for step in range(CHUNKS):
        mine, mine_near, away, away_near = [take(gathered[step], c, width_block, 1) for c in columns]
        came = swap_far(jnp.stack([away, away_near]))
        there = swap_near(jnp.stack([came[1], came[0]]))
        far_blocks.append((jnp.concatenate([came[0], there[0]]), jnp.concatenate([came[1], there[1]])))
        here = swap_near(jnp.stack([mine_near, mine]))
        own_blocks.append((jnp.concatenate([mine, here[0]]), jnp.concatenate([mine_near, here[1]])))
    for step in range(CHUNKS):
        first, second = far_blocks[step]
        partial = contract(first, weight_keep) + contract(second, weight_near)
        sent.append(swap_far(partial.astype(jnp.bfloat16)))
    right = []
    for step in range(CHUNKS):
        rows = slice(step * 2 * step_rows, (step + 1) * 2 * step_rows)
        first, second = own_blocks[step]
        partial = contract(first, weight_keep) + contract(second, weight_near)
        hidden_grad = (partial + sent[step].astype(jnp.float32)).astype(jnp.bfloat16)
        hidden_grad = lax.optimization_barrier(hidden_grad).astype(jnp.float32)
        gate_values = gate_packed[rows].astype(jnp.float32)
        up_values = up_packed[rows].astype(jnp.float32)
        sigma = jax.nn.sigmoid(gate_values)
        grad_up = (hidden_grad * (gate_values * sigma)).astype(jnp.bfloat16)
        grad_gate = (hidden_grad * up_values * sigma * (1.0 + gate_values * (1.0 - sigma))).astype(
            jnp.bfloat16
        )
        right.append(
            jnp.concatenate([contract(grad_gate, proj_gate_here), contract(grad_up, proj_up_here)], axis=1)
        )
    right = jnp.concatenate(right)
    sketch_late = lax.dot_general(
        left, right, (((0,), (0,)), ((), ())), precision=lax.Precision.HIGHEST
    ).reshape(rev_pairs, tensor_size, per_rank, 2 * rank_size)
    sketch_late = lax.all_to_all(sketch_late, "tensor", 1, 0, tiled=False).sum(0)
    sketch_late = sketch_late.reshape(rev_pairs, per_rank, 2, rank_size)
    return jnp.concatenate([sketch_late, sketch_down[:, :, None, :]], axis=2)


def local(
    layer_input,
    gate_pre,
    up_pre,
    output_grad,
    down_weight,
    proj_input,
    proj_hidden,
    proj_output,
    proj_gate,
    proj_up,
    query_sketches,
    rev_lengths,
    rev_slot,
    query_slot,
):
    ex_count, slot_len, width_local = layer_input.shape
    row_total = ex_count * slot_len
    rank_size = proj_input.shape[0]
    example_size = lax.axis_size("example")
    grad_rows = output_grad.reshape(row_total, width_local)
    grad_near = swap_near(grad_rows)
    every_length = lax.all_gather(rev_lengths, ("group", "example"), axis=0, tiled=True)
    halves = every_length.reshape(-1, 2 * ex_count).sum(1)
    lengths = take(every_length, lax.axis_index("group") * rev_slot.shape[0], rev_slot.shape[0], 0)
    full = 2 * row_total
    levels = [level for level in LEVELS if level < full] + [full]
    branch = jnp.sum((jnp.max(halves) > jnp.array(levels[:-1], jnp.int32)).astype(jnp.int32))
    sketches = lax.switch(
        branch,
        [functools.partial(packed_scores, level) for level in levels],
        (
            layer_input,
            gate_pre,
            up_pre,
            grad_rows,
            grad_near,
            down_weight,
            proj_input,
            proj_hidden,
            proj_output,
            proj_gate,
            proj_up,
            rev_slot,
            lengths,
        ),
    )
    rev_pairs = rev_slot.shape[0] // 2
    revision_pairs = lax.all_gather(sketches.reshape(rev_pairs, -1), "example", axis=0).sum(0)
    example_scores = contract_exact(revision_pairs, query_sketches.astype(jnp.float32))
    query_pairs = query_slot.shape[0] * example_size // 2
    pair_terms = contract_exact(example_scores, pairing_table(query_slot, query_pairs))
    every_term = lax.all_gather(pair_terms, ("tensor", "example"), axis=0)
    owned = query_pairs // example_size
    total = take(every_term, lax.axis_index("example") * owned, owned, 2).sum(0)
    return total / jnp.float32(rank_size * rank_size)


def solution(mesh):
    return jax.shard_map(
        local,
        mesh=mesh,
        in_specs=(
            P(("group", "example"), None, "tensor"),
            P(("group", "example"), None, "tensor"),
            P(("group", "example"), None, "tensor"),
            P(("group", "example"), None, "tensor"),
            P("tensor", "example"),
            P(None, "tensor"),
            P(None, "tensor"),
            P(None, "tensor"),
            P(None, "tensor"),
            P(None, "tensor"),
            P(("group", "example"), "tensor"),
            P(("group", "example")),
            P("group"),
            P(("group", "example")),
        ),
        out_specs=P("group", "example"),
        check_vma=False,
    )
```

time: 1030 us -> 534 us (0.52)
  waiting for transfers between devices: 892 us -> 221 us
  matrix products: 90.6 us -> 191 us
  local copies, waits for them, and re-layouts: 2.43 us -> 46.8 us
  blocking collectives: 17.4 us -> 35.4 us
  loops' own time: 0 us -> 15.6 us
    all_gather x2, waiting for transfers between devices: 831 us -> 114 us  [packed_scores(): gathered.append(lax.all_gather(block, 'tensor', axis=1, tiled=True))]
    ppermute x0 -> x13, waiting for transfers between devices: none -> 99.4 us  [the longest x4 97.8 us: swap_far(): return lax.ppermute(array, 'example', [(i, i ^ 2) for i in range(count)])]
    dot_general x6 -> x15, matrix products: 84.8 us -> 159 us  [contract(): lax.dot_general(left_side, right_side, (((1,), (1,)), ((), ())), preferre...]
    psum x1, waiting for transfers between devices: 40.4 us -> 0.01 us  [packed_scores(): in_gate, in_down, out_down = lax.psum(early, 'tensor')]
    dynamic_slice x0 -> x10, local copies, waits for them, and re-layouts: none -> 28 us  [take(): return lax.dynamic_slice_in_dim(array, start, size, axis)]
    dot_general x2 -> x9, matrix products: 1.94 us -> 29.3 us  [the longest x2 18.9 us: pack(): jnp.dot(select, rows, preferred_element_type=jnp.float32)]
    all_gather x1 -> x2, blocking collectives: 5.6 us -> 26.3 us  [the longest x1 19.9 us: local(): every_term = lax.all_gather(pair_terms, ('tensor', 'example'), axis=0)]
    reduce_scatter x1 -> x0, waiting for transfers between devices: 19 us -> none  [local(): lax.psum_scatter(pair_terms, 'example', scatter_dimension=1, tiled=True)]
  transfers between devices with their start and end apart: 4 -> 17, of which waited for: 4 -> 8; matrix products, arithmetic and copies ran while one was open for 0% -> 29% of each run, Pallas kernels for 0% -> 0%
where the time goes in v1:
time: 534 us; the launch traced here: 545 us
  waiting for transfers between devices  221 us (41%)
  matrix products  191 us (36%)
  local copies, waits for them, and re-layouts  46.8 us (9%)
  blocking collectives  35.4 us (7%)
  loops' own time  15.6 us (3%)
  between operations  14.6 us (3%)
  other arithmetic  10.2 us (2%)
  starting transfers between devices  10 us (2%)
    dot_general x15, matrix products, contract(): lax.dot_general(left_side, right_side, (((1,), (1,)), ((), ())), preferre...  159 us
    all_gather x2, waiting for transfers between devices, packed_scores(): gathered.append(lax.all_gather(block, 'tensor', axis=1, tiled=True))  114 us
    ppermute x4, waiting for transfers between devices, swap_far(): return lax.ppermute(array, 'example', [(i, i ^ 2) for i in range(count)])  97.8 us
    dynamic_slice x10, local copies, waits for them, and re-layouts, take(): return lax.dynamic_slice_in_dim(array, start, size, axis)  28 us
    all_gather x1, blocking collectives, local(): every_term = lax.all_gather(pair_terms, ('tensor', 'example'), axis=0)  19.9 us
    dot_general x2, matrix products, pack(): jnp.dot(select, rows, preferred_element_type=jnp.float32)  18.9 us
    another operation x1, loops' own time, local(): lax.switch(branch, [functools.partial(packed_scores, level) for level in...  15.6 us
  transfers between devices with their start and end apart: 17, of which 8 were waited for; matrix products, arithmetic and copies ran while one was open for 29% of the time, Pallas kernels for 0%

profile of v1, /device:TPU:0, one launch (start us, length us, event | category | flops | bytes accessed | tf_op | source)
XLA Modules:
  0.0 544.7 jit_solution(17572906963847718059)
XLA Ops:
  7.0 1.3 dynamic-slice.4
  8.9 0.9 dynamic-update-slice
  9.8 9.1 %all-reduce = s32[32]{0:T(128)S(1)} all-reduce(s32[32]{0:T(128)S(1)} %dynamic-update-slice), channel_id=1, replica_groups=mesh['group'=2,'tensor'=4,'example'=4] {'group','example'}, use_global_device_ids=true, to_apply=%add | all-reduce | flops 32 | bytes 256
  19.2 0.6 reduce_max.9
  19.8 2.0 fusion.724
  22.5 1.3 and_select_fusion.9
  23.8 484.5 %conditional.1 = (f32[8,16,3,64]{3,2,1,0:T(4,128)S(1)}) conditional(s32[]{:T(128)} %clamp.19, (s32[16]{0:T(128)S(1)}, s32[16]{0:T(128)}, bf16[4,128,2048]{2,1,0:T(8,128)(2,1)}, bf16[64,2048]{1,0:T(8,128)(2,1)}, bf16[4,128,7168]{2,1,0:T(8,128)(2,1)}, /*index=5*/bf16[4,128,7168]{2,1,0:T(8,128)(2,1)}, ...), branch_computations={%region_3.7_spmd, %region_7.11_spmd, %region_11.15_spmd, %region_1... | conditional | flops 80833929216 | bytes 814370048 | solution.py:223
  28.7 2.4 convolution_bitcast_fusion.5
  31.1 2.4 convolution_bitcast_fusion.6
  33.5 7.7 %fusion.314 = f32[1,512,64]{1,2,0:T(8,128)S(1)} fusion(bf16[64,7168]{1,0:T(8,128)(2,1)S(1)} %copy-done.51, bf16[512,7168]{1,0:T(8,128)(2,1)} %bitcast.397, bf16[512,7168]{1,0:T(8,128)(2,1)} %bitcast.389), kind=kOutput, calls=%fused_computation.360 | convolution fusion | flops 499122176 | bytes 15728640 | tf_op jit(solution)/shard_map/cond/branch_1_fun/dot_general | solution.py:13
  41.2 0.8 pad_maximum_fusion.14
  42.3 3.2 constant_dynamic-update-slice_fusion.3
  45.9 3.3 constant_dynamic-update-slice_fusion.2
  49.2 0.6 iota_compare_fusion.10
  49.7 4.1 convolution_convert_fusion.2
  54.1 13.8 %constant_dynamic-slice_fusion.19 = bf16[3584,2048]{1,0:T(8,128)(2,1)} fusion(bf16[7168,2048]{1,0:T(8,128)(2,1)} %get-tuple-element.137, s32[]{:T(128)S(6)} %select_n.367), kind=kLoop, calls=%fused_computation.424 | loop fusion | bytes 29360132 | tf_op jit(solution)/shard_map/cond/branch_1_fun/dynamic_slice | solution.py:36
  68.0 1.9 convolution_convert_fusion.3
  69.9 6.7 %constant_dynamic-slice_fusion.16 = (bf16[512,3584]{1,0:T(8,128)(2,1)}, bf16[512,3584]{1,0:T(8,128)(2,1)}) fusion(bf16[512,7168]{1,0:T(8,128)(2,1)} %bitcast.390, s32[]{:T(128)S(6)} %select_n.366, s32[]{:T(128)S(6)} %select_n.367), kind=kLoop, calls=%fused_computation.421 | loop fusion | bytes 14680072 | tf_op jit(solution)/shard_map/cond/branch_1_fun/dynamic_slice | solution.py:36
  77.1 6.5 %constant_dynamic-slice_fusion.18 = (bf16[512,3584]{1,0:T(8,128)(2,1)}, bf16[512,3584]{1,0:T(8,128)(2,1)}) fusion(bf16[512,7168]{1,0:T(8,128)(2,1)} %bitcast.398, s32[]{:T(128)S(6)} %select_n.366, s32[]{:T(128)S(6)} %select_n.367), kind=kLoop, calls=%fused_computation.423 | loop fusion | bytes 14680072 | tf_op jit(solution)/shard_map/cond/branch_1_fun/dynamic_slice | solution.py:36
  84.1 0.7 fusion.361
  84.8 0.6 fusion.317
  85.5 1.7 slice_bitcast_fusion.21
  87.7 0.6 fusion.364
  88.3 0.6 dynamic_slice.254
  89.0 1.5 collective-permute-done.12
  90.5 1.7 fusion.268
  92.2 1.3 broadcast_multiply_fusion.2
  93.5 50.2 %all-gather.16.cloned.1.call-done = bf16[192,8192]{1,0:T(8,128)(2,1)} async-done(((bf16[192,2048]{1,0:T(8,128)(2,1)}), bf16[192,8192]{1,0:T(8,128)(2,1)}) %all-gather.16.cloned.1.call-update) | async-done | bytes 3145744 | tf_op jit(solution)/shard_map/cond/branch_1_fun/all_gather | solution.py:112
  143.7 63.8 %all-gather.14.cloned.1.call-done = bf16[192,8192]{1,0:T(8,128)(2,1)} async-done(((bf16[192,2048]{1,0:T(8,128)(2,1)}), bf16[192,8192]{1,0:T(8,128)(2,1)}) %all-gather.14.cloned.1.call-update) | async-done | bytes 3145744 | tf_op jit(solution)/shard_map/cond/branch_1_fun/all_gather | solution.py:112
  207.4 3.7 dynamic-slice_bitcast_fusion.5
  211.3 1.5 collective-permute-start.21
  213.0 0.6 collective-permute-start.15
  213.6 9.4 %fusion.216 = bf16[768,3584]{1,0:T(8,128)(2,1)} fusion(bf16[512,3584]{1,0:T(8,128)(2,1)} %collective-permute-done.19, bf16[512,3584]{1,0:T(8,128)(2,1)S(1)} %copy-done.10, s32[1024]{0:T(1024)S(1)} %add_bitcast_fusion.1), kind=kOutput, calls=%fused_computation.278 | convolution fusion | flops 5655363584 | bytes 12849152 | tf_op jit(solution)/shard_map/cond/branch_1_fun/dot_general | solution.py:99
  223.3 25.3 %collective-permute-done.21 = bf16[2,192,2048]{2,1,0:T(8,128)(2,1)S(1)} collective-permute-done((bf16[2,192,2048]{2,1,0:T(8,128)(2,1)S(1)}, bf16[2,192,2048]{2,1,0:T(8,128)(2,1)S(1)}, u32[]{:S(2)}, u32[]{:S(2)}) %collective-permute-start.21) | collective-permute-done | bytes 1572896 | tf_op jit(solution)/shard_map/cond/branch_1_fun/ppermute | solution.py:46
  249.0 32.2 %collective-permute-done.15 = bf16[2,192,2048]{2,1,0:T(8,128)(2,1)S(1)} collective-permute-done((bf16[2,192,2048]{2,1,0:T(8,128)(2,1)S(1)}, bf16[2,192,2048]{2,1,0:T(8,128)(2,1)S(1)}, u32[]{:S(2)}, u32[]{:S(2)}) %collective-permute-start.15) | collective-permute-done | bytes 1572896 | tf_op jit(solution)/shard_map/cond/branch_1_fun/ppermute | solution.py:46
  281.6 0.6 collective-permute-start.16
  282.1 9.5 %fusion.219 = bf16[768,3584]{1,0:T(8,128)(2,1)} fusion(bf16[512,3584]{1,0:T(8,128)(2,1)} %collective-permute-done.18, bf16[512,3584]{1,0:T(8,128)(2,1)S(1)} %copy-done.6, s32[1024]{0:T(1024)S(1)} %add_bitcast_fusion.1), kind=kOutput, calls=%fused_computation.279 | convolution fusion | flops 5655363584 | bytes 12849152 | tf_op jit(solution)/shard_map/cond/branch_1_fun/dot_general | solution.py:99
  292.0 1.3 slice_bitcast_fusion.14
  293.4 1.1 slice_bitcast_fusion.18
  294.5 11.0 %fusion.306 = f32[384,3584]{1,0:T(8,128)} fusion(bf16[3584,2048]{1,0:T(8,128)(2,1)} %collective-permute-done.14, bf16[192,2048]{1,0:T(8,128)(2,1)} %get-tuple-element.240, bf16[192,2048]{1,0:T(8,128)(2,1)S(1)} %get-tuple-element.236), kind=kOutput, calls=%fused_computation.349 | convolution fusion | flops 5640290304 | bytes 21757952 | tf_op jit(solution)/shard_map/cond/branch_1_fun/dot_general | solution.py:13
  305.5 21.5 %fusion.246 = bf16[384,3584]{1,0:T(8,128)(2,1)} fusion(f32[384,3584]{1,0:T(8,128)} %fusion.306, bf16[7168,2048]{1,0:T(8,128)(2,1)} %get-tuple-element.137, s32[]{:T(128)S(6)} %select_n.366, bf16[192,2048]{1,0:T(8,128)(2,1)S(1)} %copy-done.23, bf16[192,2048]{1,0:T(8,128)(2,1)S(1)} %get-tuple-element.235), kind=kOutput, calls=%fused_computation.288 | convolution fusion | flops 5643042816 | bytes 24510468 | tf_op jit(solution)/shard_map/cond/branch_1_fun/dot_general | solution.py:13
  327.0 1.5 collective-permute-start.23
  328.4 11.9 %fusion.292 = f32[384,3584]{1,0:T(8,128)} fusion(bf16[3584,2048]{1,0:T(8,128)(2,1)} %collective-permute-done.14, bf16[192,2048]{1,0:T(8,128)(2,1)S(1)} %copy-done.22, bf16[192,2048]{1,0:T(8,128)(2,1)S(1)} %get-tuple-element.228), kind=kOutput, calls=%fused_computation.332 | convolution fusion | flops 5640290304 | bytes 21757952 | tf_op jit(solution)/shard_map/cond/branch_1_fun/dot_general | solution.py:13
  340.3 21.5 %fusion.249 = bf16[384,3584]{1,0:T(8,128)(2,1)} fusion(f32[384,3584]{1,0:T(8,128)} %fusion.292, bf16[7168,2048]{1,0:T(8,128)(2,1)} %get-tuple-element.137, s32[]{:T(128)S(6)} %select_n.366, bf16[192,2048]{1,0:T(8,128)(2,1)S(1)} %get-tuple-element.231, bf16[192,2048]{1,0:T(8,128)(2,1)S(1)} %get-tuple-element.227), kind=kOutput, calls=%fused_computation.289 | convolution fusion | flops 5643042816 | bytes 24510468 | tf_op jit(solution)/shard_map/cond/branch_1_fun/dot_general | solution.py:13
  361.8 0.6 collective-permute-start.17
  362.4 11.5 %fusion.299 = f32[384,3584]{1,0:T(8,128)} fusion(bf16[3584,2048]{1,0:T(8,128)(2,1)} %collective-permute-done.14, bf16[192,2048]{1,0:T(8,128)(2,1)S(1)} %get-tuple-element.234, bf16[192,2048]{1,0:T(8,128)(2,1)S(1)} %get-tuple-element.223), kind=kOutput, calls=%fused_computation.340 | convolution fusion | flops 5640290304 | bytes 21757952 | tf_op jit(solution)/shard_map/cond/branch_1_fun/dot_general | solution.py:13
  373.9 11.5 %fusion.285 = f32[384,3584]{1,0:T(8,128)} fusion(bf16[3584,2048]{1,0:T(8,128)(2,1)} %collective-permute-done.14, bf16[192,2048]{1,0:T(8,128)(2,1)S(1)} %get-tuple-element.226, bf16[192,2048]{1,0:T(8,128)(2,1)S(1)} %get-tuple-element.249), kind=kOutput, calls=%fused_computation.323 | convolution fusion | flops 5640290304 | bytes 21757952 | tf_op jit(solution)/shard_map/cond/branch_1_fun/dot_general | solution.py:13
  385.4 4.4 collective-permute-done.23
  389.8 22.0 %fusion.240 = bf16[384,3584]{1,0:T(8,128)(2,1)} fusion(f32[384,3584]{1,0:T(8,128)} %fusion.299, bf16[7168,2048]{1,0:T(8,128)(2,1)} %get-tuple-element.137, s32[]{:T(128)S(6)} %select_n.366, bf16[384,3584]{1,0:T(8,128)(2,1)} %collective-permute-done.23, bf16[192,2048]{1,0:T(8,128)(2,1)S(1)} %get-tuple-element.233, bf16[192,2048]{1,0:T(8,128)(2,1)S(1)} %get-tuple-element.224), kind=kOutput, calls=%fused_computation.286 | convolution fusion | flops 5645795328 | bytes 27262980 | tf_op jit(solution)/shard_map/cond/branch_1_fun/dot_general | solution.py:13
  411.8 36.0 %collective-permute-done.17 = bf16[384,3584]{1,0:T(8,128)(2,1)S(1)} collective-permute-done((bf16[384,3584]{1,0:T(8,128)(2,1)}, bf16[384,3584]{1,0:T(8,128)(2,1)S(1)}, u32[]{:S(2)}, u32[]{:S(2)}) %collective-permute-start.17) | collective-permute-done | bytes 2752544 | tf_op jit(solution)/shard_map/cond/branch_1_fun/ppermute | solution.py:46
  447.8 21.9 %fusion.243 = bf16[384,3584]{1,0:T(8,128)(2,1)} fusion(f32[384,3584]{1,0:T(8,128)} %fusion.285, bf16[7168,2048]{1,0:T(8,128)(2,1)} %get-tuple-element.137, s32[]{:T(128)S(6)} %select_n.366, bf16[384,3584]{1,0:T(8,128)(2,1)S(1)} %collective-permute-done.17, bf16[192,2048]{1,0:T(8,128)(2,1)S(1)} %get-tuple-element.225, ...), kind=kOutput, calls=%fused_computation.287 | convolution fusion | flops 5645795328 | bytes 27262980 | tf_op jit(solution)/shard_map/cond/branch_1_fun/dot_general | solution.py:13
  469.7 4.6 fusion.270
  474.4 4.0 fusion.272
  478.5 2.6 fusion.274
  481.2 2.6 fusion.276
  483.8 1.4 convolution_bitcast_fusion.4
  485.2 0.7 copy.65
  486.0 3.4 all-to-all-start.1
  490.1 7.7 %all-to-all-done.1 = f32[1,8,4,16,128]{4,3,1,0,2:T(8,128)S(1)} async-done(((f32[1,8,4,16,128]{4,3,1,0,2:T(8,128)}), f32[1,8,4,16,128]{4,3,1,0,2:T(8,128)S(1)}, u32[]{:S(2)}, u32[]{:S(2)}) %all-to-all-start.1) | async-done | bytes 262176 | tf_op jit(solution)/shard_map/cond/branch_1_fun/all_to_all | solution.py:190
  508.5 6.4 %all_gather.37 = f32[4,8,3072]{2,1,0:T(8,128)S(1)} all-gather(f32[1,8,3072]{2,1,0:T(8,128)S(1)} %all_gather_reshape.3), channel_id=1, replica_groups=mesh['group'=2,'tensor'=4,'example'=4] {'example'}, dimensions={0}, use_global_device_ids=true | all-gather | bytes 491520 | tf_op jit(solution)/shard_map/all_gather | solution.py:243
  515.0 1.3 fusion.730
  516.3 1.2 fusion.718
  517.5 19.9 %all-gather = f32[128,512]{1,0:T(8,128)S(1)} all-gather(f32[8,512]{1,0:T(8,128)S(1)} %fusion.718), channel_id=2, replica_groups=mesh['group'=2,'tensor'=4,'example'=4] {'tensor','example'}, dimensions={0}, use_global_device_ids=true | all-gather | bytes 278528 | tf_op jit(solution)/shard_map/all_gather | solution.py:247
  537.4 0.6 broadcast_multiply_fusion.8
  (112 shorter events, 6.2 us)
Async XLA Ops:
  6.5 508.4 %copy-start = (bf16[256,3072]{1,0:T(8,128)(2,1)S(1)}, bf16[256,3072]{1,0:T(8,128)(2,1)}, u32[]{:S(2)}) copy-start(bf16[256,3072]{1,0:T(8,128)(2,1)} %param.29) | copy-start | bytes 4718596
  6.5 17.2 %collective-permute-start.48 = (bf16[512,2048]{1,0:T(8,128)(2,1)}, bf16[512,2048]{1,0:T(8,128)(2,1)}, u32[]{:S(2)}, u32[]{:S(2)}) collective-permute-start(bf16[512,2048]{1,0:T(8,128)(2,1)} %bitcast.382), channel_id=1, source_target_pairs={{0,1},{1,0},{2,3},{3,2},{4,5},{5,4},{6,7},{7,6},{8,9},{9,8},{10,11... | collective-permute-start | bytes 6291464 | tf_op jit(solution)/shard_map/ppermute | solution.py:41
  28.6 17.0 %copy-start.44 = (s32[16]{0:T(128)}, s32[16]{0:T(128)S(1)}, u32[]{:S(2)}) copy-start(s32[16]{0:T(128)S(1)} %get-tuple-element.127) | copy-start | bytes 196 | tf_op jit(solution)/shard_map/cond
  28.7 4.8 copy-start.51
  28.7 56.8 %all-reduce.8.cloned.1.call-start = ((), (), s32[]{:S(2)}) async-start(), calls=%async_computation.7 | async-start | bytes 786432 | tf_op jit(solution)/shard_map/cond/branch_1_fun/psum | solution.py:138
  42.0 101.6 %all-gather.16.cloned.1.call-start = ((), (), s32[]{:S(2)}) async-start(), calls=%async_computation.9 | async-start | bytes 3932160 | tf_op jit(solution)/shard_map/cond/branch_1_fun/all_gather | solution.py:112
  53.9 153.5 %all-gather.14.cloned.1.call-start = ((), (), s32[]{:S(2)}) async-start(), calls=%async_computation.8 | async-start | bytes 3932160 | tf_op jit(solution)/shard_map/cond/branch_1_fun/all_gather | solution.py:112
  54.1 13.8 %copy-start.15 = (bf16[1024,2048]{1,0:T(8,128)(2,1)S(1)}, bf16[1024,2048]{1,0:T(8,128)(2,1)}, u32[]{:S(2)}) copy-start(bf16[1024,2048]{1,0:T(8,128)(2,1)} %constant_dynamic-update-slice_fusion.2) | copy-start | bytes 12582916 | tf_op jit(solution)/shard_map/cond
  68.0 226.5 %collective-permute-start.14 = (bf16[3584,2048]{1,0:T(8,128)(2,1)}, bf16[3584,2048]{1,0:T(8,128)(2,1)}, u32[]{:S(2)}, u32[]{:S(2)}) collective-permute-start(bf16[3584,2048]{1,0:T(8,128)(2,1)} %constant_dynamic-slice_fusion.19), channel_id=1, source_target_pairs={{0,1},{1,0},{2,3},{3,2},{4,5},{5,4},{6,7},{7,6},{8,9},{9,8},{10,11... | collective-permute-start | bytes 44040200 | tf_op jit(solution)/shard_map/cond/branch_1_fun/ppermute | solution.py:41
  76.7 7.0 %copy-start.45 = (s32[16]{0:T(128)S(1)}, s32[16]{0:T(128)}, u32[]{:S(2)}) copy-start(s32[16]{0:T(128)} %copy-done.44) | copy-start | bytes 196 | tf_op jit(solution)/shard_map/cond
  76.7 7.1 %copy-start.33 = (s32[16]{0:T(128)S(1)}, s32[16]{0:T(128)}, u32[]{:S(2)}) copy-start(s32[16]{0:T(128)} %get-tuple-element.128) | copy-start | bytes 196 | tf_op jit(solution)/shard_map/cond
  76.7 136.9 %collective-permute-start.19 = (bf16[512,3584]{1,0:T(8,128)(2,1)}, bf16[512,3584]{1,0:T(8,128)(2,1)}, u32[]{:S(2)}, u32[]{:S(2)}) collective-permute-start(bf16[512,3584]{1,0:T(8,128)(2,1)} %get-tuple-element.216), channel_id=1, source_target_pairs={{0,1},{1,0},{2,3},{3,2},{4,5},{5,4},{6,7},{7,6},{8,9},{9,8},{10,11... | collective-permute-start | bytes 11010056 | tf_op jit(solution)/shard_map/cond/branch_1_fun/ppermute | solution.py:41
  83.7 197.9 %collective-permute-start.18 = (bf16[512,3584]{1,0:T(8,128)(2,1)}, bf16[512,3584]{1,0:T(8,128)(2,1)}, u32[]{:S(2)}, u32[]{:S(2)}) collective-permute-start(bf16[512,3584]{1,0:T(8,128)(2,1)} %get-tuple-element.214), channel_id=1, source_target_pairs={{0,1},{1,0},{2,3},{3,2},{4,5},{5,4},{6,7},{7,6},{8,9},{9,8},{10,11... | collective-permute-start | bytes 11010056 | tf_op jit(solution)/shard_map/cond/branch_1_fun/ppermute | solution.py:41
  87.2 3.3 collective-permute-start.12
  211.1 2.5 copy-start.10
  211.3 37.3 %collective-permute-start.21 = (bf16[2,192,2048]{2,1,0:T(8,128)(2,1)S(1)}, bf16[2,192,2048]{2,1,0:T(8,128)(2,1)S(1)}, u32[]{:S(2)}, u32[]{:S(2)}) collective-permute-start(bf16[2,192,2048]{2,1,0:T(8,128)(2,1)S(1)} %pad_maximum_fusion.12), channel_id=1, source_target_pairs={{0,2},{1,3},{2,0},{3,1},{4,6},{5,7},{6,4},{7,5},{8,10},{9,11},{10,... | collective-permute-start | bytes 4718600 | tf_op jit(solution)/shard_map/cond/branch_1_fun/ppermute | solution.py:46
  213.0 68.2 %collective-permute-start.15 = (bf16[2,192,2048]{2,1,0:T(8,128)(2,1)S(1)}, bf16[2,192,2048]{2,1,0:T(8,128)(2,1)S(1)}, u32[]{:S(2)}, u32[]{:S(2)}) collective-permute-start(bf16[2,192,2048]{2,1,0:T(8,128)(2,1)S(1)} %pad_maximum_fusion.9), channel_id=1, source_target_pairs={{0,2},{1,3},{2,0},{3,1},{4,6},{5,7},{6,4},{7,5},{8,10},{9,11},{10,... | collective-permute-start | bytes 4718600 | tf_op jit(solution)/shard_map/cond/branch_1_fun/ppermute | solution.py:46
  223.1 68.6 %collective-permute-start.20 = (bf16[2,192,2048]{2,1,0:T(8,128)(2,1)S(1)}, bf16[2,192,2048]{2,1,0:T(8,128)(2,1)S(1)}, u32[]{:S(2)}, u32[]{:S(2)}) collective-permute-start(bf16[2,192,2048]{2,1,0:T(8,128)(2,1)S(1)} %pad_maximum_fusion.11), channel_id=1, source_target_pairs={{0,1},{1,0},{2,3},{3,2},{4,5},{5,4},{6,7},{7,6},{8,9},{9,8},{10,11... | collective-permute-start | bytes 4718600 | tf_op jit(solution)/shard_map/cond/branch_1_fun/ppermute | solution.py:41
  248.6 43.2 %collective-permute-start.13 = (bf16[2,192,2048]{2,1,0:T(8,128)(2,1)S(1)}, bf16[2,192,2048]{2,1,0:T(8,128)(2,1)S(1)}, u32[]{:S(2)}, u32[]{:S(2)}) collective-permute-start(bf16[2,192,2048]{2,1,0:T(8,128)(2,1)S(1)} %pad_maximum_fusion.8), channel_id=1, source_target_pairs={{0,1},{1,0},{2,3},{3,2},{4,5},{5,4},{6,7},{7,6},{8,9},{9,8},{10,11... | collective-permute-start | bytes 4718600 | tf_op jit(solution)/shard_map/cond/branch_1_fun/ppermute | solution.py:41
  249.0 33.1 %copy-start.6 = (bf16[512,3584]{1,0:T(8,128)(2,1)S(1)}, bf16[512,3584]{1,0:T(8,128)(2,1)}, u32[]{:S(2)}) copy-start(bf16[512,3584]{1,0:T(8,128)(2,1)} %get-tuple-element.213) | copy-start | bytes 11010052 | tf_op jit(solution)/shard_map/cond
  281.2 10.9 %collective-permute-start.22 = (bf16[2,192,2048]{2,1,0:T(8,128)(2,1)S(1)}, bf16[2,192,2048]{2,1,0:T(8,128)(2,1)S(1)}, u32[]{:S(2)}, u32[]{:S(2)}) collective-permute-start(bf16[2,192,2048]{2,1,0:T(8,128)(2,1)S(1)} %pad_maximum_fusion.13), channel_id=1, source_target_pairs={{0,1},{1,0},{2,3},{3,2},{4,5},{5,4},{6,7},{7,6},{8,9},{9,8},{10,11... | collective-permute-start | bytes 4718600 | tf_op jit(solution)/shard_map/cond/branch_1_fun/ppermute | solution.py:41
  281.6 11.8 %collective-permute-start.16 = (bf16[2,192,2048]{2,1,0:T(8,128)(2,1)S(1)}, bf16[2,192,2048]{2,1,0:T(8,128)(2,1)S(1)}, u32[]{:S(2)}, u32[]{:S(2)}) collective-permute-start(bf16[2,192,2048]{2,1,0:T(8,128)(2,1)S(1)} %pad_maximum_fusion.10), channel_id=1, source_target_pairs={{0,1},{1,0},{2,3},{3,2},{4,5},{5,4},{6,7},{7,6},{8,9},{9,8},{10,11... | collective-permute-start | bytes 4718600 | tf_op jit(solution)/shard_map/cond/branch_1_fun/ppermute | solution.py:41
  294.5 11.0 %copy-start.23 = (bf16[192,2048]{1,0:T(8,128)(2,1)S(1)}, bf16[192,2048]{1,0:T(8,128)(2,1)}, u32[]{:S(2)}) copy-start(bf16[192,2048]{1,0:T(8,128)(2,1)} %get-tuple-element.239) | copy-start | bytes 2359300 | tf_op jit(solution)/shard_map/cond
  305.5 23.0 %copy-start.22 = (bf16[192,2048]{1,0:T(8,128)(2,1)S(1)}, bf16[192,2048]{1,0:T(8,128)(2,1)}, u32[]{:S(2)}) copy-start(bf16[192,2048]{1,0:T(8,128)(2,1)} %get-tuple-element.232) | copy-start | bytes 2359300 | tf_op jit(solution)/shard_map/cond
  327.0 62.9 %collective-permute-start.23 = (bf16[384,3584]{1,0:T(8,128)(2,1)}, bf16[384,3584]{1,0:T(8,128)(2,1)}, u32[]{:S(2)}, u32[]{:S(2)}) collective-permute-start(bf16[384,3584]{1,0:T(8,128)(2,1)} %fusion.246), channel_id=1, source_target_pairs={{0,2},{1,3},{2,0},{3,1},{4,6},{5,7},{6,4},{7,5},{8,10},{9,11},{10,... | collective-permute-start | bytes 8257544 | tf_op jit(solution)/shard_map/cond/branch_1_fun/ppermute | solution.py:46
  361.8 86.0 %collective-permute-start.17 = (bf16[384,3584]{1,0:T(8,128)(2,1)}, bf16[384,3584]{1,0:T(8,128)(2,1)S(1)}, u32[]{:S(2)}, u32[]{:S(2)}) collective-permute-start(bf16[384,3584]{1,0:T(8,128)(2,1)} %fusion.249), channel_id=1, source_target_pairs={{0,2},{1,3},{2,0},{3,1},{4,6},{5,7},{6,4},{7,5},{8,10},{9,11},{10,... | collective-permute-start | bytes 8257544 | tf_op jit(solution)/shard_map/cond/branch_1_fun/ppermute | solution.py:46
  447.8 21.9 %copy-start.59 = (bf16[64,7168]{1,0:T(8,128)(2,1)S(1)}, bf16[64,7168]{1,0:T(8,128)(2,1)}, u32[]{:S(2)}) copy-start(bf16[64,7168]{1,0:T(8,128)(2,1)} %get-tuple-element.139) | copy-start | bytes 2752516 | tf_op jit(solution)/shard_map/cond
  469.7 4.7 copy-start.64
  469.7 8.7 %slice-start.8 = ((s8[5505024]{0:T(1024)(128)(4,1)}), s8[4194304]{0:T(1024)(128)(4,1)S(1)}, s32[]{:S(2)}) async-start(s8[5505024]{0:T(1024)(128)(4,1)} %bitcast.448), calls=%async_computation.24 | async-start | bytes 8388608 | tf_op jit(solution)/shard_map/cond
  469.7 8.7 %slice-start.10 = ((s8[5505024]{0:T(1024)(128)(4,1)}), s8[4194304]{0:T(1024)(128)(4,1)S(1)}, s32[]{:S(2)}) async-start(s8[5505024]{0:T(1024)(128)(4,1)} %bitcast.450), calls=%async_computation.26 | async-start | bytes 8388608 | tf_op jit(solution)/shard_map/cond
  474.3 4.1 copy-start.55
  474.3 4.1 slice-start.9
  474.4 4.1 copy-start.63
  474.4 4.1 slice-start.11
  481.1 2.7 copy-start.4
  481.1 8.3 %copy-start.41 = (f32[4,128]{1,0:T(4,128)S(1)}, f32[4,128]{1,0:T(4,128)}, u32[]{:S(2)}) copy-start(f32[4,128]{1,0:T(4,128)} %fusion.364) | copy-start | bytes 6148 | tf_op jit(solution)/shard_map/cond
  481.1 8.3 %copy-start.29 = (f32[4,128,16]{1,0,2:T(4,128)S(1)}, f32[4,128,16]{1,0,2:T(4,128)}, u32[]{:S(2)}) copy-start(f32[4,128,16]{1,0,2:T(4,128)} %dynamic_slice.254) | copy-start | bytes 98308 | tf_op jit(solution)/shard_map/cond
  481.1 8.3 %copy-start.25 = (f32[1,512,64]{1,2,0:T(8,128)S(1)}, f32[1,512,64]{1,2,0:T(8,128)}, u32[]{:S(2)}) copy-start(f32[1,512,64]{1,2,0:T(8,128)} %get-tuple-element.243) | copy-start | bytes 393220 | tf_op jit(solution)/shard_map/cond
  481.1 8.6 %copy-start.37 = (f32[8,8]{0,1:T(8,128)S(1)}, f32[8,8]{0,1:T(8,128)}, u32[]{:S(2)}) copy-start(f32[8,8]{0,1:T(8,128)} %fusion.361) | copy-start | bytes 772 | tf_op jit(solution)/shard_map/cond
  486.0 11.9 %all-to-all-start.1 = ((f32[1,8,4,16,128]{4,3,1,0,2:T(8,128)}), f32[1,8,4,16,128]{4,3,1,0,2:T(8,128)S(1)}, u32[]{:S(2)}, u32[]{:S(2)}) async-start(f32[1,8,4,16,128]{4,3,1,0,2:T(8,128)} %copy.65), calls=%async_computation.1 | async-start | bytes 524288 | tf_op jit(solution)/shard_map/cond/branch_1_fun/all_to_all | solution.py:190
Sparse Core Ops, SparseCore 0:
  42.2 36.7 all-reduce.7
  80.5 63.0 all-gather.15
  145.2 62.1 all-gather.13

commit v2 on v0

--- a/solution.py
+++ b/solution.py
@@ -1,7 +1,16 @@
+import functools
+
 import jax
 import jax.numpy as jnp
 from jax import lax
+from jax.experimental import pallas as pl
+from jax.experimental.pallas import tpu as pltpu
 from jax.sharding import PartitionSpec as P
+
+CHUNKS = 4
+LEVELS = (672, 704, 736, 768, 832)
+TILE = 512
+VMEM_LIMIT = 48 * 1024 * 1024
 
 
 def contract(left_side, right_side):
@@ -27,7 +36,393 @@
     return jnp.where(targets[:, None] == pair_index[None, :], signs[None, :], jnp.float32(0.0))
 
 
-def local(
+def take(array, start, size, axis):
+    return lax.dynamic_slice_in_dim(array, start, size, axis)
+
+
+def swap(array, axis, bits):
+    count = lax.axis_size(axis)
+    return lax.ppermute(array, axis, [(i, i ^ bits) for i in range(count)])
+
+
+def chain_pairs(rule):
+    pairs = []
+    for t in range(4):
+        for e in range(4):
+            far, near = e // 2, e % 2
+            goal = rule(3 - t if far else t, far, near)
+            if goal is not None:
+                order, far, near = goal
+                pairs.append((t * 4 + e, (3 - order if far else order) * 4 + 2 * far + near))
+    return pairs
+
+
+CROSS = chain_pairs(lambda u, f, n: (3 - u, 1 - f, n) if u >= 2 else None)
+UP_FIRST = chain_pairs(lambda u, f, n: (u + 1, f, n) if u in (0, 1) else None)
+UP_SECOND = chain_pairs(lambda u, f, n: (u + 1, f, n) if u in (1, 2) else None)
+UP_THIRD = chain_pairs(lambda u, f, n: (u + 1, f, n) if u == 2 else None)
+DOWN = chain_pairs(lambda u, f, n: (0, f, n) if u == 1 else None)
+
+
+def move(array, pairs):
+    return lax.ppermute(array, ("tensor", "example"), pairs)
+
+
+def kernel_params():
+    return pltpu.CompilerParams(vmem_limit_bytes=VMEM_LIMIT)
+
+
+def pack_kernel(starts, sizes, near_ref, place_ref, own_ref, other_ref, *refs):
+    outs, select = refs[:-1], refs[-1]
+    rows_own = own_ref.shape[0]
+
+    @pl.when(pl.program_id(0) == 0)
+    def _():
+        base = 0
+        for start, size in zip(starts, sizes):
+            at = lax.broadcasted_iota(jnp.int32, (size, select.shape[1]), 0) + start
+            select[base : base + size, :] = jnp.where(at == place_ref[...], 1.0, 0.0).astype(jnp.bfloat16)
+            base += size
+
+    base = 0
+    for out, size in zip(outs, sizes):
+        rows = slice(base, base + size)
+        total = jnp.dot(select[rows, :rows_own], own_ref[...], preferred_element_type=jnp.float32)
+        total += jnp.dot(select[rows, rows_own:], other_ref[...], preferred_element_type=jnp.float32)
+        out[...] = total.astype(jnp.bfloat16)
+        base += size
+
+
+def pack(starts, sizes, near_offset, place, own, other):
+    rows, columns = other.shape
+    total = sum(sizes)
+    return pl.pallas_call(
+        functools.partial(pack_kernel, starts, sizes),
+        grid_spec=pltpu.PrefetchScalarGridSpec(
+            num_scalar_prefetch=1,
+            grid=(columns // TILE,),
+            in_specs=[
+                pl.BlockSpec((1, 2 * rows), lambda i, near: (0, 0)),
+                pl.BlockSpec((rows, TILE), lambda i, near: (0, near[0] + i)),
+                pl.BlockSpec((rows, TILE), lambda i, near: (0, i)),
+            ],
+            out_specs=[pl.BlockSpec((size, TILE), lambda i, near: (0, i)) for size in sizes],
+            scratch_shapes=[pltpu.VMEM((total, 2 * rows), jnp.bfloat16)],
+        ),
+        out_shape=[jax.ShapeDtypeStruct((size, columns), jnp.bfloat16) for size in sizes],
+        compiler_params=kernel_params(),
+        cost_estimate=pl.CostEstimate(
+            flops=4 * total * rows * columns,
+            bytes_accessed=(4 * rows + 2 * total) * columns,
+            transcendentals=0,
+        ),
+        name="pack_rows",
+    )(near_offset, place, own, other)
+
+
+def partial_kernel(near_ref, a0, a1, b0, b1, keep_ref, other_ref, out_ref, left):
+    size, width = a0.shape
+
+    @pl.when(pl.program_id(0) == 0)
+    def _():
+        left[:size, :width] = a0[...]
+        left[size:, :width] = a1[...]
+        left[:size, width:] = b0[...]
+        left[size:, width:] = b1[...]
+
+    total = contract(left[:, :width], keep_ref[...])
+    total += contract(left[:, width:], other_ref[...])
+    out_ref[...] = total.astype(out_ref.dtype)
+
+
+def partial_product(part, near_offset, own_k, own_k_near, near_k, near_k_near, weight, weight_near, dtype):
+    size, width = own_k.shape[0] // 2, own_k.shape[1]
+    hidden = weight_near.shape[0]
+    rows = pl.BlockSpec((size, width), lambda i, near: (part, 0))
+    return pl.pallas_call(
+        partial_kernel,
+        grid_spec=pltpu.PrefetchScalarGridSpec(
+            num_scalar_prefetch=1,
+            grid=(hidden // TILE,),
+            in_specs=[rows] * 4
+            + [
+                pl.BlockSpec((TILE, width), lambda i, near: (near[0] + i, 0)),
+                pl.BlockSpec((TILE, width), lambda i, near: (i, 0)),
+            ],
+            out_specs=pl.BlockSpec((2 * size, TILE), lambda i, near: (0, i)),
+            scratch_shapes=[pltpu.VMEM((2 * size, 2 * width), jnp.bfloat16)],
+        ),
+        out_shape=jax.ShapeDtypeStruct((2 * size, hidden), dtype),
+        compiler_params=kernel_params(),
+        cost_estimate=pl.CostEstimate(
+            flops=8 * size * width * hidden,
+            bytes_accessed=4 * width * hidden + 8 * size * hidden,
+            transcendentals=0,
+        ),
+        name="partial_product",
+    )(near_offset, own_k, own_k_near, near_k, near_k_near, weight, weight_near)
+
+
+def finish_kernel(near_ref, own_ref, came_ref, gate_ref, up_ref, proj_gate_ref, proj_up_ref, gate_out, up_out):
+    @pl.when(pl.program_id(0) == 0)
+    def _():
+        gate_out[...] = jnp.zeros_like(gate_out)
+        up_out[...] = jnp.zeros_like(up_out)
+
+    hidden_grad = (own_ref[...] + came_ref[...].astype(jnp.float32)).astype(jnp.bfloat16)
+    hidden_grad = hidden_grad.astype(jnp.float32)
+    gate = gate_ref[...].astype(jnp.float32)
+    up = up_ref[...].astype(jnp.float32)
+    sigma = jax.nn.sigmoid(gate)
+    grad_up = (hidden_grad * (gate * sigma)).astype(jnp.bfloat16)
+    grad_gate = (hidden_grad * up * sigma * (1.0 + gate * (1.0 - sigma))).astype(jnp.bfloat16)
+    gate_out[...] += contract(grad_gate, proj_gate_ref[...])
+    up_out[...] += contract(grad_up, proj_up_ref[...])
+
+
+def finish(near_offset, own, came, gate, up, proj_gate, proj_up):
+    rows, hidden = own.shape
+    rank_size = proj_gate.shape[0]
+    tile = pl.BlockSpec((rows, TILE), lambda i, near: (0, i))
+    proj = pl.BlockSpec((rank_size, TILE), lambda i, near: (0, near[0] + i))
+    out = pl.BlockSpec((rows, rank_size), lambda i, near: (0, 0))
+    return pl.pallas_call(
+        finish_kernel,
+        grid_spec=pltpu.PrefetchScalarGridSpec(
+            num_scalar_prefetch=1,
+            grid=(hidden // TILE,),
+            in_specs=[tile, tile, tile, tile, proj, proj],
+            out_specs=[out, out],
+        ),
+        out_shape=[jax.ShapeDtypeStruct((rows, rank_size), jnp.float32)] * 2,
+        compiler_params=kernel_params(),
+        cost_estimate=pl.CostEstimate(
+            flops=4 * rows * hidden * rank_size,
+            bytes_accessed=10 * rows * hidden,
+            transcendentals=rows * hidden,
+        ),
+        name="finish_chunk",
+    )(near_offset, own, came, gate, up, proj_gate, proj_up)
+
+
+def sum_over(array, axis):
+    parts = [swap(array, axis, bits) for bits in (1, 2, 3)]
+    return (array + parts[0]) + (parts[1] + parts[2])
+
+
+def scatter_over(array, axis, dim):
+    at = lax.axis_index(axis)
+    size = array.shape[dim] // 4
+    parts = [swap(take(array, (at ^ bits) * size, size, dim), axis, bits) for bits in (1, 2, 3)]
+    return (take(array, at * size, size, dim) + parts[0]) + (parts[1] + parts[2])
+
+
+def packed_scores(capacity, args):
+    (
+        layer_input,
+        gate_pre,
+        up_pre,
+        grad_rows,
+        grad_near,
+        down_weight,
+        proj_input,
+        proj_hidden,
+        proj_output,
+        proj_gate,
+        proj_up,
+        query_sketches,
+        query_slot,
+        rev_slot,
+        own_lengths,
+        near_lengths,
+    ) = args
+    ex_count, slot_len, width_local = layer_input.shape
+    hidden_local = gate_pre.shape[2]
+    row_total = ex_count * slot_len
+    rank_size = proj_input.shape[0]
+    per_rank = rank_size // 4
+    rev_pairs = rev_slot.shape[0] // 2
+    example_at = lax.axis_index("example")
+    tensor_at = lax.axis_index("tensor")
+    near, far = example_at % 2, example_at // 2
+    order = jnp.where(far == 1, 3 - tensor_at, tensor_at)
+    half_hidden = hidden_local // 2
+    half_rows = capacity // 2
+    units = half_rows // 16
+    sizes = [16 * (units // CHUNKS + (k < units % CHUNKS)) for k in range(CHUNKS)]
+    begins = [sum(sizes[:k]) for k in range(CHUNKS)]
+    offset = (near * (half_hidden // TILE)).astype(jnp.int32).reshape(1)
+    no_offset = jnp.zeros((1,), jnp.int32)
+
+    both_lengths = jnp.concatenate([own_lengths, near_lengths])
+    own_begin = near * jnp.sum(near_lengths)
+    near_begin = (1 - near) * jnp.sum(own_lengths)
+    offsets = jnp.concatenate(
+        [
+            own_begin + jnp.cumsum(own_lengths) - own_lengths,
+            near_begin + jnp.cumsum(near_lengths) - near_lengths,
+        ]
+    )
+    positions = jnp.arange(slot_len, dtype=jnp.int32)
+    place = offsets[:, None] + positions[None, :] - near * half_rows
+    place = jnp.where(place < 0, place + capacity, place)
+    other_half = place >= half_rows
+    at = jnp.where(other_half, place - half_rows, place)
+    place = at + jnp.where(other_half, sizes[0], 0)
+    for k in range(1, CHUNKS):
+        place += jnp.where(
+            at >= begins[k], sizes[k - 1] + jnp.where(other_half, sizes[k] - sizes[k - 1], 0), 0
+        )
+    place = jnp.where(positions[None, :] < both_lengths[:, None], place, -1).reshape(1, 2 * row_total)
+
+    starts = [2 * b for b in begins]
+    doubles = [2 * s for s in sizes]
+    blocks = pack(starts, sizes, no_offset, place, grad_rows, grad_near)
+
+    weight_near = swap(take(down_weight, (1 - near) * half_hidden, half_hidden, 0), "example", 1)
+
+    def split_hidden(array):
+        rows = array.reshape(row_total, hidden_local)
+        other = swap(take(rows, (1 - near) * half_hidden, half_hidden, 1), "example", 1)
+        return pack(starts, doubles, offset, place, rows, other)
+
+    gate_packed = split_hidden(gate_pre)
+    up_packed = split_hidden(up_pre)
+
+    columns_match = near == far
+    lefts = []
+    for k in range(CHUNKS):
+        source = jnp.concatenate([blocks[k], move(blocks[k], CROSS)])
+        first = move(source, UP_FIRST)
+        down = move(source, DOWN)
+        second = move(first, UP_SECOND)
+        third = move(second, UP_THIRD)
+        outer = lax.select_n(order, source, first, second, third)
+        inner = lax.select_n(order, down, source, first, second)
+        own_k = jnp.where(columns_match, outer, inner)
+        near_k = jnp.where(columns_match, inner, outer)
+        lefts.append((own_k, swap(near_k, "example", 1), near_k, swap(own_k, "example", 1)))
+    came = [
+        swap(partial_product(1, offset, *lefts[k], down_weight, weight_near, jnp.bfloat16), "example", 2)
+        for k in range(CHUNKS)
+    ]
+    own = [
+        partial_product(0, offset, *lefts[k], down_weight, weight_near, jnp.float32)
+        for k in range(CHUNKS)
+    ]
+
+    inputs_rows = layer_input.reshape(row_total, width_local)
+    gate_values = gate_pre.reshape(row_total, hidden_local).astype(jnp.float32)
+    up_values = up_pre.reshape(row_total, hidden_local).astype(jnp.float32)
+    hidden = (gate_values * jax.nn.sigmoid(gate_values) * up_values).astype(jnp.bfloat16)
+    early = jnp.concatenate(
+        [
+            contract(inputs_rows, proj_input),
+            contract(hidden, proj_hidden),
+            contract(grad_rows, proj_output),
+        ]
+    )
+    early, _ = lax.optimization_barrier((early, lefts[-1][0]))
+    early = sum_over(early, "tensor")
+    in_gate, in_down, out_down = (early[k * row_total : (k + 1) * row_total] for k in range(3))
+    slots_here = jnp.concatenate(
+        [
+            take(rev_slot, example_at * ex_count, ex_count, 0),
+            take(rev_slot, (example_at ^ 1) * ex_count, ex_count, 0),
+        ]
+    )
+    table = pairing_table(slots_here, rev_pairs)
+    mask = (positions[None, :] < own_lengths[:, None]).astype(jnp.float32).reshape(row_total)
+    left_down = take(in_down, tensor_at * per_rank, per_rank, 1) * mask[:, None]
+    sketch_down = jnp.einsum(
+        "pe,eti,etj->pij",
+        table[:, :ex_count],
+        left_down.reshape(ex_count, slot_len, per_rank),
+        out_down.reshape(ex_count, slot_len, rank_size),
+        precision=lax.Precision.HIGHEST,
+    )
+    in_gate = jnp.concatenate([in_gate, swap(in_gate, "example", 1)])
+    select = jnp.arange(capacity, dtype=jnp.int32)[:, None] == place
+    in_gate = jnp.dot(select.astype(jnp.float32), in_gate, precision=lax.Precision.HIGHEST)
+    table_rows = jnp.dot(
+        select.astype(jnp.bfloat16), jnp.repeat(table, slot_len, axis=1).T.astype(jnp.bfloat16)
+    )
+    left = table_rows.astype(jnp.float32)[:, :, None] * in_gate[:, None, :]
+    left = left.reshape(capacity, rev_pairs * rank_size)
+
+    right = [
+        jnp.concatenate(finish(offset, own[k], came[k], gate_packed[k], up_packed[k], proj_gate, proj_up), axis=1)
+        for k in range(CHUNKS)
+    ]
+    sketch_late = lax.dot_general(
+        left, jnp.concatenate(right), (((0,), (0,)), ((), ())), precision=lax.Precision.HIGHEST
+    ).reshape(rev_pairs, rank_size, 2 * rank_size)
+    sketch_late = scatter_over(sketch_late, "tensor", 1)
+    revision_pairs = sum_over(jnp.concatenate([sketch_late, sketch_down], axis=2), "example")
+    example_scores = contract_exact(
+        revision_pairs.reshape(rev_pairs, -1), query_sketches.astype(jnp.float32)
+    )
+    query_pairs = query_slot.shape[0] * 4 // 2
+    pair_terms = contract_exact(example_scores, pairing_table(query_slot, query_pairs))
+    total = sum_over(scatter_over(pair_terms, "example", 1), "tensor")
+    return total / jnp.float32(rank_size * rank_size)
+
+
+def local_four(
+    layer_input,
+    gate_pre,
+    up_pre,
+    output_grad,
+    down_weight,
+    proj_input,
+    proj_hidden,
+    proj_output,
+    proj_gate,
+    proj_up,
+    query_sketches,
+    rev_lengths,
+    rev_slot,
+    query_slot,
+):
+    ex_count, slot_len, width_local = layer_input.shape
+    row_total = ex_count * slot_len
+    grad_rows = output_grad.reshape(row_total, width_local)
+    grad_near = swap(grad_rows, "example", 1)
+    others = [swap(rev_lengths, "example", bits) for bits in (1, 2, 3)]
+    sums = jnp.stack([jnp.sum(rev_lengths) + jnp.sum(others[0]), jnp.sum(others[1]) + jnp.sum(others[2])])
+    most = jnp.max(sums).reshape(1)
+    count = lax.axis_size("group")
+    for step in range(1, count):
+        shifted = lax.ppermute(most, "group", [(i, (i + step) % count) for i in range(count)])
+        most = jnp.maximum(most, shifted)
+    full = 2 * row_total
+    levels = [level for level in LEVELS if level < full] + [full]
+    branch = jnp.sum((most[0] > jnp.array(levels[:-1], jnp.int32)).astype(jnp.int32))
+    return lax.switch(
+        branch,
+        [functools.partial(packed_scores, level) for level in levels],
+        (
+            layer_input,
+            gate_pre,
+            up_pre,
+            grad_rows,
+            grad_near,
+            down_weight,
+            proj_input,
+            proj_hidden,
+            proj_output,
+            proj_gate,
+            proj_up,
+            query_sketches,
+            query_slot,
+            rev_slot,
+            rev_lengths,
+            others[0],
+        ),
+    )
+
+
+def local_any(
     layer_input,
     gate_pre,
     up_pre,
@@ -97,8 +492,9 @@
 
 
 def solution(mesh):
+    four = mesh.shape["tensor"] == 4 and mesh.shape["example"] == 4
     return jax.shard_map(
-        local,
+        local_four if four else local_any,
         mesh=mesh,
         in_specs=(
             P(("group", "example"), None, "tensor"),

time: 1030 us -> 544 us (0.53); the launches traced: 1030 us -> 534 us
  waiting for transfers between devices: 892 us -> 146 us
  Pallas kernels: 0 us -> 186 us
  starting transfers between devices: 0.3 us -> 104 us
  matrix products: 90.6 us -> 19 us
  local copies, waits for them, and re-layouts: 2.43 us -> 40.3 us
  loops' own time: 0 us -> 21.5 us
  blocking collectives: 17.4 us -> 0 us
    all_gather x2 -> x0, waiting for transfers between devices: 831 us -> none  [the longest x1 679 us: local(): lax.all_gather(down_weight, 'example', axis=1, tiled=True)]
    pallas_call x0 -> x15, Pallas kernels: none -> 186 us  [the longest x8 126 us: partial_product(): pl.pallas_call(partial_kernel, grid_spec=pltpu.PrefetchScalarGridSpec(num...]
    ppermute x0 -> x56, waiting for transfers between devices: none -> 146 us  [the longest x20 113 us: move(): return lax.ppermute(array, ('tensor', 'example'), pairs)]
    ppermute x0 -> x56, starting transfers between devices: none -> 104 us  [the longest x35 57 us: swap(): return lax.ppermute(array, axis, [(i, i ^ bits) for i in range(count)])]
    dot_general x6 -> x3, matrix products: 84.8 us -> 12.8 us  [contract(): lax.dot_general(left_side, right_side, (((1,), (1,)), ((), ())), preferre...]
    psum x1 -> x0, waiting for transfers between devices: 40.4 us -> none  [local(): summed = lax.psum(partials, 'tensor')]
    another operation x0 -> x1, loops' own time: none -> 21.5 us  [local_four(): lax.switch(branch, [functools.partial(packed_scores, level) for level in...]
    dynamic_slice x0 -> x6, local copies, waits for them, and re-layouts: none -> 19.9 us  [take(): return lax.dynamic_slice_in_dim(array, start, size, axis)]
  transfers between devices with their start and end apart: 4 -> 56, of which waited for: 4 -> 19; matrix products, arithmetic and copies ran while one was open for 0% -> 7% of each run, Pallas kernels for 0% -> 34%
where the time goes in v2:
time: 544 us; the launch traced here: 534 us
  Pallas kernels  186 us (34%)
  waiting for transfers between devices  146 us (27%)
  starting transfers between devices  104 us (19%)
  local copies, waits for them, and re-layouts  40.3 us (7%)
  loops' own time  21.5 us (4%)
  matrix products  19 us (3%)
  other arithmetic  13.7 us (3%)
    pallas_call x8, Pallas kernels, partial_product(): pl.pallas_call(partial_kernel, grid_spec=pltpu.PrefetchScalarGridSpec(num...  126 us
    ppermute x20, waiting for transfers between devices, move(): return lax.ppermute(array, ('tensor', 'example'), pairs)  113 us
    ppermute x35, starting transfers between devices, swap(): return lax.ppermute(array, axis, [(i, i ^ bits) for i in range(count)])  57 us
    ppermute x20, starting transfers between devices, move(): return lax.ppermute(array, ('tensor', 'example'), pairs)  43.2 us
    pallas_call x3, Pallas kernels, pack(): pl.pallas_call(functools.partial(pack_kernel, starts, sizes), grid_spec=p...  35.8 us
    ppermute x35, waiting for transfers between devices, swap(): return lax.ppermute(array, axis, [(i, i ^ bits) for i in range(count)])  32.8 us
    pallas_call x4, Pallas kernels, finish(): pl.pallas_call(finish_kernel, grid_spec=pltpu.PrefetchScalarGridSpec(num_...  23.9 us
    another operation x1, loops' own time, local_four(): lax.switch(branch, [functools.partial(packed_scores, level) for level in...  21.5 us
  transfers between devices with their start and end apart: 56, of which 19 were waited for; matrix products, arithmetic and copies ran while one was open for 7% of the time, Pallas kernels for 34%

profile of v2, /device:TPU:0, one launch (start us, length us, event | category | flops | bytes accessed | tf_op | source)
XLA Modules:
  0.0 534.1 jit_solution(1772850136955071917)
XLA Ops:
  0.5 2.9 collective-permute-start.307
  9.4 3.4 collective-permute-start.309
  13.6 1.4 fusion.422
  15.7 517.3 %conditional.1 = (f32[8,128]{1,0:T(8,128)S(1)}) conditional(s32[]{:T(128)} %clamp.3, (s32[4]{0:T(128)}, s32[4]{0:T(128)S(1)}, s32[16]{0:T(128)}, bf16[4,128,2048]{2,1,0:T(8,128)(2,1)}, bf16[64,2048]{1,0:T(8,128)(2,1)}, /*index=5*/bf16[4,128,7168]{2,1,0:T(8,128)(2,1)}, bf16[4,128,7168]{2,1,0:T(8,128)(2,1)}, ...), branch_computations={%region_5.10_spmd, %region_10.15_spmd, %region_15.20_spmd, %region... | conditional | flops 80760029184 | bytes 976615552 | solution.py:401
  24.4 13.5 %constant_dynamic-slice_fusion.35 = bf16[3584,2048]{1,0:T(8,128)(2,1)} fusion(bf16[7168,2048]{1,0:T(8,128)(2,1)} %get-tuple-element.329.keep_ref, s32[]{:T(128)S(6)} %select_n.1949), kind=kLoop, calls=%fused_computation.575 | loop fusion | bytes 29360132 | tf_op jit(solution)/shard_map/cond/branch_3_fun/dynamic_slice | solution.py:40
  41.2 5.2 pack_rows.27
  46.4 1.4 collective-permute-start.162
  50.8 2.5 fusion.445
  54.1 9.6 %fusion.212 = f32[512,64]{0,1:T(8,128)S(1)} fusion(bf16[64,7168]{1,0:T(8,128)(2,1)S(1)} %copy-done.237, bf16[512,7168]{1,0:T(8,128)(2,1)} %bitcast.453, bf16[512,7168]{1,0:T(8,128)(2,1)} %bitcast.429), kind=kOutput, calls=%fused_computation.460 | convolution fusion | flops 499122176 | bytes 15728640 | tf_op jit(solution)/shard_map/cond/branch_3_fun/dot_general | solution.py:17
  64.8 4.0 collective-permute-start.163
  73.2 4.0 collective-permute-done.153
  77.2 4.5 collective-permute-start.174
  81.7 3.5 collective-permute-done.181
  86.6 8.0 %collective-permute-start.154 = (bf16[192,2048]{1,0:T(8,128)(2,1)S(1)}, bf16[192,2048]{1,0:T(8,128)(2,1)}, u32[]{:S(2)}, u32[]{:S(2)}) collective-permute-start(bf16[192,2048]{1,0:T(8,128)(2,1)S(1)} %constant_dynamic-update-slice_fusion.24), channel_id=1, source_target_pairs={{0,4},{1,5},{4,8},{5,9},{10,6},{11,7},{14,10},{15,11},{16,20},{17,... | collective-permute-start | bytes 2359304 | tf_op jit(solution)/shard_map/cond/branch_3_fun/ppermute | solution.py:68
  95.5 1.6 collective-permute-start.164
  97.1 2.0 constant_dynamic-slice_fusion.34
  99.1 4.4 collective-permute-done.174
  103.5 1.6 collective-permute-start.175
  105.1 4.7 collective-permute-done.177
  109.7 7.2 %collective-permute-start.182 = (bf16[192,2048]{1,0:T(8,128)(2,1)S(1)}, bf16[192,2048]{1,0:T(8,128)(2,1)}, u32[]{:S(2)}, u32[]{:S(2)}) collective-permute-start(bf16[192,2048]{1,0:T(8,128)(2,1)S(1)} %constant_dynamic-update-slice_fusion.30), channel_id=1, source_target_pairs={{0,4},{1,5},{4,8},{5,9},{10,6},{11,7},{14,10},{15,11},{16,20},{17,... | collective-permute-start | bytes 2359304 | tf_op jit(solution)/shard_map/cond/branch_3_fun/ppermute | solution.py:68
  116.9 3.4 collective-permute-done.154
  120.3 1.5 collective-permute-start.155
  121.9 1.6 collective-permute-start.165
  123.5 4.3 constant_dynamic-slice_fusion.33
  128.6 8.2 %collective-permute-done.182 = bf16[192,2048]{1,0:T(8,128)(2,1)} collective-permute-done((bf16[192,2048]{1,0:T(8,128)(2,1)S(1)}, bf16[192,2048]{1,0:T(8,128)(2,1)}, u32[]{:S(2)}, u32[]{:S(2)}) %collective-permute-start.182) | collective-permute-done | bytes 786464 | tf_op jit(solution)/shard_map/cond/branch_3_fun/ppermute | solution.py:68
  141.0 1.7 broadcast_select_fusion.27
  142.7 51.1 %collective-permute-done.157 = bf16[192,2048]{1,0:T(8,128)(2,1)S(1)} collective-permute-done((bf16[192,2048]{1,0:T(8,128)(2,1)S(1)}, bf16[192,2048]{1,0:T(8,128)(2,1)S(1)}, u32[]{:S(2)}, u32[]{:S(2)}) %collective-permute-start.157) | collective-permute-done | bytes 786464 | tf_op jit(solution)/shard_map/cond/branch_3_fun/ppermute | solution.py:68
  195.8 1.7 broadcast_select_fusion.24
  197.7 33.2 %collective-permute-done.185 = bf16[192,2048]{1,0:T(8,128)(2,1)S(1)} collective-permute-done((bf16[192,2048]{1,0:T(8,128)(2,1)S(1)}, bf16[192,2048]{1,0:T(8,128)(2,1)S(1)}, u32[]{:S(2)}, u32[]{:S(2)}) %collective-permute-start.185) | collective-permute-done | bytes 786464 | tf_op jit(solution)/shard_map/cond/branch_3_fun/ppermute | solution.py:68
  230.9 21.3 %collective-permute-start.159 = (f32[1536,64]{0,1:T(8,128)S(1)}, f32[1536,64]{0,1:T(8,128)S(1)}, u32[]{:S(2)}, u32[]{:S(2)}) collective-permute-start(f32[1536,64]{0,1:T(8,128)S(1)} %pad_maximum_fusion.6), channel_id=1, source_target_pairs={{0,8},{4,12},{8,0},{12,4},{1,9},{5,13},{9,1},{13,5},{2,10},{6,14},... | collective-permute-start | bytes 1179656 | tf_op jit(solution)/shard_map/cond/branch_3_fun/ppermute | solution.py:45
  252.2 1.4 broadcast_select_fusion.25
  253.7 7.8 %collective-permute-start.160 = (f32[1536,64]{0,1:T(8,128)S(1)}, f32[1536,64]{0,1:T(8,128)S(1)}, u32[]{:S(2)}, u32[]{:S(2)}) collective-permute-start(f32[1536,64]{0,1:T(8,128)S(1)} %pad_maximum_fusion.6), channel_id=1, source_target_pairs={{0,12},{4,8},{8,4},{12,0},{1,13},{5,9},{9,5},{13,1},{2,14},{6,10},... | collective-permute-start | bytes 1179656 | tf_op jit(solution)/shard_map/cond/branch_3_fun/ppermute | solution.py:45
  261.6 14.6 %collective-permute-done.159 = f32[1536,64]{0,1:T(8,128)S(1)} collective-permute-done((f32[1536,64]{0,1:T(8,128)S(1)}, f32[1536,64]{0,1:T(8,128)S(1)}, u32[]{:S(2)}, u32[]{:S(2)}) %collective-permute-start.159) | collective-permute-done | bytes 393248 | tf_op jit(solution)/shard_map/cond/branch_3_fun/ppermute | solution.py:45
  277.1 1.5 collective-permute-done.161
  278.7 1.7 fusion.214
  282.2 21.3 %pack_rows.28 = (bf16[192,3584]{1,0:T(8,128)(2,1)S(1)}, bf16[192,3584]{1,0:T(8,128)(2,1)S(1)}, bf16[192,3584]{1,0:T(8,128)(2,1)S(1)}, bf16[192,3584]{1,0:T(8,128)(2,1)S(1)}) custom-call(s32[1]{0:T(128)} %bitcast.67.near_ref, s32[1,1024]{1,0:T(1,128)S(1)} %bitcast_select_fusion.3.place_ref, bf16[512,7168]{1,0:T(8,128)(2,1)} %bitcast.430, ...), custom_call_target="tpu_custom_call" | custom-call | flops 5637144576 | bytes 12845056 | tf_op jit(solution)/shard_map/cond/branch_3_fun/pack_rows/pallas_call | solution.py:99
  308.4 9.3 %pack_rows.29 = (bf16[192,3584]{1,0:T(8,128)(2,1)S(1)}, bf16[192,3584]{1,0:T(8,128)(2,1)S(1)}, bf16[192,3584]{1,0:T(8,128)(2,1)S(1)}, bf16[192,3584]{1,0:T(8,128)(2,1)S(1)}) custom-call(s32[1]{0:T(128)} %bitcast.67.near_ref, s32[1,1024]{1,0:T(1,128)S(1)} %bitcast_select_fusion.3.place_ref, bf16[512,7168]{1,0:T(8,128)(2,1)} %bitcast.455, ...), custom_call_target="tpu_custom_call" | custom-call | flops 5637144576 | bytes 12845056 | tf_op jit(solution)/shard_map/cond/branch_3_fun/pack_rows/pallas_call | solution.py:99
  322.7 16.2 %partial_product.73 = bf16[192,3584]{1,0:T(8,128)(2,1)} custom-call(s32[1]{0:T(128)} %bitcast.67.near_ref, bf16[192,2048]{1,0:T(8,128)(2,1)S(1)} %broadcast_select_fusion.30.a0, bf16[192,2048]{1,0:T(8,128)(2,1)S(1)} %collective-permute-done.167.a1, bf16[192,2048]{1,0:T(8,128)(2,1)S(1)} %get-tuple-element.469.b0, ...), custom_call_target="tpu_custom_call" | custom-call | flops 5637144576 | bytes 32112640 | tf_op jit(solution)/shard_map/cond/branch_3_fun/partial_product/pallas_call | solution.py:142
  340.0 16.2 %partial_product.75 = bf16[192,3584]{1,0:T(8,128)(2,1)} custom-call(s32[1]{0:T(128)} %bitcast.67.near_ref, bf16[192,2048]{1,0:T(8,128)(2,1)S(1)} %broadcast_select_fusion.28.a0, bf16[192,2048]{1,0:T(8,128)(2,1)S(1)} %collective-permute-done.178.a1, bf16[192,2048]{1,0:T(8,128)(2,1)S(1)} %get-tuple-element.472.b0, ...), custom_call_target="tpu_custom_call" | custom-call | flops 5637144576 | bytes 32112640 | tf_op jit(solution)/shard_map/cond/branch_3_fun/partial_product/pallas_call | solution.py:142
  357.5 16.2 %partial_product.77 = bf16[192,3584]{1,0:T(8,128)(2,1)} custom-call(s32[1]{0:T(128)} %bitcast.67.near_ref, bf16[192,2048]{1,0:T(8,128)(2,1)S(1)} %broadcast_select_fusion.26.a0, bf16[192,2048]{1,0:T(8,128)(2,1)S(1)} %collective-permute-done.186.a1, bf16[192,2048]{1,0:T(8,128)(2,1)S(1)} %get-tuple-element.475.b0, ...), custom_call_target="tpu_custom_call" | custom-call | flops 5637144576 | bytes 32112640 | tf_op jit(solution)/shard_map/cond/branch_3_fun/partial_product/pallas_call | solution.py:142
  374.4 16.2 %partial_product.79 = bf16[192,3584]{1,0:T(8,128)(2,1)} custom-call(s32[1]{0:T(128)} %bitcast.67.near_ref, bf16[192,2048]{1,0:T(8,128)(2,1)S(1)} %broadcast_select_fusion.31.a0, bf16[192,2048]{1,0:T(8,128)(2,1)S(1)} %collective-permute-done.189.a1, bf16[192,2048]{1,0:T(8,128)(2,1)S(1)} %get-tuple-element.478.b0, ...), custom_call_target="tpu_custom_call" | custom-call | flops 5637144576 | bytes 32112640 | tf_op jit(solution)/shard_map/cond/branch_3_fun/partial_product/pallas_call | solution.py:142
  391.9 15.3 %partial_product.72.own_ref = f32[192,3584]{1,0:T(8,128)S(1)} custom-call(s32[1]{0:T(128)} %bitcast.67.near_ref, bf16[192,2048]{1,0:T(8,128)(2,1)S(1)} %broadcast_select_fusion.30.a0, bf16[192,2048]{1,0:T(8,128)(2,1)S(1)} %collective-permute-done.167.a1, bf16[192,2048]{1,0:T(8,128)(2,1)S(1)} %get-tuple-element.469.b0, ...), custom_call_target="tpu_custom_call" | custom-call | flops 5637144576 | bytes 32112640 | tf_op jit(solution)/shard_map/cond/branch_3_fun/partial_product/pallas_call | solution.py:142
  407.3 1.5 copy-done.10
  408.8 15.3 %partial_product.74.own_ref = f32[192,3584]{1,0:T(8,128)S(1)} custom-call(s32[1]{0:T(128)} %bitcast.67.near_ref, bf16[192,2048]{1,0:T(8,128)(2,1)S(1)} %broadcast_select_fusion.28.a0, bf16[192,2048]{1,0:T(8,128)(2,1)S(1)} %collective-permute-done.178.a1, bf16[192,2048]{1,0:T(8,128)(2,1)S(1)} %get-tuple-element.472.b0, ...), custom_call_target="tpu_custom_call" | custom-call | flops 5637144576 | bytes 32112640 | tf_op jit(solution)/shard_map/cond/branch_3_fun/partial_product/pallas_call | solution.py:142
  424.1 1.6 copy-done.8
  425.7 15.3 %partial_product.76.own_ref = f32[192,3584]{1,0:T(8,128)S(1)} custom-call(s32[1]{0:T(128)} %bitcast.67.near_ref, bf16[192,2048]{1,0:T(8,128)(2,1)S(1)} %broadcast_select_fusion.26.a0, bf16[192,2048]{1,0:T(8,128)(2,1)S(1)} %collective-permute-done.186.a1, bf16[192,2048]{1,0:T(8,128)(2,1)S(1)} %get-tuple-element.475.b0, ...), custom_call_target="tpu_custom_call" | custom-call | flops 5637144576 | bytes 32112640 | tf_op jit(solution)/shard_map/cond/branch_3_fun/partial_product/pallas_call | solution.py:142
  441.1 1.6 copy-done.6
  442.6 15.5 %partial_product.78.own_ref = f32[192,3584]{1,0:T(8,128)S(1)} custom-call(s32[1]{0:T(128)} %bitcast.67.near_ref, bf16[192,2048]{1,0:T(8,128)(2,1)S(1)} %broadcast_select_fusion.31.a0, bf16[192,2048]{1,0:T(8,128)(2,1)S(1)} %collective-permute-done.189.a1, bf16[192,2048]{1,0:T(8,128)(2,1)S(1)} %get-tuple-element.478.b0, ...), custom_call_target="tpu_custom_call" | custom-call | flops 5637144576 | bytes 32112640 | tf_op jit(solution)/shard_map/cond/branch_3_fun/partial_product/pallas_call | solution.py:142
  458.2 1.5 copy-done.3
  459.7 6.0 %finish_chunk.36 = (f32[192,64]{1,0:T(8,128)S(1)}, f32[192,64]{1,0:T(8,128)S(1)}) custom-call(s32[1]{0:T(128)} %bitcast.67.near_ref, f32[192,3584]{1,0:T(8,128)} %copy-done.10, bf16[192,3584]{1,0:T(8,128)(2,1)} %collective-permute-done.170.came_ref, bf16[192,3584]{1,0:T(8,128)(2,1)S(1)} %copy-done.83, bf16[192,3584]{1,0:T(8,128)(2,1)S(1)} %copy-done.93, ...), custom_call_target="tpu_custom_call" | custom-call | flops 176160768 | bytes 6881280 | tf_op jit(solution)/shard_map/cond/branch_3_fun/finish_chunk/pallas_call | solution.py:189
  465.8 6.0 %finish_chunk.37 = (f32[192,64]{1,0:T(8,128)S(1)}, f32[192,64]{1,0:T(8,128)S(1)}) custom-call(s32[1]{0:T(128)} %bitcast.67.near_ref, f32[192,3584]{1,0:T(8,128)} %copy-done.8, bf16[192,3584]{1,0:T(8,128)(2,1)} %collective-permute-done.180.came_ref, bf16[192,3584]{1,0:T(8,128)(2,1)S(1)} %copy-done.73, bf16[192,3584]{1,0:T(8,128)(2,1)S(1)} %copy-done.89, ...), custom_call_target="tpu_custom_call" | custom-call | flops 176160768 | bytes 6881280 | tf_op jit(solution)/shard_map/cond/branch_3_fun/finish_chunk/pallas_call | solution.py:189
  471.9 6.0 %finish_chunk.38 = (f32[192,64]{1,0:T(8,128)S(1)}, f32[192,64]{1,0:T(8,128)S(1)}) custom-call(s32[1]{0:T(128)} %bitcast.67.near_ref, f32[192,3584]{1,0:T(8,128)} %copy-done.6, bf16[192,3584]{1,0:T(8,128)(2,1)} %collective-permute-done.188.came_ref, bf16[192,3584]{1,0:T(8,128)(2,1)S(1)} %copy-done.61, bf16[192,3584]{1,0:T(8,128)(2,1)S(1)} %copy-done.81, ...), custom_call_target="tpu_custom_call" | custom-call | flops 176160768 | bytes 6881280 | tf_op jit(solution)/shard_map/cond/branch_3_fun/finish_chunk/pallas_call | solution.py:189
  477.9 5.9 %finish_chunk.39 = (f32[192,64]{1,0:T(8,128)S(1)}, f32[192,64]{1,0:T(8,128)S(1)}) custom-call(s32[1]{0:T(128)} %bitcast.67.near_ref, f32[192,3584]{1,0:T(8,128)} %copy-done.3, bf16[192,3584]{1,0:T(8,128)(2,1)} %collective-permute-done.191.came_ref, bf16[192,3584]{1,0:T(8,128)(2,1)S(1)} %copy-done.55, bf16[192,3584]{1,0:T(8,128)(2,1)S(1)} %copy-done.69, ...), custom_call_target="tpu_custom_call" | custom-call | flops 176160768 | bytes 6881280 | tf_op jit(solution)/shard_map/cond/branch_3_fun/finish_chunk/pallas_call | solution.py:189
  483.8 1.5 fusion.216
  485.3 6.2 %collective-permute-start.192 = (f32[8,16,128]{2,1,0:T(8,128)S(1)}, f32[8,16,128]{2,1,0:T(8,128)S(1)}, u32[]{:S(2)}, u32[]{:S(2)}) collective-permute-start(f32[8,16,128]{2,1,0:T(8,128)S(1)} %get-tuple-element.562), channel_id=1, source_target_pairs={{0,4},{4,0},{8,12},{12,8},{1,5},{5,1},{9,13},{13,9},{2,6},{6,2},{1... | collective-permute-start | bytes 196616 | tf_op jit(solution)/shard_map/cond/branch_3_fun/ppermute | solution.py:45
  491.5 2.0 collective-permute-start.193
  493.5 1.4 collective-permute-start.194
  495.2 3.6 collective-permute-done.193
  501.7 4.5 collective-permute-done.196
  506.1 1.9 collective-permute-done.197
  512.0 2.0 collective-permute-done.199
  515.2 1.8 collective-permute-start.202
  516.9 1.5 collective-permute-start.203
  519.7 2.7 collective-permute-done.203
  (224 shorter events, 52.1 us)
Async XLA Ops:
  0.0 15.7 %collective-permute-start.310 = (bf16[512,2048]{1,0:T(8,128)(2,1)}, bf16[512,2048]{1,0:T(8,128)(2,1)}, u32[]{:S(2)}, u32[]{:S(2)}) collective-permute-start(bf16[512,2048]{1,0:T(8,128)(2,1)} %bitcast.411), channel_id=1, source_target_pairs={{0,1},{1,0},{2,3},{3,2},{4,5},{5,4},{6,7},{7,6},{8,9},{9,8},{10,11... | collective-permute-start | bytes 6291464 | tf_op jit(solution)/shard_map/ppermute | solution.py:45
  0.5 4.4 collective-permute-start.306
  0.5 6.3 %collective-permute-start.307 = (s32[4]{0:T(128)}, s32[4]{0:T(128)S(1)}, u32[]{:S(2)}, u32[]{:S(2)}) collective-permute-start(s32[4]{0:T(128)} %param.32), channel_id=1, source_target_pairs={{0,2},{1,3},{2,0},{3,1},{4,6},{5,7},{6,4},{7,5},{8,10},{9,11},{10,... | collective-permute-start | bytes 56 | tf_op jit(solution)/shard_map/ppermute | solution.py:45
  3.5 4.0 collective-permute-start.308
  9.4 3.6 collective-permute-start.309
  37.8 284.8 %collective-permute-start.169 = (bf16[3584,2048]{1,0:T(8,128)(2,1)}, bf16[3584,2048]{1,0:T(8,128)(2,1)}, u32[]{:S(2)}, u32[]{:S(2)}) collective-permute-start(bf16[3584,2048]{1,0:T(8,128)(2,1)} %constant_dynamic-slice_fusion.35), channel_id=1, source_target_pairs={{0,1},{1,0},{2,3},{3,2},{4,5},{5,4},{6,7},{7,6},{8,9},{9,8},{10,11... | collective-permute-start | bytes 44040200 | tf_op jit(solution)/shard_map/cond/branch_3_fun/ppermute | solution.py:45
  46.4 17.4 %collective-permute-start.162 = (bf16[96,2048]{1,0:T(8,128)(2,1)S(1)}, bf16[96,2048]{1,0:T(8,128)(2,1)}, u32[]{:S(2)}, u32[]{:S(2)}) collective-permute-start(bf16[96,2048]{1,0:T(8,128)(2,1)S(1)} %get-tuple-element.328), channel_id=1, source_target_pairs={{2,0},{3,1},{6,4},{7,5},{8,10},{9,11},{12,14},{13,15},{18,16},{19,... | collective-permute-start | bytes 1179656 | tf_op jit(solution)/shard_map/cond/branch_3_fun/ppermute | solution.py:68
  47.8 23.0 %collective-permute-start.173 = (bf16[96,2048]{1,0:T(8,128)(2,1)S(1)}, bf16[96,2048]{1,0:T(8,128)(2,1)}, u32[]{:S(2)}, u32[]{:S(2)}) collective-permute-start(bf16[96,2048]{1,0:T(8,128)(2,1)S(1)} %get-tuple-element.336), channel_id=1, source_target_pairs={{2,0},{3,1},{6,4},{7,5},{8,10},{9,11},{12,14},{13,15},{18,16},{19,... | collective-permute-start | bytes 1179656 | tf_op jit(solution)/shard_map/cond/branch_3_fun/ppermute | solution.py:68
  49.1 28.1 %collective-permute-start.153 = (bf16[96,2048]{1,0:T(8,128)(2,1)S(1)}, bf16[96,2048]{1,0:T(8,128)(2,1)S(1)}, u32[]{:S(2)}, u32[]{:S(2)}) collective-permute-start(bf16[96,2048]{1,0:T(8,128)(2,1)S(1)} %get-tuple-element.326), channel_id=1, source_target_pairs={{2,0},{3,1},{6,4},{7,5},{8,10},{9,11},{12,14},{13,15},{18,16},{19,... | collective-permute-start | bytes 1179656 | tf_op jit(solution)/shard_map/cond/branch_3_fun/ppermute | solution.py:68
  54.0 43.0 %slice-start.2 = ((s8[7340032]{0:T(1024)(128)(4,1)}), s8[4194304]{0:T(1024)(128)(4,1)S(1)}, s32[]{:S(2)}) async-start(s8[7340032]{0:T(1024)(128)(4,1)} %bitcast.431), calls=%async_computation.2 | async-start | bytes 8388608 | tf_op jit(solution)/shard_map/cond
  54.1 43.0 %slice-start.3 = ((s8[7340032]{0:T(1024)(128)(4,1)}), s8[3145728]{0:T(1024)(128)(4,1)S(1)}, s32[]{:S(2)}) async-start(s8[7340032]{0:T(1024)(128)(4,1)} %bitcast.431), calls=%async_computation.3 | async-start | bytes 6291456 | tf_op jit(solution)/shard_map/cond
  64.8 21.7 %copy-start.178 = (bf16[192,2048]{1,0:T(8,128)(2,1)}, bf16[192,2048]{1,0:T(8,128)(2,1)S(1)}, u32[]{:S(2)}) copy-start(bf16[192,2048]{1,0:T(8,128)(2,1)S(1)} %constant_dynamic-update-slice_fusion.26) | copy-start | bytes 2359300 | tf_op jit(solution)/shard_map/cond
  64.8 21.8 %collective-permute-start.163 = (bf16[192,2048]{1,0:T(8,128)(2,1)S(1)}, bf16[192,2048]{1,0:T(8,128)(2,1)S(1)}, u32[]{:S(2)}, u32[]{:S(2)}) collective-permute-start(bf16[192,2048]{1,0:T(8,128)(2,1)S(1)} %constant_dynamic-update-slice_fusion.26), channel_id=1, source_target_pairs={{0,4},{1,5},{4,8},{5,9},{10,6},{11,7},{14,10},{15,11},{16,20},{17,... | collective-permute-start | bytes 2359304 | tf_op jit(solution)/shard_map/cond/branch_3_fun/ppermute | solution.py:68
  68.8 25.8 %collective-permute-start.166 = (bf16[192,2048]{1,0:T(8,128)(2,1)S(1)}, bf16[192,2048]{1,0:T(8,128)(2,1)S(1)}, u32[]{:S(2)}, u32[]{:S(2)}) collective-permute-start(bf16[192,2048]{1,0:T(8,128)(2,1)S(1)} %constant_dynamic-update-slice_fusion.26), channel_id=1, source_target_pairs={{4,0},{5,1},{10,14},{11,15},{20,16},{21,17},{26,30},{27,31}} | collective-permute-start | bytes 2359304 | tf_op jit(solution)/shard_map/cond/branch_3_fun/ppermute | solution.py:68
  70.8 14.4 %collective-permute-start.181 = (bf16[96,2048]{1,0:T(8,128)(2,1)S(1)}, bf16[96,2048]{1,0:T(8,128)(2,1)S(1)}, u32[]{:S(2)}, u32[]{:S(2)}) collective-permute-start(bf16[96,2048]{1,0:T(8,128)(2,1)S(1)} %get-tuple-element.341), channel_id=1, source_target_pairs={{2,0},{3,1},{6,4},{7,5},{8,10},{9,11},{12,14},{13,15},{18,16},{19,... | collective-permute-start | bytes 1179656 | tf_op jit(solution)/shard_map/cond/branch_3_fun/ppermute | solution.py:68
  73.2 26.0 %copy-start.176 = (bf16[192,2048]{1,0:T(8,128)(2,1)}, bf16[192,2048]{1,0:T(8,128)(2,1)S(1)}, u32[]{:S(2)}) copy-start(bf16[192,2048]{1,0:T(8,128)(2,1)S(1)} %constant_dynamic-update-slice_fusion.28) | copy-start | bytes 2359300 | tf_op jit(solution)/shard_map/cond
  77.2 26.3 %collective-permute-start.174 = (bf16[192,2048]{1,0:T(8,128)(2,1)S(1)}, bf16[192,2048]{1,0:T(8,128)(2,1)}, u32[]{:S(2)}, u32[]{:S(2)}) collective-permute-start(bf16[192,2048]{1,0:T(8,128)(2,1)S(1)} %constant_dynamic-update-slice_fusion.28), channel_id=1, source_target_pairs={{0,4},{1,5},{4,8},{5,9},{10,6},{11,7},{14,10},{15,11},{16,20},{17,... | collective-permute-start | bytes 2359304 | tf_op jit(solution)/shard_map/cond/branch_3_fun/ppermute | solution.py:68
  81.7 17.4 %copy-start.174 = (bf16[192,2048]{1,0:T(8,128)(2,1)}, bf16[192,2048]{1,0:T(8,128)(2,1)S(1)}, u32[]{:S(2)}) copy-start(bf16[192,2048]{1,0:T(8,128)(2,1)S(1)} %constant_dynamic-update-slice_fusion.24) | copy-start | bytes 2359300 | tf_op jit(solution)/shard_map/cond
  85.2 24.5 %collective-permute-start.177 = (bf16[192,2048]{1,0:T(8,128)(2,1)S(1)}, bf16[192,2048]{1,0:T(8,128)(2,1)S(1)}, u32[]{:S(2)}, u32[]{:S(2)}) collective-permute-start(bf16[192,2048]{1,0:T(8,128)(2,1)S(1)} %constant_dynamic-update-slice_fusion.28), channel_id=1, source_target_pairs={{4,0},{5,1},{10,14},{11,15},{20,16},{21,17},{26,30},{27,31}} | collective-permute-start | bytes 2359304 | tf_op jit(solution)/shard_map/cond/branch_3_fun/ppermute | solution.py:68
  86.6 33.7 %collective-permute-start.154 = (bf16[192,2048]{1,0:T(8,128)(2,1)S(1)}, bf16[192,2048]{1,0:T(8,128)(2,1)}, u32[]{:S(2)}, u32[]{:S(2)}) collective-permute-start(bf16[192,2048]{1,0:T(8,128)(2,1)S(1)} %constant_dynamic-update-slice_fusion.24), channel_id=1, source_target_pairs={{0,4},{1,5},{4,8},{5,9},{10,6},{11,7},{14,10},{15,11},{16,20},{17,... | collective-permute-start | bytes 2359304 | tf_op jit(solution)/shard_map/cond/branch_3_fun/ppermute | solution.py:68
  95.5 26.4 %collective-permute-start.164 = (bf16[192,2048]{1,0:T(8,128)(2,1)S(1)}, bf16[192,2048]{1,0:T(8,128)(2,1)}, u32[]{:S(2)}, u32[]{:S(2)}) collective-permute-start(bf16[192,2048]{1,0:T(8,128)(2,1)S(1)} %collective-permute-done.163), channel_id=1, source_target_pairs={{4,8},{5,9},{6,2},{7,3},{8,12},{9,13},{10,6},{11,7},{20,24},{21,25... | collective-permute-start | bytes 2359304 | tf_op jit(solution)/shard_map/cond/branch_3_fun/ppermute | solution.py:68
  103.5 24.3 %collective-permute-start.175 = (bf16[192,2048]{1,0:T(8,128)(2,1)}, bf16[192,2048]{1,0:T(8,128)(2,1)}, u32[]{:S(2)}, u32[]{:S(2)}) collective-permute-start(bf16[192,2048]{1,0:T(8,128)(2,1)} %collective-permute-done.174), channel_id=1, source_target_pairs={{4,8},{5,9},{6,2},{7,3},{8,12},{9,13},{10,6},{11,7},{20,24},{21,25... | collective-permute-start | bytes 2359304 | tf_op jit(solution)/shard_map/cond/branch_3_fun/ppermute | solution.py:68
  109.7 27.1 %collective-permute-start.182 = (bf16[192,2048]{1,0:T(8,128)(2,1)S(1)}, bf16[192,2048]{1,0:T(8,128)(2,1)}, u32[]{:S(2)}, u32[]{:S(2)}) collective-permute-start(bf16[192,2048]{1,0:T(8,128)(2,1)S(1)} %constant_dynamic-update-slice_fusion.30), channel_id=1, source_target_pairs={{0,4},{1,5},{4,8},{5,9},{10,6},{11,7},{14,10},{15,11},{16,20},{17,... | collective-permute-start | bytes 2359304 | tf_op jit(solution)/shard_map/cond/branch_3_fun/ppermute | solution.py:68
  120.3 17.8 %collective-permute-start.155 = (bf16[192,2048]{1,0:T(8,128)(2,1)}, bf16[192,2048]{1,0:T(8,128)(2,1)}, u32[]{:S(2)}, u32[]{:S(2)}) collective-permute-start(bf16[192,2048]{1,0:T(8,128)(2,1)} %collective-permute-done.154), channel_id=1, source_target_pairs={{4,8},{5,9},{6,2},{7,3},{8,12},{9,13},{10,6},{11,7},{20,24},{21,25... | collective-permute-start | bytes 2359304 | tf_op jit(solution)/shard_map/cond/branch_3_fun/ppermute | solution.py:68
  121.9 16.9 %collective-permute-start.165 = (bf16[192,2048]{1,0:T(8,128)(2,1)}, bf16[192,2048]{1,0:T(8,128)(2,1)}, u32[]{:S(2)}, u32[]{:S(2)}) collective-permute-start(bf16[192,2048]{1,0:T(8,128)(2,1)} %collective-permute-done.164), channel_id=1, source_target_pairs={{6,2},{7,3},{8,12},{9,13},{22,18},{23,19},{24,28},{25,29}} | collective-permute-start | bytes 2359304 | tf_op jit(solution)/shard_map/cond/branch_3_fun/ppermute | solution.py:68
  127.8 13.1 %collective-permute-start.176 = (bf16[192,2048]{1,0:T(8,128)(2,1)}, bf16[192,2048]{1,0:T(8,128)(2,1)S(1)}, u32[]{:S(2)}, u32[]{:S(2)}) collective-permute-start(bf16[192,2048]{1,0:T(8,128)(2,1)} %collective-permute-done.175), channel_id=1, source_target_pairs={{6,2},{7,3},{8,12},{9,13},{22,18},{23,19},{24,28},{25,29}} | collective-permute-start | bytes 2359304 | tf_op jit(solution)/shard_map/cond/branch_3_fun/ppermute | solution.py:68
  136.8 57.0 %collective-permute-start.157 = (bf16[192,2048]{1,0:T(8,128)(2,1)S(1)}, bf16[192,2048]{1,0:T(8,128)(2,1)S(1)}, u32[]{:S(2)}, u32[]{:S(2)}) collective-permute-start(bf16[192,2048]{1,0:T(8,128)(2,1)S(1)} %copy-done.175), channel_id=1, source_target_pairs={{4,0},{5,1},{10,14},{11,15},{20,16},{21,17},{26,30},{27,31}} | collective-permute-start | bytes 2359304 | tf_op jit(solution)/shard_map/cond/branch_3_fun/ppermute | solution.py:68
  138.1 55.7 %collective-permute-start.183 = (bf16[192,2048]{1,0:T(8,128)(2,1)}, bf16[192,2048]{1,0:T(8,128)(2,1)S(1)}, u32[]{:S(2)}, u32[]{:S(2)}) collective-permute-start(bf16[192,2048]{1,0:T(8,128)(2,1)} %collective-permute-done.182), channel_id=1, source_target_pairs={{4,8},{5,9},{6,2},{7,3},{8,12},{9,13},{10,6},{11,7},{20,24},{21,25... | collective-permute-start | bytes 2359304 | tf_op jit(solution)/shard_map/cond/branch_3_fun/ppermute | solution.py:68
  138.8 56.3 %collective-permute-start.156 = (bf16[192,2048]{1,0:T(8,128)(2,1)}, bf16[192,2048]{1,0:T(8,128)(2,1)S(1)}, u32[]{:S(2)}, u32[]{:S(2)}) collective-permute-start(bf16[192,2048]{1,0:T(8,128)(2,1)} %collective-permute-done.155), channel_id=1, source_target_pairs={{6,2},{7,3},{8,12},{9,13},{22,18},{23,19},{24,28},{25,29}} | collective-permute-start | bytes 2359304 | tf_op jit(solution)/shard_map/cond/branch_3_fun/ppermute | solution.py:68
  140.9 139.5 %collective-permute-start.171 = (bf16[512,3584]{1,0:T(8,128)(2,1)S(1)}, bf16[512,3584]{1,0:T(8,128)(2,1)S(1)}, u32[]{:S(2)}, u32[]{:S(2)}) collective-permute-start(bf16[512,3584]{1,0:T(8,128)(2,1)S(1)} %copy-done.165), channel_id=1, source_target_pairs={{0,1},{1,0},{2,3},{3,2},{4,5},{5,4},{6,7},{7,6},{8,9},{9,8},{10,11... | collective-permute-start | bytes 11010056 | tf_op jit(solution)/shard_map/cond/branch_3_fun/ppermute | solution.py:45
  193.8 114.2 %collective-permute-start.172 = (bf16[512,3584]{1,0:T(8,128)(2,1)}, bf16[512,3584]{1,0:T(8,128)(2,1)}, u32[]{:S(2)}, u32[]{:S(2)}) collective-permute-start(bf16[512,3584]{1,0:T(8,128)(2,1)} %constant_dynamic-slice_fusion.33), channel_id=1, source_target_pairs={{0,1},{1,0},{2,3},{3,2},{4,5},{5,4},{6,7},{7,6},{8,9},{9,8},{10,11... | collective-permute-start | bytes 11010056 | tf_op jit(solution)/shard_map/cond/branch_3_fun/ppermute | solution.py:45
  193.8 37.1 %collective-permute-start.185 = (bf16[192,2048]{1,0:T(8,128)(2,1)S(1)}, bf16[192,2048]{1,0:T(8,128)(2,1)S(1)}, u32[]{:S(2)}, u32[]{:S(2)}) collective-permute-start(bf16[192,2048]{1,0:T(8,128)(2,1)S(1)} %constant_dynamic-update-slice_fusion.30), channel_id=1, source_target_pairs={{4,0},{5,1},{10,14},{11,15},{20,16},{21,17},{26,30},{27,31}} | collective-permute-start | bytes 2359304 | tf_op jit(solution)/shard_map/cond/branch_3_fun/ppermute | solution.py:68
  195.1 35.8 %collective-permute-start.184 = (bf16[192,2048]{1,0:T(8,128)(2,1)S(1)}, bf16[192,2048]{1,0:T(8,128)(2,1)S(1)}, u32[]{:S(2)}, u32[]{:S(2)}) collective-permute-start(bf16[192,2048]{1,0:T(8,128)(2,1)S(1)} %collective-permute-done.183), channel_id=1, source_target_pairs={{6,2},{7,3},{8,12},{9,13},{22,18},{23,19},{24,28},{25,29}} | collective-permute-start | bytes 2359304 | tf_op jit(solution)/shard_map/cond/branch_3_fun/ppermute | solution.py:68
  230.9 22.8 %collective-permute-start.158 = (f32[1536,64]{0,1:T(8,128)S(1)}, f32[1536,64]{0,1:T(8,128)S(1)}, u32[]{:S(2)}, u32[]{:S(2)}) collective-permute-start(f32[1536,64]{0,1:T(8,128)S(1)} %pad_maximum_fusion.6), channel_id=1, source_target_pairs={{0,4},{4,0},{8,12},{12,8},{1,5},{5,1},{9,13},{13,9},{2,6},{6,2},{1... | collective-permute-start | bytes 1179656 | tf_op jit(solution)/shard_map/cond/branch_3_fun/ppermute | solution.py:45
  230.9 45.2 %collective-permute-start.159 = (f32[1536,64]{0,1:T(8,128)S(1)}, f32[1536,64]{0,1:T(8,128)S(1)}, u32[]{:S(2)}, u32[]{:S(2)}) collective-permute-start(f32[1536,64]{0,1:T(8,128)S(1)} %pad_maximum_fusion.6), channel_id=1, source_target_pairs={{0,8},{4,12},{8,0},{12,4},{1,9},{5,13},{9,1},{13,5},{2,10},{6,14},... | collective-permute-start | bytes 1179656 | tf_op jit(solution)/shard_map/cond/branch_3_fun/ppermute | solution.py:45
  253.7 22.4 %collective-permute-start.160 = (f32[1536,64]{0,1:T(8,128)S(1)}, f32[1536,64]{0,1:T(8,128)S(1)}, u32[]{:S(2)}, u32[]{:S(2)}) collective-permute-start(f32[1536,64]{0,1:T(8,128)S(1)} %pad_maximum_fusion.6), channel_id=1, source_target_pairs={{0,12},{4,8},{8,4},{12,0},{1,13},{5,9},{9,5},{13,1},{2,14},{6,10},... | collective-permute-start | bytes 1179656 | tf_op jit(solution)/shard_map/cond/branch_3_fun/ppermute | solution.py:45
  276.1 46.0 %collective-permute-start.168 = (bf16[192,2048]{1,0:T(8,128)(2,1)S(1)}, bf16[192,2048]{1,0:T(8,128)(2,1)S(1)}, u32[]{:S(2)}, u32[]{:S(2)}) collective-permute-start(bf16[192,2048]{1,0:T(8,128)(2,1)S(1)} %broadcast_select_fusion.30.a0), channel_id=1, source_target_pairs={{0,1},{1,0},{2,3},{3,2},{4,5},{5,4},{6,7},{7,6},{8,9},{9,8},{10,11... | collective-permute-start | bytes 2359304 | tf_op jit(solution)/shard_map/cond/branch_3_fun/ppermute | solution.py:45
  276.3 2.3 collective-permute-start.161
  278.6 43.6 %collective-permute-start.167 = (bf16[192,2048]{1,0:T(8,128)(2,1)S(1)}, bf16[192,2048]{1,0:T(8,128)(2,1)S(1)}, u32[]{:S(2)}, u32[]{:S(2)}) collective-permute-start(bf16[192,2048]{1,0:T(8,128)(2,1)S(1)} %get-tuple-element.469.b0), channel_id=1, source_target_pairs={{0,1},{1,0},{2,3},{3,2},{4,5},{5,4},{6,7},{7,6},{8,9},{9,8},{10,11... | collective-permute-start | bytes 2359304 | tf_op jit(solution)/shard_map/cond/branch_3_fun/ppermute | solution.py:45
  280.5 58.5 %collective-permute-start.179 = (bf16[192,2048]{1,0:T(8,128)(2,1)S(1)}, bf16[192,2048]{1,0:T(8,128)(2,1)S(1)}, u32[]{:S(2)}, u32[]{:S(2)}) collective-permute-start(bf16[192,2048]{1,0:T(8,128)(2,1)S(1)} %broadcast_select_fusion.28.a0), channel_id=1, source_target_pairs={{0,1},{1,0},{2,3},{3,2},{4,5},{5,4},{6,7},{7,6},{8,9},{9,8},{10,11... | collective-permute-start | bytes 2359304 | tf_op jit(solution)/shard_map/cond/branch_3_fun/ppermute | solution.py:45
  308.0 31.3 %collective-permute-start.178 = (bf16[192,2048]{1,0:T(8,128)(2,1)S(1)}, bf16[192,2048]{1,0:T(8,128)(2,1)S(1)}, u32[]{:S(2)}, u32[]{:S(2)}) collective-permute-start(bf16[192,2048]{1,0:T(8,128)(2,1)S(1)} %get-tuple-element.472.b0), channel_id=1, source_target_pairs={{0,1},{1,0},{2,3},{3,2},{4,5},{5,4},{6,7},{7,6},{8,9},{9,8},{10,11... | collective-permute-start | bytes 2359304 | tf_op jit(solution)/shard_map/cond/branch_3_fun/ppermute | solution.py:45
  322.1 52.3 %collective-permute-start.190 = (bf16[192,2048]{1,0:T(8,128)(2,1)S(1)}, bf16[192,2048]{1,0:T(8,128)(2,1)S(1)}, u32[]{:S(2)}, u32[]{:S(2)}) collective-permute-start(bf16[192,2048]{1,0:T(8,128)(2,1)S(1)} %broadcast_select_fusion.31.a0), channel_id=1, source_target_pairs={{0,1},{1,0},{2,3},{3,2},{4,5},{5,4},{6,7},{7,6},{8,9},{9,8},{10,11... | collective-permute-start | bytes 2359304 | tf_op jit(solution)/shard_map/cond/branch_3_fun/ppermute | solution.py:45
  322.2 33.9 %collective-permute-start.187 = (bf16[192,2048]{1,0:T(8,128)(2,1)S(1)}, bf16[192,2048]{1,0:T(8,128)(2,1)S(1)}, u32[]{:S(2)}, u32[]{:S(2)}) collective-permute-start(bf16[192,2048]{1,0:T(8,128)(2,1)S(1)} %broadcast_select_fusion.26.a0), channel_id=1, source_target_pairs={{0,1},{1,0},{2,3},{3,2},{4,5},{5,4},{6,7},{7,6},{8,9},{9,8},{10,11... | collective-permute-start | bytes 2359304 | tf_op jit(solution)/shard_map/cond/branch_3_fun/ppermute | solution.py:45
  322.6 34.9 %collective-permute-start.186 = (bf16[192,2048]{1,0:T(8,128)(2,1)S(1)}, bf16[192,2048]{1,0:T(8,128)(2,1)S(1)}, u32[]{:S(2)}, u32[]{:S(2)}) collective-permute-start(bf16[192,2048]{1,0:T(8,128)(2,1)S(1)} %get-tuple-element.475.b0), channel_id=1, source_target_pairs={{0,1},{1,0},{2,3},{3,2},{4,5},{5,4},{6,7},{7,6},{8,9},{9,8},{10,11... | collective-permute-start | bytes 2359304 | tf_op jit(solution)/shard_map/cond/branch_3_fun/ppermute | solution.py:45
  338.9 35.4 %collective-permute-start.189 = (bf16[192,2048]{1,0:T(8,128)(2,1)S(1)}, bf16[192,2048]{1,0:T(8,128)(2,1)S(1)}, u32[]{:S(2)}, u32[]{:S(2)}) collective-permute-start(bf16[192,2048]{1,0:T(8,128)(2,1)S(1)} %get-tuple-element.478.b0), channel_id=1, source_target_pairs={{0,1},{1,0},{2,3},{3,2},{4,5},{5,4},{6,7},{7,6},{8,9},{9,8},{10,11... | collective-permute-start | bytes 2359304 | tf_op jit(solution)/shard_map/cond/branch_3_fun/ppermute | solution.py:45
  339.3 120.4 %collective-permute-start.170 = (bf16[192,3584]{1,0:T(8,128)(2,1)}, bf16[192,3584]{1,0:T(8,128)(2,1)}, u32[]{:S(2)}, u32[]{:S(2)}) collective-permute-start(bf16[192,3584]{1,0:T(8,128)(2,1)} %partial_product.73), channel_id=1, source_target_pairs={{0,2},{1,3},{2,0},{3,1},{4,6},{5,7},{6,4},{7,5},{8,10},{9,11},{10,... | collective-permute-start | bytes 4128776 | tf_op jit(solution)/shard_map/cond/branch_3_fun/ppermute | solution.py:45
  356.2 109.6 %collective-permute-start.180 = (bf16[192,3584]{1,0:T(8,128)(2,1)}, bf16[192,3584]{1,0:T(8,128)(2,1)}, u32[]{:S(2)}, u32[]{:S(2)}) collective-permute-start(bf16[192,3584]{1,0:T(8,128)(2,1)} %partial_product.75), channel_id=1, source_target_pairs={{0,2},{1,3},{2,0},{3,1},{4,6},{5,7},{6,4},{7,5},{8,10},{9,11},{10,... | collective-permute-start | bytes 4128776 | tf_op jit(solution)/shard_map/cond/branch_3_fun/ppermute | solution.py:45
  373.7 98.1 %collective-permute-start.188 = (bf16[192,3584]{1,0:T(8,128)(2,1)}, bf16[192,3584]{1,0:T(8,128)(2,1)}, u32[]{:S(2)}, u32[]{:S(2)}) collective-permute-start(bf16[192,3584]{1,0:T(8,128)(2,1)} %partial_product.77), channel_id=1, source_target_pairs={{0,2},{1,3},{2,0},{3,1},{4,6},{5,7},{6,4},{7,5},{8,10},{9,11},{10,... | collective-permute-start | bytes 4128776 | tf_op jit(solution)/shard_map/cond/branch_3_fun/ppermute | solution.py:45
  390.5 87.4 %collective-permute-start.191 = (bf16[192,3584]{1,0:T(8,128)(2,1)}, bf16[192,3584]{1,0:T(8,128)(2,1)}, u32[]{:S(2)}, u32[]{:S(2)}) collective-permute-start(bf16[192,3584]{1,0:T(8,128)(2,1)} %partial_product.79), channel_id=1, source_target_pairs={{0,2},{1,3},{2,0},{3,1},{4,6},{5,7},{6,4},{7,5},{8,10},{9,11},{10,... | collective-permute-start | bytes 4128776 | tf_op jit(solution)/shard_map/cond/branch_3_fun/ppermute | solution.py:45
  442.6 17.1 %copy-start.129 = (bf16[64,7168]{1,0:T(8,128)(2,1)S(1)}, bf16[64,7168]{1,0:T(8,128)(2,1)}, u32[]{:S(2)}) copy-start(bf16[64,7168]{1,0:T(8,128)(2,1)} %get-tuple-element.333.proj_up_ref) | copy-start | bytes 2752516 | tf_op jit(solution)/shard_map/cond
  483.8 17.9 %copy-start.219 = (s32[256]{0:T(256)S(1)}, s32[256]{0:T(256)}, u32[]{:S(2)}) copy-start(s32[256]{0:T(256)} %get-tuple-element.351) | copy-start | bytes 3076 | tf_op jit(solution)/shard_map/cond
  483.8 24.4 %copy-start.146 = (bf16[256,3072]{1,0:T(8,128)(2,1)S(1)}, bf16[256,3072]{1,0:T(8,128)(2,1)}, u32[]{:S(2)}) copy-start(bf16[256,3072]{1,0:T(8,128)(2,1)} %get-tuple-element.350) | copy-start | bytes 4718596 | tf_op jit(solution)/shard_map/cond
  485.3 9.9 %collective-permute-start.192 = (f32[8,16,128]{2,1,0:T(8,128)S(1)}, f32[8,16,128]{2,1,0:T(8,128)S(1)}, u32[]{:S(2)}, u32[]{:S(2)}) collective-permute-start(f32[8,16,128]{2,1,0:T(8,128)S(1)} %get-tuple-element.562), channel_id=1, source_target_pairs={{0,4},{4,0},{8,12},{12,8},{1,5},{5,1},{9,13},{13,9},{2,6},{6,2},{1... | collective-permute-start | bytes 196616 | tf_op jit(solution)/shard_map/cond/branch_3_fun/ppermute | solution.py:45
  491.5 7.2 %collective-permute-start.193 = (f32[8,16,128]{2,1,0:T(8,128)S(1)}, f32[8,16,128]{2,1,0:T(8,128)S(1)}, u32[]{:S(2)}, u32[]{:S(2)}) collective-permute-start(f32[8,16,128]{2,1,0:T(8,128)S(1)} %get-tuple-element.564), channel_id=1, source_target_pairs={{0,8},{4,12},{8,0},{12,4},{1,9},{5,13},{9,1},{13,5},{2,10},{6,14},... | collective-permute-start | bytes 196616 | tf_op jit(solution)/shard_map/cond/branch_3_fun/ppermute | solution.py:45
  493.5 6.1 %collective-permute-start.194 = (f32[8,16,128]{2,1,0:T(8,128)S(1)}, f32[8,16,128]{2,1,0:T(8,128)S(1)}, u32[]{:S(2)}, u32[]{:S(2)}) collective-permute-start(f32[8,16,128]{2,1,0:T(8,128)S(1)} %get-tuple-element.563), channel_id=1, source_target_pairs={{0,12},{4,8},{8,4},{12,0},{1,13},{5,9},{9,5},{13,1},{2,14},{6,10},... | collective-permute-start | bytes 196616 | tf_op jit(solution)/shard_map/cond/branch_3_fun/ppermute | solution.py:45
  499.7 2.0 collective-permute-start.195
  499.8 6.4 %collective-permute-start.196 = (f32[8,16,192]{2,1,0:T(8,128)S(1)}, f32[8,16,192]{2,1,0:T(8,128)S(1)}, u32[]{:S(2)}, u32[]{:S(2)}) collective-permute-start(f32[8,16,192]{2,1,0:T(8,128)S(1)} %pad_maximum_fusion.7), channel_id=1, source_target_pairs={{0,2},{1,3},{2,0},{3,1},{4,6},{5,7},{6,4},{7,5},{8,10},{9,11},{10,... | collective-permute-start | bytes 294920 | tf_op jit(solution)/shard_map/cond/branch_3_fun/ppermute | solution.py:45
  500.3 7.8 %collective-permute-start.197 = (f32[8,16,192]{2,1,0:T(8,128)S(1)}, f32[8,16,192]{2,1,0:T(8,128)S(1)}, u32[]{:S(2)}, u32[]{:S(2)}) collective-permute-start(f32[8,16,192]{2,1,0:T(8,128)S(1)} %pad_maximum_fusion.7), channel_id=1, source_target_pairs={{0,3},{1,2},{2,1},{3,0},{4,7},{5,6},{6,5},{7,4},{8,11},{9,10},{10,... | collective-permute-start | bytes 294920 | tf_op jit(solution)/shard_map/cond/branch_3_fun/ppermute | solution.py:45
  510.1 1.9 collective-permute-start.198
  510.4 3.6 collective-permute-start.199
  510.8 3.2 collective-permute-start.200
  514.0 4.5 collective-permute-start.201
  515.2 4.5 collective-permute-start.202
  516.9 5.4 %collective-permute-start.203 = (f32[8,128]{1,0:T(8,128)S(1)}, f32[8,128]{1,0:T(8,128)S(1)}, u32[]{:S(2)}, u32[]{:S(2)}) collective-permute-start(f32[8,128]{1,0:T(8,128)S(1)} %add_add_fusion.15), channel_id=1, source_target_pairs={{0,12},{4,8},{8,4},{12,0},{1,13},{5,9},{9,5},{13,1},{2,14},{6,10},... | collective-permute-start | bytes 12296 | tf_op jit(solution)/shard_map/cond/branch_3_fun/ppermute | solution.py:45
  (39 other events, 273.6 us)

commit v3 on v2

--- a/solution.py
+++ b/solution.py
@@ -10,6 +10,7 @@
 CHUNKS = 4
 LEVELS = (672, 704, 736, 768, 832)
 TILE = 512
+WIDE = 896
 VMEM_LIMIT = 48 * 1024 * 1024
 
 
@@ -45,35 +46,12 @@
     return lax.ppermute(array, axis, [(i, i ^ bits) for i in range(count)])
 
 
-def chain_pairs(rule):
-    pairs = []
-    for t in range(4):
-        for e in range(4):
-            far, near = e // 2, e % 2
-            goal = rule(3 - t if far else t, far, near)
-            if goal is not None:
-                order, far, near = goal
-                pairs.append((t * 4 + e, (3 - order if far else order) * 4 + 2 * far + near))
-    return pairs
-
-
-CROSS = chain_pairs(lambda u, f, n: (3 - u, 1 - f, n) if u >= 2 else None)
-UP_FIRST = chain_pairs(lambda u, f, n: (u + 1, f, n) if u in (0, 1) else None)
-UP_SECOND = chain_pairs(lambda u, f, n: (u + 1, f, n) if u in (1, 2) else None)
-UP_THIRD = chain_pairs(lambda u, f, n: (u + 1, f, n) if u == 2 else None)
-DOWN = chain_pairs(lambda u, f, n: (0, f, n) if u == 1 else None)
-
-
-def move(array, pairs):
-    return lax.ppermute(array, ("tensor", "example"), pairs)
-
-
 def kernel_params():
     return pltpu.CompilerParams(vmem_limit_bytes=VMEM_LIMIT)
 
 
 def pack_kernel(starts, sizes, near_ref, place_ref, own_ref, other_ref, *refs):
-    outs, select = refs[:-1], refs[-1]
+    outs, select = refs[-1 - len(sizes) : -1], refs[-1]
     rows_own = own_ref.shape[0]
 
     @pl.when(pl.program_id(0) == 0)
@@ -93,7 +71,7 @@
         base += size
 
 
-def pack(starts, sizes, near_offset, place, own, other):
+def pack(starts, sizes, near_offset, place, own, other, after=()):
     rows, columns = other.shape
     total = sum(sizes)
     return pl.pallas_call(
@@ -105,7 +83,8 @@
                 pl.BlockSpec((1, 2 * rows), lambda i, near: (0, 0)),
                 pl.BlockSpec((rows, TILE), lambda i, near: (0, near[0] + i)),
                 pl.BlockSpec((rows, TILE), lambda i, near: (0, i)),
-            ],
+            ]
+            + [pl.BlockSpec(memory_space=pl.ANY)] * len(after),
             out_specs=[pl.BlockSpec((size, TILE), lambda i, near: (0, i)) for size in sizes],
             scratch_shapes=[pltpu.VMEM((total, 2 * rows), jnp.bfloat16)],
         ),
@@ -117,40 +96,98 @@
             transcendentals=0,
         ),
         name="pack_rows",
-    )(near_offset, place, own, other)
-
-
-def partial_kernel(near_ref, a0, a1, b0, b1, keep_ref, other_ref, out_ref, left):
+    )(near_offset, place, own, other, *after)
+
+
+def cut_kernel(far_ref, mine_in, away_in, *refs):
+    mine_out, away_out = refs[-2:]
+    mine_out[...] = mine_in[...]
+    away_out[...] = away_in[...]
+
+
+def cut(far, gathered, width, after):
+    rows = gathered.shape[0]
+    block = width // 2
+    return pl.pallas_call(
+        cut_kernel,
+        grid_spec=pltpu.PrefetchScalarGridSpec(
+            num_scalar_prefetch=1,
+            grid=(4,),
+            in_specs=[
+                pl.BlockSpec((rows, block), lambda i, far: (0, 4 * far[0] + i)),
+                pl.BlockSpec((rows, block), lambda i, far: (0, 4 * (1 - far[0]) + i)),
+            ]
+            + [pl.BlockSpec(memory_space=pl.ANY)] * len(after),
+            out_specs=[pl.BlockSpec((rows, block), lambda i, far: (0, i))] * 2,
+        ),
+        out_shape=[jax.ShapeDtypeStruct((rows, 2 * width), gathered.dtype)] * 2,
+        compiler_params=kernel_params(),
+        cost_estimate=pl.CostEstimate(flops=0, bytes_accessed=16 * rows * width, transcendentals=0),
+        name="cut_columns",
+    )(far, gathered, gathered, *after)
+
+
+def gate_kernel(value, *refs):
+    refs[-1][...] = value[...]
+
+
+def ordered(value, after):
+    return pl.pallas_call(
+        gate_kernel,
+        in_specs=[pl.BlockSpec(memory_space=pltpu.VMEM)]
+        + [pl.BlockSpec(memory_space=pl.ANY)] * len(after),
+        out_specs=pl.BlockSpec(memory_space=pltpu.VMEM),
+        out_shape=jax.ShapeDtypeStruct(value.shape, value.dtype),
+        compiler_params=kernel_params(),
+        name="ordered_copy",
+    )(value, *after)
+
+
+def partial_kernel(near_ref, a0, a1, b0, b1, keep_ref, other_ref, *refs):
+    out_ref, left, right = refs[-3:]
     size, width = a0.shape
 
     @pl.when(pl.program_id(0) == 0)
     def _():
-        left[:size, :width] = a0[...]
-        left[size:, :width] = a1[...]
-        left[:size, width:] = b0[...]
-        left[size:, width:] = b1[...]
-
-    total = contract(left[:, :width], keep_ref[...])
-    total += contract(left[:, width:], other_ref[...])
-    out_ref[...] = total.astype(out_ref.dtype)
-
-
-def partial_product(part, near_offset, own_k, own_k_near, near_k, near_k_near, weight, weight_near, dtype):
-    size, width = own_k.shape[0] // 2, own_k.shape[1]
+        left[...] = jnp.zeros_like(left)
+        left[:size, :] = a0[...]
+        left[size : 2 * size, :] = a1[...]
+        right[:width, :] = left[...].T
+        left[:size, :] = b0[...]
+        left[size : 2 * size, :] = b1[...]
+        right[width:, :] = left[...].T
+
+    total = jnp.dot(keep_ref[...], right[:width, :], preferred_element_type=jnp.float32)
+    total += jnp.dot(other_ref[...], right[width:, :], preferred_element_type=jnp.float32)
+    out_ref[...] = total.T[: 2 * size, :].astype(out_ref.dtype)
+
+
+def partial_product(near_offset, near, rows_here, rows_near, weight, weight_near, dtype, after):
+    size, width = rows_here.shape[0], rows_here.shape[1] // 2
     hidden = weight_near.shape[0]
-    rows = pl.BlockSpec((size, width), lambda i, near: (part, 0))
+    padded = -(-2 * size // 128) * 128
+    first = pl.BlockSpec((size, width), lambda i, offset, near: (0, near[0]))
+    second = pl.BlockSpec((size, width), lambda i, offset, near: (0, 1 - near[0]))
+
+    def body(offset_ref, near_ref, *refs):
+        partial_kernel(near_ref, *refs)
+
     return pl.pallas_call(
-        partial_kernel,
+        body,
         grid_spec=pltpu.PrefetchScalarGridSpec(
-            num_scalar_prefetch=1,
+            num_scalar_prefetch=2,
             grid=(hidden // TILE,),
-            in_specs=[rows] * 4
+            in_specs=[first, first, second, second]
             + [
-                pl.BlockSpec((TILE, width), lambda i, near: (near[0] + i, 0)),
-                pl.BlockSpec((TILE, width), lambda i, near: (i, 0)),
+                pl.BlockSpec((TILE, width), lambda i, offset, near: (offset[0] + i, 0)),
+                pl.BlockSpec((TILE, width), lambda i, offset, near: (i, 0)),
+            ]
+            + [pl.BlockSpec(memory_space=pl.ANY)] * len(after),
+            out_specs=pl.BlockSpec((2 * size, TILE), lambda i, offset, near: (0, i)),
+            scratch_shapes=[
+                pltpu.VMEM((padded, width), jnp.bfloat16),
+                pltpu.VMEM((2 * width, padded), jnp.bfloat16),
             ],
-            out_specs=pl.BlockSpec((2 * size, TILE), lambda i, near: (0, i)),
-            scratch_shapes=[pltpu.VMEM((2 * size, 2 * width), jnp.bfloat16)],
         ),
         out_shape=jax.ShapeDtypeStruct((2 * size, hidden), dtype),
         compiler_params=kernel_params(),
@@ -160,10 +197,12 @@
             transcendentals=0,
         ),
         name="partial_product",
-    )(near_offset, own_k, own_k_near, near_k, near_k_near, weight, weight_near)
-
-
-def finish_kernel(near_ref, own_ref, came_ref, gate_ref, up_ref, proj_gate_ref, proj_up_ref, gate_out, up_out):
+    )(near_offset, near, rows_here, rows_near, rows_here, rows_near, weight, weight_near, *after)
+
+
+def finish_kernel(near_ref, own_ref, came_ref, gate_ref, up_ref, proj_gate_ref, proj_up_ref, *refs):
+    gate_out, up_out = refs[-2:]
+
     @pl.when(pl.program_id(0) == 0)
     def _():
         gate_out[...] = jnp.zeros_like(gate_out)
@@ -180,18 +219,19 @@
     up_out[...] += contract(grad_up, proj_up_ref[...])
 
 
-def finish(near_offset, own, came, gate, up, proj_gate, proj_up):
+def finish(near_offset, own, came, gate, up, proj_gate, proj_up, after):
     rows, hidden = own.shape
     rank_size = proj_gate.shape[0]
-    tile = pl.BlockSpec((rows, TILE), lambda i, near: (0, i))
-    proj = pl.BlockSpec((rank_size, TILE), lambda i, near: (0, near[0] + i))
+    tile = pl.BlockSpec((rows, WIDE), lambda i, near: (0, i))
+    proj = pl.BlockSpec((rank_size, WIDE), lambda i, near: (0, near[0] + i))
     out = pl.BlockSpec((rows, rank_size), lambda i, near: (0, 0))
     return pl.pallas_call(
         finish_kernel,
         grid_spec=pltpu.PrefetchScalarGridSpec(
             num_scalar_prefetch=1,
-            grid=(hidden // TILE,),
-            in_specs=[tile, tile, tile, tile, proj, proj],
+            grid=(hidden // WIDE,),
+            in_specs=[tile, tile, tile, tile, proj, proj]
+            + [pl.BlockSpec(memory_space=pl.ANY)] * len(after),
             out_specs=[out, out],
         ),
         out_shape=[jax.ShapeDtypeStruct((rows, rank_size), jnp.float32)] * 2,
@@ -202,7 +242,7 @@
             transcendentals=rows * hidden,
         ),
         name="finish_chunk",
-    )(near_offset, own, came, gate, up, proj_gate, proj_up)
+    )(near_offset, own, came, gate, up, proj_gate, proj_up, *after)
 
 
 def sum_over(array, axis):
@@ -245,13 +285,13 @@
     example_at = lax.axis_index("example")
     tensor_at = lax.axis_index("tensor")
     near, far = example_at % 2, example_at // 2
-    order = jnp.where(far == 1, 3 - tensor_at, tensor_at)
     half_hidden = hidden_local // 2
     half_rows = capacity // 2
     units = half_rows // 16
     sizes = [16 * (units // CHUNKS + (k < units % CHUNKS)) for k in range(CHUNKS)]
     begins = [sum(sizes[:k]) for k in range(CHUNKS)]
     offset = (near * (half_hidden // TILE)).astype(jnp.int32).reshape(1)
+    wide_offset = (near * (half_hidden // WIDE)).astype(jnp.int32).reshape(1)
     no_offset = jnp.zeros((1,), jnp.int32)
 
     both_lengths = jnp.concatenate([own_lengths, near_lengths])
@@ -278,38 +318,53 @@
     starts = [2 * b for b in begins]
     doubles = [2 * s for s in sizes]
     blocks = pack(starts, sizes, no_offset, place, grad_rows, grad_near)
-
+    gathered = [lax.all_gather(block, "tensor", axis=1, tiled=True) for block in blocks]
     weight_near = swap(take(down_weight, (1 - near) * half_hidden, half_hidden, 0), "example", 1)
 
-    def split_hidden(array):
+    def send_hidden(array):
         rows = array.reshape(row_total, hidden_local)
-        other = swap(take(rows, (1 - near) * half_hidden, half_hidden, 1), "example", 1)
-        return pack(starts, doubles, offset, place, rows, other)
-
-    gate_packed = split_hidden(gate_pre)
-    up_packed = split_hidden(up_pre)
-
-    columns_match = near == far
-    lefts = []
+        return rows, swap(take(rows, (1 - near) * half_hidden, half_hidden, 1), "example", 1)
+
+    gate_both, up_both = send_hidden(gate_pre), send_hidden(up_pre)
+
+    near_at, far_at = near.astype(jnp.int32).reshape(1), far.astype(jnp.int32).reshape(1)
+    width = down_weight.shape[1]
+    came, own, right = [], [], []
+    packed = {}
+
+    def product(rows_here, rows_near, dtype, after):
+        return partial_product(offset, near_at, rows_here, rows_near, down_weight, weight_near, dtype, after)
+
+    def finish_step(k, after):
+        right.append(
+            jnp.concatenate(
+                finish(wide_offset, own[k], came[k], packed["gate"][k], packed["up"][k], proj_gate, proj_up, after),
+                axis=1,
+            )
+        )
+
+    last, waiting = (), []
     for k in range(CHUNKS):
-        source = jnp.concatenate([blocks[k], move(blocks[k], CROSS)])
-        first = move(source, UP_FIRST)
-        down = move(source, DOWN)
-        second = move(first, UP_SECOND)
-        third = move(second, UP_THIRD)
-        outer = lax.select_n(order, source, first, second, third)
-        inner = lax.select_n(order, down, source, first, second)
-        own_k = jnp.where(columns_match, outer, inner)
-        near_k = jnp.where(columns_match, inner, outer)
-        lefts.append((own_k, swap(near_k, "example", 1), near_k, swap(own_k, "example", 1)))
-    came = [
-        swap(partial_product(1, offset, *lefts[k], down_weight, weight_near, jnp.bfloat16), "example", 2)
-        for k in range(CHUNKS)
-    ]
-    own = [
-        partial_product(0, offset, *lefts[k], down_weight, weight_near, jnp.float32)
-        for k in range(CHUNKS)
-    ]
+        mine, away = cut(far_at, gathered[k], width, last)
+        far_rows = swap(away, "example", 2)
+        mine_near = swap(mine, "example", 1)
+        done = []
+        if k == 1:
+            packed["gate"] = pack(starts, doubles, offset, place, *gate_both, after=(away,))
+            packed["up"] = pack(starts, doubles, offset, place, *up_both, after=(away,))
+        if k > 0:
+            own.append(product(*waiting, jnp.float32, (away,)))
+            done.append(own[-1])
+        if k > 1:
+            finish_step(k - 2, (away,))
+            done.append(right[-1])
+        waiting = [mine, mine_near]
+        partial = product(far_rows, swap(far_rows, "example", 1), jnp.bfloat16, tuple(done))
+        came.append(swap(partial, "example", 2))
+        last = (partial,)
+    own.append(product(*waiting, jnp.float32, last))
+    finish_step(CHUNKS - 2, (own[-1],))
+    finish_step(CHUNKS - 1, (right[-1],))
 
     inputs_rows = layer_input.reshape(row_total, width_local)
     gate_values = gate_pre.reshape(row_total, hidden_local).astype(jnp.float32)
@@ -322,8 +377,7 @@
             contract(grad_rows, proj_output),
         ]
     )
-    early, _ = lax.optimization_barrier((early, lefts[-1][0]))
-    early = sum_over(early, "tensor")
+    early = sum_over(ordered(early, last), "tensor")
     in_gate, in_down, out_down = (early[k * row_total : (k + 1) * row_total] for k in range(3))
     slots_here = jnp.concatenate(
         [
@@ -350,10 +404,6 @@
     left = table_rows.astype(jnp.float32)[:, :, None] * in_gate[:, None, :]
     left = left.reshape(capacity, rev_pairs * rank_size)
 
-    right = [
-        jnp.concatenate(finish(offset, own[k], came[k], gate_packed[k], up_packed[k], proj_gate, proj_up), axis=1)
-        for k in range(CHUNKS)
-    ]
     sketch_late = lax.dot_general(
         left, jnp.concatenate(right), (((0,), (0,)), ((), ())), precision=lax.Precision.HIGHEST
     ).reshape(rev_pairs, rank_size, 2 * rank_size)

time: 544 us -> 467 us (0.86); the launches traced: 534 us -> 467 us
  starting transfers between devices: 104 us -> 39 us
  waiting for transfers between devices: 146 us -> 122 us
  loops' own time: 21.5 us -> 37.9 us
  between operations: 4.4 us -> 17.1 us
  Pallas kernels: 186 us -> 175 us
  local copies, waits for them, and re-layouts: 40.3 us -> 47.9 us
    ppermute x20 -> x0, waiting for transfers between devices: 113 us -> none  [move(): return lax.ppermute(array, ('tensor', 'example'), pairs)]
    ppermute x35 -> x39, waiting for transfers between devices: 32.8 us -> 77.8 us  [swap(): return lax.ppermute(array, axis, [(i, i ^ bits) for i in range(count)])]
    ppermute x20 -> x0, starting transfers between devices: 43.2 us -> none  [move(): return lax.ppermute(array, ('tensor', 'example'), pairs)]
    all_gather x0 -> x4, waiting for transfers between devices: none -> 42 us  [packed_scores(): lax.all_gather(block, 'tensor', axis=1, tiled=True)]
    ppermute x35 -> x39, starting transfers between devices: 57 us -> 35.4 us  [swap(): return lax.ppermute(array, axis, [(i, i ^ bits) for i in range(count)])]
    another operation x1, loops' own time: 21.5 us -> 37.9 us  [local_four(): lax.switch(branch, [functools.partial(packed_scores, level) for level in...]
    pallas_call x3, Pallas kernels: 35.8 us -> 26.4 us  [pack(): pl.pallas_call(functools.partial(pack_kernel, starts, sizes), grid_spec=p...]
    select_n x8 -> x0, other arithmetic: 6.48 us -> none  [the longest x4 6.15 us: packed_scores(): near_k = jnp.where(columns_match, inner, outer)]
  transfers between devices with their start and end apart: 56 -> 44, of which waited for: 19 -> 15; matrix products, arithmetic and copies ran while one was open for 7% -> 9% of each run, Pallas kernels for 34% -> 36%
where the time goes in v3:
time: 467 us
  Pallas kernels  175 us (37%)
  waiting for transfers between devices  122 us (26%)
  local copies, waits for them, and re-layouts  47.9 us (10%)
  starting transfers between devices  39 us (8%)
  loops' own time  37.9 us (8%)
  matrix products  20.5 us (4%)
  between operations  17.1 us (4%)
  other arithmetic  8.9 us (2%)
    pallas_call x8, Pallas kernels, partial_product(): pl.pallas_call(body, grid_spec=pltpu.PrefetchScalarGridSpec(num_scalar_pr...  124 us
    ppermute x39, waiting for transfers between devices, swap(): return lax.ppermute(array, axis, [(i, i ^ bits) for i in range(count)])  77.8 us
    all_gather x4, waiting for transfers between devices, packed_scores(): lax.all_gather(block, 'tensor', axis=1, tiled=True)  42 us
    another operation x1, loops' own time, local_four(): lax.switch(branch, [functools.partial(packed_scores, level) for level in...  37.9 us
    ppermute x39, starting transfers between devices, swap(): return lax.ppermute(array, axis, [(i, i ^ bits) for i in range(count)])  35.4 us
    pallas_call x3, Pallas kernels, pack(): pl.pallas_call(functools.partial(pack_kernel, starts, sizes), grid_spec=p...  26.4 us
    dynamic_slice x6, local copies, waits for them, and re-layouts, take(): return lax.dynamic_slice_in_dim(array, start, size, axis)  22.4 us
    cond x77, local copies, waits for them, and re-layouts  18.9 us
  transfers between devices with their start and end apart: 44, of which 15 were waited for; matrix products, arithmetic and copies ran while one was open for 9% of the time, Pallas kernels for 36%

profile of v3, /device:TPU:0, one launch (start us, length us, event | category | flops | bytes accessed | tf_op | source)
XLA Modules:
  0.0 467.4 jit_solution(16378455615715312851)
XLA Ops:
  7.0 2.9 collective-permute-start.211
  10.0 1.4 reduce_sum.153
  15.8 3.4 collective-permute-start.213
  20.2 1.4 fusion.392
  22.2 437.9 %conditional.1 = (f32[8,128]{1,0:T(8,128)S(1)}) conditional(s32[]{:T(128)} %clamp.3, (s32[4]{0:T(128)}, s32[4]{0:T(128)S(1)}, s32[16]{0:T(128)}, bf16[4,128,2048]{2,1,0:T(8,128)(2,1)}, bf16[64,2048]{1,0:T(8,128)(2,1)}, /*index=5*/bf16[4,128,7168]{2,1,0:T(8,128)(2,1)}, bf16[4,128,7168]{2,1,0:T(8,128)(2,1)}, ...), branch_computations={%region_5.10_spmd, %region_10.15_spmd, %region_15.20_spmd, %region... | conditional | flops 80743350272 | bytes 817149952 | solution.py:451
  48.6 13.6 %constant_dynamic-slice_fusion.44 = bf16[3584,2048]{1,0:T(8,128)(2,1)} fusion(bf16[7168,2048]{1,0:T(8,128)(2,1)} %get-tuple-element.396.refs_4_, s32[]{:T(128)S(6)} %select_n.1033), kind=kLoop, calls=%fused_computation.591 | loop fusion | bytes 29360132 | tf_op jit(solution)/shard_map/cond/branch_4_fun/dynamic_slice | solution.py:41
  65.4 5.4 %pack_rows.30 = (bf16[112,2048]{1,0:T(8,128)(2,1)}, bf16[112,2048]{1,0:T(8,128)(2,1)}, bf16[96,2048]{1,0:T(8,128)(2,1)}, bf16[96,2048]{1,0:T(8,128)(2,1)}) custom-call(s32[1]{0:T(128)} %constant.611.clone.near_ref, s32[1,1024]{1,0:T(1,128)S(1)} %bitcast_select_fusion.4.place_ref, bf16[512,2048]{1,0:T(8,128)(2,1)S(1)} %copy-done.253, ...), custom_call_target="tpu_custom_call" | custom-call | flops 1744830464 | bytes 5898240 | tf_op jit(solution)/shard_map/cond/branch_4_fun/pack_rows/pallas_call | solution.py:77
  72.5 41.9 %all-gather.63.cloned.1.call-done.mine_in.away_in = bf16[112,8192]{1,0:T(8,128)(2,1)} async-done(((bf16[112,2048]{1,0:T(8,128)(2,1)}), bf16[112,8192]{1,0:T(8,128)(2,1)}) %all-gather.63.cloned.1.call-update) | async-done | bytes 1835024 | tf_op jit(solution)/shard_map/cond/branch_4_fun/all_gather | solution.py:321
  114.4 1.5 copy-done.26
  116.4 1.5 collective-permute-start.140
  117.9 20.6 %collective-permute-done.140.refs_0_.refs_2_ = bf16[112,4096]{1,0:T(8,128)(2,1)S(1)} collective-permute-done((bf16[112,4096]{1,0:T(8,128)(2,1)S(1)}, bf16[112,4096]{1,0:T(8,128)(2,1)S(1)}, u32[]{:S(2)}, u32[]{:S(2)}) %collective-permute-start.140) | collective-permute-done | bytes 917536 | tf_op jit(solution)/shard_map/cond/branch_4_fun/ppermute | solution.py:46
  138.5 4.5 constant_dynamic-slice_fusion.43
  143.2 4.2 constant_dynamic-slice_fusion.42
  151.1 15.3 %partial_product.80.refs_0_ = bf16[224,3584]{1,0:T(8,128)(2,1)S(1)} custom-call(s32[1]{0:T(128)} %bitcast.101.offset_ref.near_ref, s32[1]{0:T(128)} %bitcast.102.near_ref, bf16[112,4096]{1,0:T(8,128)(2,1)S(1)} %copy-done.63, bf16[112,4096]{1,0:T(8,128)(2,1)S(1)} %copy-done.65, bf16[112,4096]{1,0:T(8,128)(2,1)S(1)} %copy-done.63, ...), custom_call_target="tpu_custom_call" | custom-call | flops 6576668672 | bytes 32571392 | tf_op jit(solution)/shard_map/cond/branch_4_fun/partial_product/pallas_call | solution.py:175
  166.5 1.5 copy-done.25
  168.0 1.8 cut_columns.41
  169.7 1.5 collective-permute-start.143
  171.2 8.5 %fusion.265 = f32[512,64]{1,0:T(8,128)} fusion(bf16[64,7168]{1,0:T(8,128)(2,1)S(1)} %copy-done.326, bf16[512,7168]{1,0:T(8,128)(2,1)} %bitcast.419, bf16[512,7168]{1,0:T(8,128)(2,1)} %bitcast.401), kind=kOutput, calls=%fused_computation.506 | convolution fusion | flops 499122176 | bytes 15728640 | tf_op jit(solution)/shard_map/cond/branch_4_fun/dot_general | solution.py:18
  179.9 12.6 %collective-permute-done.143.refs_0_.refs_2_ = bf16[112,4096]{1,0:T(8,128)(2,1)} collective-permute-done((bf16[112,4096]{1,0:T(8,128)(2,1)}, bf16[112,4096]{1,0:T(8,128)(2,1)}, u32[]{:S(2)}, u32[]{:S(2)}) %collective-permute-start.143) | collective-permute-done | bytes 917536 | tf_op jit(solution)/shard_map/cond/branch_4_fun/ppermute | solution.py:46
  192.6 3.0 fusion.422
  195.6 1.4 collective-permute-start.149
  197.0 15.5 %partial_product.81.refs_6_.own_ref = f32[224,3584]{1,0:T(8,128)S(1)} custom-call(s32[1]{0:T(128)} %bitcast.101.offset_ref.near_ref, s32[1]{0:T(128)} %bitcast.102.near_ref, bf16[112,4096]{1,0:T(8,128)(2,1)S(1)} %get-tuple-element.398.refs_0_.refs_2_, bf16[112,4096]{1,0:T(8,128)(2,1)} %collective-permute-done.145.refs_1_.refs_3_, ...), custom_call_target="tpu_custom_call" | custom-call | flops 6576668672 | bytes 32571392 | tf_op jit(solution)/shard_map/cond/branch_4_fun/partial_product/pallas_call | solution.py:175
  212.5 1.7 copy-done.1
  214.2 15.6 %partial_product.82.refs_0_ = bf16[224,3584]{1,0:T(8,128)(2,1)S(1)} custom-call(s32[1]{0:T(128)} %bitcast.101.offset_ref.near_ref, s32[1]{0:T(128)} %bitcast.102.near_ref, bf16[112,4096]{1,0:T(8,128)(2,1)} %collective-permute-done.143.refs_0_.refs_2_, bf16[112,4096]{1,0:T(8,128)(2,1)} %collective-permute-done.144.refs_1_.refs_3_, ...), custom_call_target="tpu_custom_call" | custom-call | flops 6576668672 | bytes 32571392 | tf_op jit(solution)/shard_map/cond/branch_4_fun/partial_product/pallas_call | solution.py:175
  229.8 1.4 copy-done.31
  231.2 1.7 cut_columns.42
  233.8 10.4 %pack_rows.31 = (bf16[224,3584]{1,0:T(8,128)(2,1)S(1)}, bf16[224,3584]{1,0:T(8,128)(2,1)}, bf16[192,3584]{1,0:T(8,128)(2,1)S(1)}, bf16[192,3584]{1,0:T(8,128)(2,1)S(1)}) custom-call(s32[1]{0:T(128)} %bitcast.101.offset_ref.near_ref, s32[1,1024]{1,0:T(1,128)S(1)} %bitcast_select_fusion.4.place_ref, bf16[512,7168]{1,0:T(8,128)(2,1)} %bitcast.402, ...), custom_call_target="tpu_custom_call" | custom-call | flops 6106906624 | bytes 13303808 | tf_op jit(solution)/shard_map/cond/branch_4_fun/pack_rows/pallas_call | solution.py:77
  245.2 7.3 %collective-permute-done.146.refs_0_.refs_2_ = bf16[96,4096]{1,0:T(8,128)(2,1)S(1)} collective-permute-done((bf16[96,4096]{1,0:T(8,128)(2,1)S(1)}, bf16[96,4096]{1,0:T(8,128)(2,1)S(1)}, u32[]{:S(2)}, u32[]{:S(2)}) %collective-permute-start.146) | collective-permute-done | bytes 786464 | tf_op jit(solution)/shard_map/cond/branch_4_fun/ppermute | solution.py:46
  252.6 10.6 %pack_rows.32 = (bf16[224,3584]{1,0:T(8,128)(2,1)S(1)}, bf16[224,3584]{1,0:T(8,128)(2,1)}, bf16[192,3584]{1,0:T(8,128)(2,1)S(1)}, bf16[192,3584]{1,0:T(8,128)(2,1)S(1)}) custom-call(s32[1]{0:T(128)} %bitcast.101.offset_ref.near_ref, s32[1,1024]{1,0:T(1,128)S(1)} %bitcast_select_fusion.4.place_ref, bf16[512,7168]{1,0:T(8,128)(2,1)} %bitcast.420, ...), custom_call_target="tpu_custom_call" | custom-call | flops 6106906624 | bytes 13303808 | tf_op jit(solution)/shard_map/cond/branch_4_fun/pack_rows/pallas_call | solution.py:77
  265.0 4.7 %finish_chunk.40 = (f32[224,64]{1,0:T(8,128)S(1)}, f32[224,64]{1,0:T(8,128)S(1)}) custom-call(s32[1]{0:T(128)} %bitcast.105.near_ref, f32[224,3584]{1,0:T(8,128)} %copy-done.1, bf16[224,3584]{1,0:T(8,128)(2,1)} %collective-permute-done.149.came_ref, bf16[224,3584]{1,0:T(8,128)(2,1)S(1)} %get-tuple-element.401.gate_ref, ...), custom_call_target="tpu_custom_call" | custom-call | flops 205520896 | bytes 8028160 | tf_op jit(solution)/shard_map/cond/branch_4_fun/finish_chunk/pallas_call | solution.py:228
  269.9 15.2 %partial_product.83.refs_6_.own_ref = f32[224,3584]{1,0:T(8,128)S(1)} custom-call(s32[1]{0:T(128)} %bitcast.101.offset_ref.near_ref, s32[1]{0:T(128)} %bitcast.102.near_ref, bf16[112,4096]{1,0:T(8,128)(2,1)S(1)} %copy-done.61, bf16[112,4096]{1,0:T(8,128)(2,1)S(1)} %collective-permute-done.148.refs_1_.refs_3_, bf16[112,4096]{1,0:T(8,128)(2,1)S(1)} %copy-done.61, ...), custom_call_target="tpu_custom_call" | custom-call | flops 6576668672 | bytes 32571392 | tf_op jit(solution)/shard_map/cond/branch_4_fun/partial_product/pallas_call | solution.py:175
  285.1 1.7 copy-done
  286.8 15.1 %partial_product.84.refs_0_ = bf16[192,3584]{1,0:T(8,128)(2,1)S(1)} custom-call(s32[1]{0:T(128)} %bitcast.101.offset_ref.near_ref, s32[1]{0:T(128)} %bitcast.102.near_ref, bf16[96,4096]{1,0:T(8,128)(2,1)S(1)} %collective-permute-done.146.refs_0_.refs_2_, bf16[96,4096]{1,0:T(8,128)(2,1)S(1)} %collective-permute-done.147.refs_1_.refs_3_, ...), custom_call_target="tpu_custom_call" | custom-call | flops 5637144576 | bytes 32112640 | tf_op jit(solution)/shard_map/cond/branch_4_fun/partial_product/pallas_call | solution.py:175
  302.0 1.4 copy-done.33
  303.4 1.9 cut_columns.43
  305.3 1.3 collective-permute-start.152
  307.4 2.3 fusion.421
  309.8 15.5 %collective-permute-done.152.refs_0_.refs_2_ = bf16[96,4096]{1,0:T(8,128)(2,1)} collective-permute-done((bf16[96,4096]{1,0:T(8,128)(2,1)}, bf16[96,4096]{1,0:T(8,128)(2,1)}, u32[]{:S(2)}, u32[]{:S(2)}) %collective-permute-start.152) | collective-permute-done | bytes 786464 | tf_op jit(solution)/shard_map/cond/branch_4_fun/ppermute | solution.py:46
  326.9 15.6 %partial_product.85.refs_6_.own_ref = f32[192,3584]{1,0:T(8,128)S(1)} custom-call(s32[1]{0:T(128)} %bitcast.101.offset_ref.near_ref, s32[1]{0:T(128)} %bitcast.102.near_ref, bf16[96,4096]{1,0:T(8,128)(2,1)} %get-tuple-element.408.refs_0_.refs_2_, bf16[96,4096]{1,0:T(8,128)(2,1)} %collective-permute-done.154.refs_1_.refs_3_, ...), custom_call_target="tpu_custom_call" | custom-call | flops 5637144576 | bytes 32112640 | tf_op jit(solution)/shard_map/cond/branch_4_fun/partial_product/pallas_call | solution.py:175
  342.5 2.4 copy-done.102
  344.9 4.8 %finish_chunk.41 = (f32[224,64]{1,0:T(8,128)S(1)}, f32[224,64]{1,0:T(8,128)S(1)}) custom-call(s32[1]{0:T(128)} %bitcast.105.near_ref, f32[224,3584]{1,0:T(8,128)} %copy-done, bf16[224,3584]{1,0:T(8,128)(2,1)} %collective-permute-done.155.came_ref, bf16[224,3584]{1,0:T(8,128)(2,1)S(1)} %copy-done.101, bf16[224,3584]{1,0:T(8,128)(2,1)S(1)} %copy-done.102, ...), custom_call_target="tpu_custom_call" | custom-call | flops 205520896 | bytes 8028160 | tf_op jit(solution)/shard_map/cond/branch_4_fun/finish_chunk/pallas_call | solution.py:228
  349.8 16.1 %partial_product.86.refs_0_.refs_6_ = bf16[192,3584]{1,0:T(8,128)(2,1)} custom-call(s32[1]{0:T(128)} %bitcast.101.offset_ref.near_ref, s32[1]{0:T(128)} %bitcast.102.near_ref, bf16[96,4096]{1,0:T(8,128)(2,1)} %collective-permute-done.152.refs_0_.refs_2_, bf16[96,4096]{1,0:T(8,128)(2,1)S(1)} %collective-permute-done.153.refs_1_.refs_3_, ...), custom_call_target="tpu_custom_call" | custom-call | flops 5637144576 | bytes 32112640 | tf_op jit(solution)/shard_map/cond/branch_4_fun/partial_product/pallas_call | solution.py:175
  367.9 1.9 collective-permute-start.157
  369.9 2.3 collective-permute-start.158
  372.2 15.9 %partial_product.87.refs_0_.own_ref = f32[192,3584]{1,0:T(8,128)S(1)} custom-call(s32[1]{0:T(128)} %bitcast.101.offset_ref.near_ref, s32[1]{0:T(128)} %bitcast.102.near_ref, bf16[96,4096]{1,0:T(8,128)(2,1)} %get-tuple-element.415.refs_0_.refs_2_, bf16[96,4096]{1,0:T(8,128)(2,1)} %collective-permute-done.161.refs_1_.refs_3_, ...), custom_call_target="tpu_custom_call" | custom-call | flops 5637144576 | bytes 32112640 | tf_op jit(solution)/shard_map/cond/branch_4_fun/partial_product/pallas_call | solution.py:175
  388.0 1.6 copy-done.3
  389.7 4.3 finish_chunk.42
  395.3 2.7 collective-permute-done.157
  399.3 2.2 copy.105
  401.4 1.4 add_add_fusion.16
  404.5 1.7 fusion.267
  406.2 4.3 finish_chunk.43
  410.5 1.7 fusion.269
  412.3 6.8 %collective-permute-start.163 = (f32[8,16,128]{2,1,0:T(8,128)S(1)}, f32[8,16,128]{2,1,0:T(8,128)S(1)}, u32[]{:S(2)}, u32[]{:S(2)}) collective-permute-start(f32[8,16,128]{2,1,0:T(8,128)S(1)} %get-tuple-element.548), channel_id=1, source_target_pairs={{0,4},{4,0},{8,12},{12,8},{1,5},{5,1},{9,13},{13,9},{2,6},{6,2},{1... | collective-permute-start | bytes 196616 | tf_op jit(solution)/shard_map/cond/branch_4_fun/ppermute | solution.py:46
  420.1 1.4 collective-permute-start.165
  421.8 5.5 %collective-permute-done.164 = f32[8,16,128]{2,1,0:T(8,128)S(1)} collective-permute-done((f32[8,16,128]{2,1,0:T(8,128)S(1)}, f32[8,16,128]{2,1,0:T(8,128)S(1)}, u32[]{:S(2)}, u32[]{:S(2)}) %collective-permute-start.164) | collective-permute-done | bytes 65568 | tf_op jit(solution)/shard_map/cond/branch_4_fun/ppermute | solution.py:46
  427.4 1.4 collective-permute-start.167
  429.3 4.5 collective-permute-done.167
  433.8 1.9 collective-permute-done.168
  439.6 2.0 collective-permute-done.170
  443.6 1.4 collective-permute-start.173
  445.0 1.7 collective-permute-start.174
  446.7 1.4 collective-permute-done.173
  448.2 2.3 collective-permute-done.174
  (184 shorter events, 32.4 us)
Async XLA Ops:
  6.5 15.7 %collective-permute-start.214 = (bf16[512,2048]{1,0:T(8,128)(2,1)}, bf16[512,2048]{1,0:T(8,128)(2,1)}, u32[]{:S(2)}, u32[]{:S(2)}) collective-permute-start(bf16[512,2048]{1,0:T(8,128)(2,1)} %bitcast.381), channel_id=1, source_target_pairs={{0,1},{1,0},{2,3},{3,2},{4,5},{5,4},{6,7},{7,6},{8,9},{9,8},{10,11... | collective-permute-start | bytes 6291464 | tf_op jit(solution)/shard_map/ppermute | solution.py:46
  7.0 4.4 collective-permute-start.210
  7.0 6.2 %collective-permute-start.211 = (s32[4]{0:T(128)}, s32[4]{0:T(128)S(1)}, u32[]{:S(2)}, u32[]{:S(2)}) collective-permute-start(s32[4]{0:T(128)} %param.32), channel_id=1, source_target_pairs={{0,2},{1,3},{2,0},{3,1},{4,6},{5,7},{6,4},{7,5},{8,10},{9,11},{10,... | collective-permute-start | bytes 56 | tf_op jit(solution)/shard_map/ppermute | solution.py:46
  10.0 3.9 collective-permute-start.212
  15.8 3.8 collective-permute-start.213
  48.5 65.9 %all-gather.63.cloned.1.call-start = ((), (), s32[]{:S(2)}) async-start(), calls=%async_computation.19 | async-start | bytes 2293760 | tf_op jit(solution)/shard_map/cond/branch_4_fun/all_gather | solution.py:321
  48.6 14.9 %copy-start.287 = (s32[4]{0:T(128)S(1)}, s32[4]{0:T(128)}, u32[]{:S(2)}) copy-start(s32[4]{0:T(128)} %get-tuple-element.380) | copy-start | bytes 52 | tf_op jit(solution)/shard_map/cond
  48.6 16.5 %copy-start.293 = (s32[16]{0:T(128)S(1)}, s32[16]{0:T(128)}, u32[]{:S(2)}) copy-start(s32[16]{0:T(128)} %get-tuple-element.382) | copy-start | bytes 196 | tf_op jit(solution)/shard_map/cond
  48.6 16.8 %copy-start.253 = (bf16[512,2048]{1,0:T(8,128)(2,1)S(1)}, bf16[512,2048]{1,0:T(8,128)(2,1)}, u32[]{:S(2)}) copy-start(bf16[512,2048]{1,0:T(8,128)(2,1)} %get-tuple-element.388.own_ref) | copy-start | bytes 6291460 | tf_op jit(solution)/shard_map/cond
  62.2 86.6 %collective-permute-start.142 = (bf16[3584,2048]{1,0:T(8,128)(2,1)}, bf16[3584,2048]{1,0:T(8,128)(2,1)}, u32[]{:S(2)}, u32[]{:S(2)}) collective-permute-start(bf16[3584,2048]{1,0:T(8,128)(2,1)} %constant_dynamic-slice_fusion.44), channel_id=1, source_target_pairs={{0,1},{1,0},{2,3},{3,2},{4,5},{5,4},{6,7},{7,6},{8,9},{9,8},{10,11... | collective-permute-start | bytes 44040200 | tf_op jit(solution)/shard_map/cond/branch_4_fun/ppermute | solution.py:46
  70.9 95.5 %all-gather.61.cloned.1.call-start = ((), (), s32[]{:S(2)}) async-start(), calls=%async_computation.18 | async-start | bytes 2293760 | tf_op jit(solution)/shard_map/cond/branch_4_fun/all_gather | solution.py:321
  71.7 158.2 %all-gather.59.cloned.1.call-start = ((), (), s32[]{:S(2)}) async-start(), calls=%async_computation.17 | async-start | bytes 1966080 | tf_op jit(solution)/shard_map/cond/branch_4_fun/all_gather | solution.py:321
  72.4 229.5 %all-gather.57.cloned.1.call-start = ((), (), s32[]{:S(2)}) async-start(), calls=%async_computation.16 | async-start | bytes 1966080 | tf_op jit(solution)/shard_map/cond/branch_4_fun/all_gather | solution.py:321
  116.4 22.1 %collective-permute-start.140 = (bf16[112,4096]{1,0:T(8,128)(2,1)S(1)}, bf16[112,4096]{1,0:T(8,128)(2,1)S(1)}, u32[]{:S(2)}, u32[]{:S(2)}) collective-permute-start(bf16[112,4096]{1,0:T(8,128)(2,1)S(1)} %get-tuple-element.395), channel_id=1, source_target_pairs={{0,2},{1,3},{2,0},{3,1},{4,6},{5,7},{6,4},{7,5},{8,10},{9,11},{10,... | collective-permute-start | bytes 2752520 | tf_op jit(solution)/shard_map/cond/branch_4_fun/ppermute | solution.py:46
  138.5 4.5 copy-start.62
  138.5 9.3 %collective-permute-start.141 = (bf16[112,4096]{1,0:T(8,128)(2,1)S(1)}, bf16[112,4096]{1,0:T(8,128)(2,1)S(1)}, u32[]{:S(2)}, u32[]{:S(2)}) collective-permute-start(bf16[112,4096]{1,0:T(8,128)(2,1)S(1)} %collective-permute-done.140.refs_0_.refs_2_), channel_id=1, source_target_pairs={{0,1},{1,0},{2,3},{3,2},{4,5},{5,4},{6,7},{7,6},{8,9},{9,8},{10,11... | collective-permute-start | bytes 2752520 | tf_op jit(solution)/shard_map/cond/branch_4_fun/ppermute | solution.py:46
  143.1 90.7 %collective-permute-start.150 = (bf16[512,3584]{1,0:T(8,128)(2,1)}, bf16[512,3584]{1,0:T(8,128)(2,1)}, u32[]{:S(2)}, u32[]{:S(2)}) collective-permute-start(bf16[512,3584]{1,0:T(8,128)(2,1)} %constant_dynamic-slice_fusion.43), channel_id=1, source_target_pairs={{0,1},{1,0},{2,3},{3,2},{4,5},{5,4},{6,7},{7,6},{8,9},{9,8},{10,11... | collective-permute-start | bytes 11010056 | tf_op jit(solution)/shard_map/cond/branch_4_fun/ppermute | solution.py:46
  147.4 105.2 %collective-permute-start.151 = (bf16[512,3584]{1,0:T(8,128)(2,1)}, bf16[512,3584]{1,0:T(8,128)(2,1)}, u32[]{:S(2)}, u32[]{:S(2)}) collective-permute-start(bf16[512,3584]{1,0:T(8,128)(2,1)} %constant_dynamic-slice_fusion.42), channel_id=1, source_target_pairs={{0,1},{1,0},{2,3},{3,2},{4,5},{5,4},{6,7},{7,6},{8,9},{9,8},{10,11... | collective-permute-start | bytes 11010056 | tf_op jit(solution)/shard_map/cond/branch_4_fun/ppermute | solution.py:46
  169.7 10.0 %copy-start.60 = (bf16[112,4096]{1,0:T(8,128)(2,1)}, bf16[112,4096]{1,0:T(8,128)(2,1)S(1)}, u32[]{:S(2)}) copy-start(bf16[112,4096]{1,0:T(8,128)(2,1)S(1)} %get-tuple-element.400.refs_0_.refs_2_) | copy-start | bytes 2752516 | tf_op jit(solution)/shard_map/cond
  169.7 22.7 %collective-permute-start.143 = (bf16[112,4096]{1,0:T(8,128)(2,1)}, bf16[112,4096]{1,0:T(8,128)(2,1)}, u32[]{:S(2)}, u32[]{:S(2)}) collective-permute-start(bf16[112,4096]{1,0:T(8,128)(2,1)} %get-tuple-element.397.refs_6_.refs_0_), channel_id=1, source_target_pairs={{0,2},{1,3},{2,0},{3,1},{4,6},{5,7},{6,4},{7,5},{8,10},{9,11},{10,... | collective-permute-start | bytes 2752520 | tf_op jit(solution)/shard_map/cond/branch_4_fun/ppermute | solution.py:46
  171.2 21.3 %copy-start.269 = (bf16[64,2048]{1,0:T(8,128)(2,1)S(1)}, bf16[64,2048]{1,0:T(8,128)(2,1)}, u32[]{:S(2)}) copy-start(bf16[64,2048]{1,0:T(8,128)(2,1)} %get-tuple-element.389) | copy-start | bytes 786436 | tf_op jit(solution)/shard_map/cond
  179.7 17.3 %collective-permute-start.145 = (bf16[112,4096]{1,0:T(8,128)(2,1)S(1)}, bf16[112,4096]{1,0:T(8,128)(2,1)}, u32[]{:S(2)}, u32[]{:S(2)}) collective-permute-start(bf16[112,4096]{1,0:T(8,128)(2,1)S(1)} %get-tuple-element.398.refs_0_.refs_2_), channel_id=1, source_target_pairs={{0,1},{1,0},{2,3},{3,2},{4,5},{5,4},{6,7},{7,6},{8,9},{9,8},{10,11... | collective-permute-start | bytes 2752520 | tf_op jit(solution)/shard_map/cond/branch_4_fun/ppermute | solution.py:46
  192.5 21.7 %collective-permute-start.144 = (bf16[112,4096]{1,0:T(8,128)(2,1)}, bf16[112,4096]{1,0:T(8,128)(2,1)}, u32[]{:S(2)}, u32[]{:S(2)}) collective-permute-start(bf16[112,4096]{1,0:T(8,128)(2,1)} %collective-permute-done.143.refs_0_.refs_2_), channel_id=1, source_target_pairs={{0,1},{1,0},{2,3},{3,2},{4,5},{5,4},{6,7},{7,6},{8,9},{9,8},{10,11... | collective-permute-start | bytes 2752520 | tf_op jit(solution)/shard_map/cond/branch_4_fun/ppermute | solution.py:46
  195.6 69.5 %collective-permute-start.149 = (bf16[224,3584]{1,0:T(8,128)(2,1)S(1)}, bf16[224,3584]{1,0:T(8,128)(2,1)}, u32[]{:S(2)}, u32[]{:S(2)}) collective-permute-start(bf16[224,3584]{1,0:T(8,128)(2,1)S(1)} %partial_product.80.refs_0_), channel_id=1, source_target_pairs={{0,2},{1,3},{2,0},{3,1},{4,6},{5,7},{6,4},{7,5},{8,10},{9,11},{10,... | collective-permute-start | bytes 4816904 | tf_op jit(solution)/shard_map/cond/branch_4_fun/ppermute | solution.py:46
  232.9 19.7 %collective-permute-start.146 = (bf16[96,4096]{1,0:T(8,128)(2,1)S(1)}, bf16[96,4096]{1,0:T(8,128)(2,1)S(1)}, u32[]{:S(2)}, u32[]{:S(2)}) collective-permute-start(bf16[96,4096]{1,0:T(8,128)(2,1)S(1)} %get-tuple-element.399.refs_6_.refs_0_), channel_id=1, source_target_pairs={{0,2},{1,3},{2,0},{3,1},{4,6},{5,7},{6,4},{7,5},{8,10},{9,11},{10,... | collective-permute-start | bytes 2359304 | tf_op jit(solution)/shard_map/cond/branch_4_fun/ppermute | solution.py:46
  233.7 36.2 %collective-permute-start.148 = (bf16[112,4096]{1,0:T(8,128)(2,1)S(1)}, bf16[112,4096]{1,0:T(8,128)(2,1)S(1)}, u32[]{:S(2)}, u32[]{:S(2)}) collective-permute-start(bf16[112,4096]{1,0:T(8,128)(2,1)S(1)} %copy-done.61), channel_id=1, source_target_pairs={{0,1},{1,0},{2,3},{3,2},{4,5},{5,4},{6,7},{7,6},{8,9},{9,8},{10,11... | collective-permute-start | bytes 2752520 | tf_op jit(solution)/shard_map/cond/branch_4_fun/ppermute | solution.py:46
  245.2 18.0 %copy-start.123 = (bf16[192,3584]{1,0:T(8,128)(2,1)}, bf16[192,3584]{1,0:T(8,128)(2,1)S(1)}, u32[]{:S(2)}) copy-start(bf16[192,3584]{1,0:T(8,128)(2,1)S(1)} %get-tuple-element.413.gate_ref) | copy-start | bytes 4128772 | tf_op jit(solution)/shard_map/cond
  252.6 34.2 %collective-permute-start.147 = (bf16[96,4096]{1,0:T(8,128)(2,1)S(1)}, bf16[96,4096]{1,0:T(8,128)(2,1)S(1)}, u32[]{:S(2)}, u32[]{:S(2)}) collective-permute-start(bf16[96,4096]{1,0:T(8,128)(2,1)S(1)} %collective-permute-done.146.refs_0_.refs_2_), channel_id=1, source_target_pairs={{0,1},{1,0},{2,3},{3,2},{4,5},{5,4},{6,7},{7,6},{8,9},{9,8},{10,11... | collective-permute-start | bytes 2359304 | tf_op jit(solution)/shard_map/cond/branch_4_fun/ppermute | solution.py:46
  264.3 5.5 %copy-start.127 = (bf16[192,3584]{1,0:T(8,128)(2,1)}, bf16[192,3584]{1,0:T(8,128)(2,1)S(1)}, u32[]{:S(2)}) copy-start(bf16[192,3584]{1,0:T(8,128)(2,1)S(1)} %get-tuple-element.414.up_ref) | copy-start | bytes 4128772 | tf_op jit(solution)/shard_map/cond
  264.3 78.2 %collective-permute-start.155 = (bf16[224,3584]{1,0:T(8,128)(2,1)S(1)}, bf16[224,3584]{1,0:T(8,128)(2,1)}, u32[]{:S(2)}, u32[]{:S(2)}) collective-permute-start(bf16[224,3584]{1,0:T(8,128)(2,1)S(1)} %partial_product.82.refs_0_), channel_id=1, source_target_pairs={{0,2},{1,3},{2,0},{3,1},{4,6},{5,7},{6,4},{7,5},{8,10},{9,11},{10,... | collective-permute-start | bytes 4816904 | tf_op jit(solution)/shard_map/cond/branch_4_fun/ppermute | solution.py:46
  303.4 4.0 copy-start.264
  305.3 20.0 %collective-permute-start.152 = (bf16[96,4096]{1,0:T(8,128)(2,1)}, bf16[96,4096]{1,0:T(8,128)(2,1)}, u32[]{:S(2)}, u32[]{:S(2)}) collective-permute-start(bf16[96,4096]{1,0:T(8,128)(2,1)} %get-tuple-element.407.refs_6_.refs_0_), channel_id=1, source_target_pairs={{0,2},{1,3},{2,0},{3,1},{4,6},{5,7},{6,4},{7,5},{8,10},{9,11},{10,... | collective-permute-start | bytes 2359304 | tf_op jit(solution)/shard_map/cond/branch_4_fun/ppermute | solution.py:46
  307.3 19.6 %collective-permute-start.154 = (bf16[96,4096]{1,0:T(8,128)(2,1)}, bf16[96,4096]{1,0:T(8,128)(2,1)}, u32[]{:S(2)}, u32[]{:S(2)}) collective-permute-start(bf16[96,4096]{1,0:T(8,128)(2,1)} %get-tuple-element.408.refs_0_.refs_2_), channel_id=1, source_target_pairs={{0,1},{1,0},{2,3},{3,2},{4,5},{5,4},{6,7},{7,6},{8,9},{9,8},{10,11... | collective-permute-start | bytes 2359304 | tf_op jit(solution)/shard_map/cond/branch_4_fun/ppermute | solution.py:46
  325.3 24.5 %collective-permute-start.153 = (bf16[96,4096]{1,0:T(8,128)(2,1)}, bf16[96,4096]{1,0:T(8,128)(2,1)S(1)}, u32[]{:S(2)}, u32[]{:S(2)}) collective-permute-start(bf16[96,4096]{1,0:T(8,128)(2,1)} %collective-permute-done.152.refs_0_.refs_2_), channel_id=1, source_target_pairs={{0,1},{1,0},{2,3},{3,2},{4,5},{5,4},{6,7},{7,6},{8,9},{9,8},{10,11... | collective-permute-start | bytes 2359304 | tf_op jit(solution)/shard_map/cond/branch_4_fun/ppermute | solution.py:46
  325.4 64.3 %collective-permute-start.160 = (bf16[192,3584]{1,0:T(8,128)(2,1)S(1)}, bf16[192,3584]{1,0:T(8,128)(2,1)}, u32[]{:S(2)}, u32[]{:S(2)}) collective-permute-start(bf16[192,3584]{1,0:T(8,128)(2,1)S(1)} %partial_product.84.refs_0_), channel_id=1, source_target_pairs={{0,2},{1,3},{2,0},{3,1},{4,6},{5,7},{6,4},{7,5},{8,10},{9,11},{10,... | collective-permute-start | bytes 4128776 | tf_op jit(solution)/shard_map/cond/branch_4_fun/ppermute | solution.py:46
  326.7 15.8 %copy-start.101 = (bf16[224,3584]{1,0:T(8,128)(2,1)S(1)}, bf16[224,3584]{1,0:T(8,128)(2,1)}, u32[]{:S(2)}) copy-start(bf16[224,3584]{1,0:T(8,128)(2,1)} %get-tuple-element.409.gate_ref) | copy-start | bytes 4816900 | tf_op jit(solution)/shard_map/cond
  326.7 43.2 %collective-permute-start.161 = (bf16[96,4096]{1,0:T(8,128)(2,1)}, bf16[96,4096]{1,0:T(8,128)(2,1)}, u32[]{:S(2)}, u32[]{:S(2)}) collective-permute-start(bf16[96,4096]{1,0:T(8,128)(2,1)} %get-tuple-element.415.refs_0_.refs_2_), channel_id=1, source_target_pairs={{0,1},{1,0},{2,3},{3,2},{4,5},{5,4},{6,7},{7,6},{8,9},{9,8},{10,11... | collective-permute-start | bytes 2359304 | tf_op jit(solution)/shard_map/cond/branch_4_fun/ppermute | solution.py:46
  342.5 7.3 %copy-start.13 = (f32[192,3584]{1,0:T(8,128)}, f32[192,3584]{1,0:T(8,128)S(1)}, u32[]{:S(2)}) copy-start(f32[192,3584]{1,0:T(8,128)S(1)} %partial_product.85.refs_6_.own_ref) | copy-start | bytes 8257540 | tf_op jit(solution)/shard_map/cond
  365.9 40.3 %collective-permute-start.162 = (bf16[192,3584]{1,0:T(8,128)(2,1)}, bf16[192,3584]{1,0:T(8,128)(2,1)}, u32[]{:S(2)}, u32[]{:S(2)}) collective-permute-start(bf16[192,3584]{1,0:T(8,128)(2,1)} %partial_product.86.refs_0_.refs_6_), channel_id=1, source_target_pairs={{0,2},{1,3},{2,0},{3,1},{4,6},{5,7},{6,4},{7,5},{8,10},{9,11},{10,... | collective-permute-start | bytes 4128776 | tf_op jit(solution)/shard_map/cond/branch_4_fun/ppermute | solution.py:46
  367.7 22.0 %copy-start.124 = (bf16[192,3584]{1,0:T(8,128)(2,1)S(1)}, bf16[192,3584]{1,0:T(8,128)(2,1)}, u32[]{:S(2)}) copy-start(bf16[192,3584]{1,0:T(8,128)(2,1)} %copy-done.123) | copy-start | bytes 4128772 | tf_op jit(solution)/shard_map/cond
  367.7 22.0 %copy-start.128 = (bf16[192,3584]{1,0:T(8,128)(2,1)S(1)}, bf16[192,3584]{1,0:T(8,128)(2,1)}, u32[]{:S(2)}) copy-start(bf16[192,3584]{1,0:T(8,128)(2,1)} %copy-done.127) | copy-start | bytes 4128772 | tf_op jit(solution)/shard_map/cond
  367.7 22.0 %copy-start.219 = (bf16[64,7168]{1,0:T(8,128)(2,1)S(1)}, bf16[64,7168]{1,0:T(8,128)(2,1)}, u32[]{:S(2)}) copy-start(bf16[64,7168]{1,0:T(8,128)(2,1)} %get-tuple-element.403.proj_gate_ref) | copy-start | bytes 2752516 | tf_op jit(solution)/shard_map/cond
  367.7 22.0 %copy-start.239 = (bf16[64,7168]{1,0:T(8,128)(2,1)S(1)}, bf16[64,7168]{1,0:T(8,128)(2,1)}, u32[]{:S(2)}) copy-start(bf16[64,7168]{1,0:T(8,128)(2,1)} %get-tuple-element.404.proj_up_ref) | copy-start | bytes 2752516 | tf_op jit(solution)/shard_map/cond
  367.7 26.4 %collective-permute-start.156 = (f32[1536,64]{0,1:T(8,128)}, f32[1536,64]{0,1:T(8,128)}, u32[]{:S(2)}, u32[]{:S(2)}) collective-permute-start(f32[1536,64]{0,1:T(8,128)} %copy.100), channel_id=1, source_target_pairs={{0,4},{4,0},{8,12},{12,8},{1,5},{5,1},{9,13},{13,9},{2,6},{6,2},{1... | collective-permute-start | bytes 1179656 | tf_op jit(solution)/shard_map/cond/branch_4_fun/ppermute | solution.py:46
  367.9 30.1 %collective-permute-start.157 = (f32[1536,64]{0,1:T(8,128)}, f32[1536,64]{0,1:T(8,128)}, u32[]{:S(2)}, u32[]{:S(2)}) collective-permute-start(f32[1536,64]{0,1:T(8,128)} %copy.100), channel_id=1, source_target_pairs={{0,8},{4,12},{8,0},{12,4},{1,9},{5,13},{9,1},{13,5},{2,10},{6,14},... | collective-permute-start | bytes 1179656 | tf_op jit(solution)/shard_map/cond/branch_4_fun/ppermute | solution.py:46
  369.9 29.4 %collective-permute-start.158 = (f32[1536,64]{0,1:T(8,128)}, f32[1536,64]{0,1:T(8,128)}, u32[]{:S(2)}, u32[]{:S(2)}) collective-permute-start(f32[1536,64]{0,1:T(8,128)} %copy.100), channel_id=1, source_target_pairs={{0,12},{4,8},{8,4},{12,0},{1,13},{5,9},{9,5},{13,1},{2,14},{6,10},... | collective-permute-start | bytes 1179656 | tf_op jit(solution)/shard_map/cond/branch_4_fun/ppermute | solution.py:46
  401.4 4.7 %copy-start.240 = (bf16[64,7168]{1,0:T(8,128)(2,1)S(1)}, bf16[64,7168]{1,0:T(8,128)(2,1)}, u32[]{:S(2)}) copy-start(bf16[64,7168]{1,0:T(8,128)(2,1)} %get-tuple-element.404.proj_up_ref) | copy-start | bytes 2752516 | tf_op jit(solution)/shard_map/cond
  402.8 3.4 copy-start.105
  402.8 3.4 copy-start.108
  402.9 1.6 collective-permute-start.159
  410.5 18.8 %copy-start.299 = (s32[256]{0:T(256)S(1)}, s32[256]{0:T(256)}, u32[]{:S(2)}) copy-start(s32[256]{0:T(256)} %get-tuple-element.423) | copy-start | bytes 3076 | tf_op jit(solution)/shard_map/cond
  410.5 25.3 %copy-start.259 = (bf16[256,3072]{1,0:T(8,128)(2,1)S(1)}, bf16[256,3072]{1,0:T(8,128)(2,1)}, u32[]{:S(2)}) copy-start(bf16[256,3072]{1,0:T(8,128)(2,1)} %get-tuple-element.422) | copy-start | bytes 4718596 | tf_op jit(solution)/shard_map/cond
  412.3 9.5 %collective-permute-start.163 = (f32[8,16,128]{2,1,0:T(8,128)S(1)}, f32[8,16,128]{2,1,0:T(8,128)S(1)}, u32[]{:S(2)}, u32[]{:S(2)}) collective-permute-start(f32[8,16,128]{2,1,0:T(8,128)S(1)} %get-tuple-element.548), channel_id=1, source_target_pairs={{0,4},{4,0},{8,12},{12,8},{1,5},{5,1},{9,13},{13,9},{2,6},{6,2},{1... | collective-permute-start | bytes 196616 | tf_op jit(solution)/shard_map/cond/branch_4_fun/ppermute | solution.py:46
  419.0 8.2 %collective-permute-start.164 = (f32[8,16,128]{2,1,0:T(8,128)S(1)}, f32[8,16,128]{2,1,0:T(8,128)S(1)}, u32[]{:S(2)}, u32[]{:S(2)}) collective-permute-start(f32[8,16,128]{2,1,0:T(8,128)S(1)} %get-tuple-element.550), channel_id=1, source_target_pairs={{0,8},{4,12},{8,0},{12,4},{1,9},{5,13},{9,1},{13,5},{2,10},{6,14},... | collective-permute-start | bytes 196616 | tf_op jit(solution)/shard_map/cond/branch_4_fun/ppermute | solution.py:46
  420.1 7.2 %collective-permute-start.165 = (f32[8,16,128]{2,1,0:T(8,128)S(1)}, f32[8,16,128]{2,1,0:T(8,128)S(1)}, u32[]{:S(2)}, u32[]{:S(2)}) collective-permute-start(f32[8,16,128]{2,1,0:T(8,128)S(1)} %get-tuple-element.549), channel_id=1, source_target_pairs={{0,12},{4,8},{8,4},{12,0},{1,13},{5,9},{9,5},{13,1},{2,14},{6,10},... | collective-permute-start | bytes 196616 | tf_op jit(solution)/shard_map/cond/branch_4_fun/ppermute | solution.py:46
  427.3 2.0 collective-permute-start.166
  427.4 6.4 %collective-permute-start.167 = (f32[8,16,192]{2,1,0:T(8,128)S(1)}, f32[8,16,192]{2,1,0:T(8,128)S(1)}, u32[]{:S(2)}, u32[]{:S(2)}) collective-permute-start(f32[8,16,192]{2,1,0:T(8,128)S(1)} %pad_maximum_fusion.21), channel_id=1, source_target_pairs={{0,2},{1,3},{2,0},{3,1},{4,6},{5,7},{6,4},{7,5},{8,10},{9,11},{10,... | collective-permute-start | bytes 294920 | tf_op jit(solution)/shard_map/cond/branch_4_fun/ppermute | solution.py:46
  428.8 6.9 %collective-permute-start.168 = (f32[8,16,192]{2,1,0:T(8,128)S(1)}, f32[8,16,192]{2,1,0:T(8,128)S(1)}, u32[]{:S(2)}, u32[]{:S(2)}) collective-permute-start(f32[8,16,192]{2,1,0:T(8,128)S(1)} %pad_maximum_fusion.21), channel_id=1, source_target_pairs={{0,3},{1,2},{2,1},{3,0},{4,7},{5,6},{6,5},{7,4},{8,11},{9,10},{10,... | collective-permute-start | bytes 294920 | tf_op jit(solution)/shard_map/cond/branch_4_fun/ppermute | solution.py:46
  437.7 1.9 collective-permute-start.169
  438.0 3.6 collective-permute-start.170
  439.3 3.0 collective-permute-start.171
  442.3 4.4 collective-permute-start.172
  443.6 4.5 collective-permute-start.173
  445.0 5.4 %collective-permute-start.174 = (f32[8,128]{1,0:T(8,128)S(1)}, f32[8,128]{1,0:T(8,128)S(1)}, u32[]{:S(2)}, u32[]{:S(2)}) collective-permute-start(f32[8,128]{1,0:T(8,128)S(1)} %add_add_fusion.19), channel_id=1, source_target_pairs={{0,12},{4,8},{8,4},{12,0},{1,13},{5,9},{9,5},{13,1},{2,14},{6,10},... | collective-permute-start | bytes 12296 | tf_op jit(solution)/shard_map/cond/branch_4_fun/ppermute | solution.py:46
  (19 other events, 33.3 us)
Sparse Core Ops, SparseCore 0:
  71.0 43.2 all-gather.62
  115.9 40.2 all-gather.60
  157.8 35.9 all-gather.58
  195.2 35.9 all-gather.56

commit v4 on v3

--- a/solution.py
+++ b/solution.py
@@ -8,10 +8,11 @@
 from jax.sharding import PartitionSpec as P
 
 CHUNKS = 4
-LEVELS = (672, 704, 736, 768, 832)
+LEVELS = (736, 832)
 TILE = 512
+STEP = 256
 WIDE = 896
-VMEM_LIMIT = 48 * 1024 * 1024
+VMEM_LIMIT = 58 * 1024 * 1024
 
 
 def contract(left_side, right_side):
@@ -143,61 +144,106 @@
     )(value, *after)
 
 
-def partial_kernel(near_ref, a0, a1, b0, b1, keep_ref, other_ref, *refs):
-    out_ref, left, right = refs[-3:]
-    size, width = a0.shape
+def partial_kernel(parts, offset_ref, near_ref, keep_ref, other_ref, *refs):
+    ins, outs = refs[: 4 * parts], refs[-1 - 2 * parts : -1 - parts]
+    rights, left = refs[-1 - parts : -1], refs[-1]
+    width = keep_ref.shape[1]
 
     @pl.when(pl.program_id(0) == 0)
     def _():
         left[...] = jnp.zeros_like(left)
-        left[:size, :] = a0[...]
-        left[size : 2 * size, :] = a1[...]
-        right[:width, :] = left[...].T
-        left[:size, :] = b0[...]
-        left[size : 2 * size, :] = b1[...]
-        right[width:, :] = left[...].T
-
-    total = jnp.dot(keep_ref[...], right[:width, :], preferred_element_type=jnp.float32)
-    total += jnp.dot(other_ref[...], right[width:, :], preferred_element_type=jnp.float32)
-    out_ref[...] = total.T[: 2 * size, :].astype(out_ref.dtype)
-
-
-def partial_product(near_offset, near, rows_here, rows_near, weight, weight_near, dtype, after):
-    size, width = rows_here.shape[0], rows_here.shape[1] // 2
-    hidden = weight_near.shape[0]
-    padded = -(-2 * size // 128) * 128
-    first = pl.BlockSpec((size, width), lambda i, offset, near: (0, near[0]))
-    second = pl.BlockSpec((size, width), lambda i, offset, near: (0, 1 - near[0]))
-
-    def body(offset_ref, near_ref, *refs):
-        partial_kernel(near_ref, *refs)
-
+        for part in range(parts):
+            size = ins[4 * part].shape[0]
+            padded = rights[part].shape[1]
+            for side in range(2):
+                left[:size, :] = ins[4 * part + 2 * side][...]
+                left[size : 2 * size, :] = ins[4 * part + 2 * side + 1][...]
+
+                @pl.loop(0, width // STEP)
+                def _(c):
+                    at = pl.multiple_of(c * STEP, STEP)
+                    to = pl.multiple_of(side * width + c * STEP, STEP)
+                    rights[part][pl.ds(to, STEP), :] = left[:padded, pl.ds(at, STEP)].T
+
+    @pl.loop(0, TILE // STEP)
+    def _(r):
+        at = pl.multiple_of(r * STEP, STEP)
+        rows = pl.ds(at, STEP)
+        for part in range(parts):
+            total = jnp.dot(keep_ref[rows, :], rights[part][:width, :], preferred_element_type=jnp.float32)
+            total += jnp.dot(other_ref[rows, :], rights[part][width:, :], preferred_element_type=jnp.float32)
+            out = outs[part]
+            out[:, rows] = total.T[: out.shape[0], :].astype(out.dtype)
+
+
+def partial_products(near_offset, near, parts, weight, weight_near, after):
+    hidden, width = weight_near.shape
+    ins, in_specs, out_specs, out_shape, rights = [], [], [], [], []
+    most = 0
+    for here, near_rows, dtype in parts:
+        size = here.shape[0]
+        padded = -(-2 * size // 128) * 128
+        most = max(most, padded)
+        ins += [here, near_rows, here, near_rows]
+        in_specs += [pl.BlockSpec((size, width), lambda i, offset, near: (0, near[0]))] * 2
+        in_specs += [pl.BlockSpec((size, width), lambda i, offset, near: (0, 1 - near[0]))] * 2
+        out_specs.append(pl.BlockSpec((2 * size, TILE), lambda i, offset, near: (0, i)))
+        out_shape.append(jax.ShapeDtypeStruct((2 * size, hidden), dtype))
+        rights.append(pltpu.VMEM((2 * width, padded), jnp.bfloat16))
+    total = sum(shape.shape[0] for shape in out_shape)
     return pl.pallas_call(
-        body,
+        functools.partial(partial_kernel, len(parts)),
         grid_spec=pltpu.PrefetchScalarGridSpec(
             num_scalar_prefetch=2,
             grid=(hidden // TILE,),
-            in_specs=[first, first, second, second]
-            + [
+            in_specs=[
                 pl.BlockSpec((TILE, width), lambda i, offset, near: (offset[0] + i, 0)),
                 pl.BlockSpec((TILE, width), lambda i, offset, near: (i, 0)),
             ]
+            + in_specs
             + [pl.BlockSpec(memory_space=pl.ANY)] * len(after),
-            out_specs=pl.BlockSpec((2 * size, TILE), lambda i, offset, near: (0, i)),
-            scratch_shapes=[
-                pltpu.VMEM((padded, width), jnp.bfloat16),
-                pltpu.VMEM((2 * width, padded), jnp.bfloat16),
-            ],
-        ),
-        out_shape=jax.ShapeDtypeStruct((2 * size, hidden), dtype),
+            out_specs=out_specs,
+            scratch_shapes=rights + [pltpu.VMEM((most, width), jnp.bfloat16)],
+        ),
+        out_shape=out_shape,
         compiler_params=kernel_params(),
         cost_estimate=pl.CostEstimate(
-            flops=8 * size * width * hidden,
-            bytes_accessed=4 * width * hidden + 8 * size * hidden,
+            flops=4 * total * width * hidden,
+            bytes_accessed=4 * width * hidden + 4 * total * hidden,
             transcendentals=0,
         ),
-        name="partial_product",
-    )(near_offset, near, rows_here, rows_near, rows_here, rows_near, weight, weight_near, *after)
+        name="partial_products",
+    )(near_offset, near, weight, weight_near, *ins, *after)
+
+
+def copy_kernel(at_ref, value, *refs):
+    refs[-1][...] = value[...]
+
+
+def copy_half(array, at, axis, after):
+    rows, columns = array.shape
+    steps = 7
+    if axis == 0:
+        rows //= 2
+        block = (rows // steps, columns)
+        source, goal = (lambda i, at: (at[0] * steps + i, 0)), (lambda i, at: (i, 0))
+    else:
+        columns //= 2
+        block = (rows, columns // steps)
+        source, goal = (lambda i, at: (0, at[0] * steps + i)), (lambda i, at: (0, i))
+    return pl.pallas_call(
+        copy_kernel,
+        grid_spec=pltpu.PrefetchScalarGridSpec(
+            num_scalar_prefetch=1,
+            grid=(steps,),
+            in_specs=[pl.BlockSpec(block, source)] + [pl.BlockSpec(memory_space=pl.ANY)] * len(after),
+            out_specs=pl.BlockSpec(block, goal),
+        ),
+        out_shape=jax.ShapeDtypeStruct((rows, columns), array.dtype),
+        compiler_params=kernel_params(),
+        cost_estimate=pl.CostEstimate(flops=0, bytes_accessed=4 * rows * columns, transcendentals=0),
+        name="copy_half",
+    )(at, array, *after)
 
 
 def finish_kernel(near_ref, own_ref, came_ref, gate_ref, up_ref, proj_gate_ref, proj_up_ref, *refs):
@@ -270,8 +316,6 @@
         proj_output,
         proj_gate,
         proj_up,
-        query_sketches,
-        query_slot,
         rev_slot,
         own_lengths,
         near_lengths,
@@ -319,21 +363,22 @@
     doubles = [2 * s for s in sizes]
     blocks = pack(starts, sizes, no_offset, place, grad_rows, grad_near)
     gathered = [lax.all_gather(block, "tensor", axis=1, tiled=True) for block in blocks]
-    weight_near = swap(take(down_weight, (1 - near) * half_hidden, half_hidden, 0), "example", 1)
-
-    def send_hidden(array):
-        rows = array.reshape(row_total, hidden_local)
-        return rows, swap(take(rows, (1 - near) * half_hidden, half_hidden, 1), "example", 1)
-
-    gate_both, up_both = send_hidden(gate_pre), send_hidden(up_pre)
-
     near_at, far_at = near.astype(jnp.int32).reshape(1), far.astype(jnp.int32).reshape(1)
+    gate_rows = gate_pre.reshape(row_total, hidden_local)
+    up_rows = up_pre.reshape(row_total, hidden_local)
+    weight_sent = copy_half(down_weight, 1 - near_at, 0, (blocks[0],))
+    gate_sent = copy_half(gate_rows, 1 - near_at, 1, (weight_sent,))
+    up_sent = copy_half(up_rows, 1 - near_at, 1, (gate_sent,))
+    weight_near = swap(weight_sent, "example", 1)
+    gate_near = swap(gate_sent, "example", 1)
+    up_near = swap(up_sent, "example", 1)
+
     width = down_weight.shape[1]
     came, own, right = [], [], []
     packed = {}
 
-    def product(rows_here, rows_near, dtype, after):
-        return partial_product(offset, near_at, rows_here, rows_near, down_weight, weight_near, dtype, after)
+    def products(parts, after):
+        return partial_products(offset, near_at, parts, down_weight, weight_near, after)
 
     def finish_step(k, after):
         right.append(
@@ -343,26 +388,28 @@
             )
         )
 
-    last, waiting = (), []
+    last, waiting = (up_sent,), []
     for k in range(CHUNKS):
         mine, away = cut(far_at, gathered[k], width, last)
         far_rows = swap(away, "example", 2)
         mine_near = swap(mine, "example", 1)
         done = []
         if k == 1:
-            packed["gate"] = pack(starts, doubles, offset, place, *gate_both, after=(away,))
-            packed["up"] = pack(starts, doubles, offset, place, *up_both, after=(away,))
-        if k > 0:
-            own.append(product(*waiting, jnp.float32, (away,)))
-            done.append(own[-1])
+            packed["gate"] = pack(starts, doubles, offset, place, gate_rows, gate_near, after=(away,))
+            packed["up"] = pack(starts, doubles, offset, place, up_rows, up_near, after=(away,))
+            done += [packed["gate"][0], packed["up"][0]]
         if k > 1:
             finish_step(k - 2, (away,))
             done.append(right[-1])
+        parts = [(far_rows, swap(far_rows, "example", 1), jnp.bfloat16)]
+        if k > 0:
+            parts.append((*waiting, jnp.float32))
+        results = products(parts, tuple(done))
+        own += results[1:]
         waiting = [mine, mine_near]
-        partial = product(far_rows, swap(far_rows, "example", 1), jnp.bfloat16, tuple(done))
-        came.append(swap(partial, "example", 2))
-        last = (partial,)
-    own.append(product(*waiting, jnp.float32, last))
+        came.append(swap(results[0], "example", 2))
+        last = (results[0],)
+    own += products([(*waiting, jnp.float32)], last)
     finish_step(CHUNKS - 2, (own[-1],))
     finish_step(CHUNKS - 1, (right[-1],))
 
@@ -407,15 +454,7 @@
     sketch_late = lax.dot_general(
         left, jnp.concatenate(right), (((0,), (0,)), ((), ())), precision=lax.Precision.HIGHEST
     ).reshape(rev_pairs, rank_size, 2 * rank_size)
-    sketch_late = scatter_over(sketch_late, "tensor", 1)
-    revision_pairs = sum_over(jnp.concatenate([sketch_late, sketch_down], axis=2), "example")
-    example_scores = contract_exact(
-        revision_pairs.reshape(rev_pairs, -1), query_sketches.astype(jnp.float32)
-    )
-    query_pairs = query_slot.shape[0] * 4 // 2
-    pair_terms = contract_exact(example_scores, pairing_table(query_slot, query_pairs))
-    total = sum_over(scatter_over(pair_terms, "example", 1), "tensor")
-    return total / jnp.float32(rank_size * rank_size)
+    return sketch_late, sketch_down
 
 
 def local_four(
@@ -448,7 +487,7 @@
     full = 2 * row_total
     levels = [level for level in LEVELS if level < full] + [full]
     branch = jnp.sum((most[0] > jnp.array(levels[:-1], jnp.int32)).astype(jnp.int32))
-    return lax.switch(
+    sketch_late, sketch_down = lax.switch(
         branch,
         [functools.partial(packed_scores, level) for level in levels],
         (
@@ -463,13 +502,22 @@
             proj_output,
             proj_gate,
             proj_up,
-            query_sketches,
-            query_slot,
             rev_slot,
             rev_lengths,
             others[0],
         ),
     )
+    rank_size = proj_input.shape[0]
+    rev_pairs = rev_slot.shape[0] // 2
+    sketch_late = scatter_over(sketch_late, "tensor", 1)
+    revision_pairs = sum_over(jnp.concatenate([sketch_late, sketch_down], axis=2), "example")
+    example_scores = contract_exact(
+        revision_pairs.reshape(rev_pairs, -1), query_sketches.astype(jnp.float32)
+    )
+    query_pairs = query_slot.shape[0] * 4 // 2
+    pair_terms = contract_exact(example_scores, pairing_table(query_slot, query_pairs))
+    total = sum_over(scatter_over(pair_terms, "example", 1), "tensor")
+    return total / jnp.float32(rank_size * rank_size)
 
 
 def local_any(

time: 467 us -> 440 us (0.942); the launches traced: 467 us -> 435 us
  local copies, waits for them, and re-layouts: 47.9 us -> 16.3 us
  Pallas kernels: 175 us -> 205 us
  loops' own time: 37.9 us -> 12.9 us
  waiting for transfers between devices: 122 us -> 108 us
  other arithmetic: 8.9 us -> 21.6 us
    another operation x1, loops' own time: 37.9 us -> 12.9 us  [local_four(): lax.switch(branch, [functools.partial(packed_scores, level) for level in...]
    dynamic_slice x6 -> x3, local copies, waits for them, and re-layouts: 22.4 us -> 1.02 us  [take(): return lax.dynamic_slice_in_dim(array, start, size, axis)]
    pallas_call x8, Pallas kernels: 124 us -> 141 us  [the longest x5 115 us: partial_products(): pl.pallas_call(functools.partial(partial_kernel, len(parts)), grid_spec=p...]
    all_gather x4, waiting for transfers between devices: 42 us -> 25.7 us  [packed_scores(): lax.all_gather(block, 'tensor', axis=1, tiled=True)]
    cond x77 -> x54, local copies, waits for them, and re-layouts: 18.9 us -> 6.43 us
    pallas_call x4, Pallas kernels: 5.93 us -> 15.2 us  [cut(): pl.pallas_call(cut_kernel, grid_spec=pltpu.PrefetchScalarGridSpec(num_sca...]
    concatenate x3, other arithmetic: 0.28 us -> 5.03 us  [finish_step(): jnp.concatenate(finish(wide_offset, own[k], came[k], packed['gate'][k], p...]
  transfers between devices with their start and end apart: 44 -> 44, of which waited for: 15 -> 15; matrix products, arithmetic and copies ran while one was open for 9% -> 8% of each run, Pallas kernels for 36% -> 42%
where the time goes in v4:
time: 440 us; the launch traced here: 435 us
  Pallas kernels  205 us (47%)
  waiting for transfers between devices  108 us (25%)
  starting transfers between devices  36 us (8%)
  other arithmetic  21.6 us (5%)
  matrix products  17.8 us (4%)
  between operations  17.3 us (4%)
  local copies, waits for them, and re-layouts  16.3 us (4%)
  loops' own time  12.9 us (3%)
    pallas_call x5, Pallas kernels, partial_products(): pl.pallas_call(functools.partial(partial_kernel, len(parts)), grid_spec=p...  115 us
    ppermute x39, waiting for transfers between devices, swap(): return lax.ppermute(array, axis, [(i, i ^ bits) for i in range(count)])  81.6 us
    ppermute x39, starting transfers between devices, swap(): return lax.ppermute(array, axis, [(i, i ^ bits) for i in range(count)])  31.9 us
    pallas_call x3, Pallas kernels, pack(): pl.pallas_call(functools.partial(pack_kernel, starts, sizes), grid_spec=p...  26.1 us
    all_gather x4, waiting for transfers between devices, packed_scores(): lax.all_gather(block, 'tensor', axis=1, tiled=True)  25.7 us
    pallas_call x3, Pallas kernels, copy_half(): pl.pallas_call(copy_kernel, grid_spec=pltpu.PrefetchScalarGridSpec(num_sc...  25.3 us
    pallas_call x4, Pallas kernels, finish(): pl.pallas_call(finish_kernel, grid_spec=pltpu.PrefetchScalarGridSpec(num_...  21 us
    pallas_call x4, Pallas kernels, cut(): pl.pallas_call(cut_kernel, grid_spec=pltpu.PrefetchScalarGridSpec(num_sca...  15.2 us
  transfers between devices with their start and end apart: 44, of which 15 were waited for; matrix products, arithmetic and copies ran while one was open for 8% of the time, Pallas kernels for 42%

profile of v4, /device:TPU:0, one launch (start us, length us, event | category | flops | bytes accessed | tf_op | source)
XLA Modules:
  0.0 435.2 jit_solution(780279954775273361)
XLA Ops:
  7.0 2.9 collective-permute-start.70
  10.0 1.4 reduce_sum.99
  15.9 3.4 collective-permute-start.72
  20.3 1.4 fusion.178
  22.4 367.1 %conditional.1 = (f32[8,64,128]{2,1,0:T(8,128)}, f32[8,16,64]{2,1,0:T(8,128)}) conditional(s32[]{:T(128)} %clamp.3, (s32[4]{0:T(128)}, s32[4]{0:T(128)S(1)}, s32[16]{0:T(128)}, bf16[4,128,2048]{2,1,0:T(8,128)(2,1)}, bf16[64,2048]{1,0:T(8,128)(2,1)}, /*index=5*/bf16[4,128,7168]{2,1,0:T(8,128)(2,1)}, ...), branch_computations={%region_5.10_spmd, %region_10.15_spmd, %region_15.20_spmd} | conditional | flops 80654819328 | bytes 579718464 | solution.py:490
  24.7 1.3 bitcast_subtract_fusion.1
  28.2 5.8 %pack_rows.9 = (bf16[96,2048]{1,0:T(8,128)(2,1)}, bf16[96,2048]{1,0:T(8,128)(2,1)}, bf16[96,2048]{1,0:T(8,128)(2,1)}, bf16[80,2048]{1,0:T(8,128)(2,1)}) custom-call(s32[1]{0:T(128)} %constant.245.clone.near_ref, s32[1,1024]{1,0:T(1,128)} %bitcast_select_fusion.place_ref, bf16[512,2048]{1,0:T(8,128)(2,1)} %get-tuple-element.97.own_ref, ...), custom_call_target="tpu_custom_call" | custom-call | flops 1543503872 | bytes 5701632 | tf_op jit(solution)/shard_map/cond/branch_0_fun/pack_rows/pallas_call | solution.py:78
  34.0 13.1 %copy_half.9.refs_0_ = bf16[3584,2048]{1,0:T(8,128)(2,1)} custom-call(s32[1]{0:T(128)S(6)} %sub.136.at_ref, bf16[7168,2048]{1,0:T(8,128)(2,1)} %get-tuple-element.99.value.keep_ref, bf16[96,2048]{1,0:T(8,128)(2,1)} %get-tuple-element.101.refs_0_), custom_call_target="tpu_custom_call" | custom-call | bytes 29360128 | tf_op jit(solution)/shard_map/cond/branch_0_fun/copy_half/pallas_call | solution.py:234
  47.9 6.1 %copy_half.10.refs_0_ = bf16[512,3584]{1,0:T(8,128)(2,1)} custom-call(s32[1]{0:T(128)S(6)} %sub.136.at_ref, bf16[512,7168]{1,0:T(8,128)(2,1)} %bitcast.189, bf16[3584,2048]{1,0:T(8,128)(2,1)} %copy_half.9.refs_0_), custom_call_target="tpu_custom_call" | custom-call | bytes 7340032 | tf_op jit(solution)/shard_map/cond/branch_0_fun/copy_half/pallas_call | solution.py:234
  54.0 6.1 %copy_half.11.refs_0_ = bf16[512,3584]{1,0:T(8,128)(2,1)} custom-call(s32[1]{0:T(128)S(6)} %sub.136.at_ref, bf16[512,7168]{1,0:T(8,128)(2,1)} %bitcast.180, bf16[512,3584]{1,0:T(8,128)(2,1)} %copy_half.10.refs_0_), custom_call_target="tpu_custom_call" | custom-call | bytes 7340032 | tf_op jit(solution)/shard_map/cond/branch_0_fun/copy_half/pallas_call | solution.py:234
  60.6 25.6 %all-gather.19.cloned.1.call-done.mine_in.away_in = bf16[96,8192]{1,0:T(8,128)(2,1)} async-done(((bf16[96,2048]{1,0:T(8,128)(2,1)}), bf16[96,8192]{1,0:T(8,128)(2,1)}) %all-gather.19.cloned.1.call-update) | async-done | bytes 1572880 | tf_op jit(solution)/shard_map/cond/branch_0_fun/all_gather | solution.py:365
  86.2 3.7 cut_columns.12
  90.0 1.5 collective-permute-start.1
  92.0 17.3 %collective-permute-done.1.refs_0_.refs_2_ = bf16[96,4096]{1,0:T(8,128)(2,1)S(1)} collective-permute-done((bf16[96,4096]{1,0:T(8,128)(2,1)}, bf16[96,4096]{1,0:T(8,128)(2,1)S(1)}, u32[]{:S(2)}, u32[]{:S(2)}) %collective-permute-start.1) | collective-permute-done | bytes 786464 | tf_op jit(solution)/shard_map/cond/branch_0_fun/ppermute | solution.py:47
  109.3 2.3 collective-permute-done.2.refs_1_.refs_3_
  112.5 18.1 %partial_products.15.refs_0_ = bf16[192,3584]{1,0:T(8,128)(2,1)} custom-call(s32[1]{0:T(128)} %bitcast.9.offset_ref.near_ref, s32[1]{0:T(128)} %bitcast.10.near_ref, bf16[7168,2048]{1,0:T(8,128)(2,1)} %get-tuple-element.99.value.keep_ref, bf16[3584,2048]{1,0:T(8,128)(2,1)} %collective-permute-done.other_ref, bf16[96,4096]{1,0:T(8,128)(2,1)} %copy-done.29, ...), custom_call_target="tpu_custom_call" | custom-call | flops 5637144576 | bytes 32112640 | tf_op jit(solution)/shard_map/cond/branch_0_fun/partial_products/pallas_call | solution.py:194
  130.6 3.8 cut_columns.13
  134.5 1.5 collective-permute-start.3
  136.7 18.4 %collective-permute-done.3.refs_0_.refs_2_ = bf16[96,4096]{1,0:T(8,128)(2,1)S(1)} collective-permute-done((bf16[96,4096]{1,0:T(8,128)(2,1)}, bf16[96,4096]{1,0:T(8,128)(2,1)S(1)}, u32[]{:S(2)}, u32[]{:S(2)}) %collective-permute-start.3) | collective-permute-done | bytes 786464 | tf_op jit(solution)/shard_map/cond/branch_0_fun/ppermute | solution.py:47
  155.1 10.3 %pack_rows.11 = (bf16[192,3584]{1,0:T(8,128)(2,1)}, bf16[192,3584]{1,0:T(8,128)(2,1)}, bf16[192,3584]{1,0:T(8,128)(2,1)}, bf16[160,3584]{1,0:T(8,128)(2,1)}) custom-call(s32[1]{0:T(128)} %bitcast.9.offset_ref.near_ref, s32[1,1024]{1,0:T(1,128)} %bitcast_select_fusion.place_ref, bf16[512,7168]{1,0:T(8,128)(2,1)} %bitcast.181, ...), custom_call_target="tpu_custom_call" | custom-call | flops 5402263552 | bytes 12615680 | tf_op jit(solution)/shard_map/cond/branch_0_fun/pack_rows/pallas_call | solution.py:78
  165.4 10.1 %pack_rows.10 = (bf16[192,3584]{1,0:T(8,128)(2,1)}, bf16[192,3584]{1,0:T(8,128)(2,1)}, bf16[192,3584]{1,0:T(8,128)(2,1)}, bf16[160,3584]{1,0:T(8,128)(2,1)}) custom-call(s32[1]{0:T(128)} %bitcast.9.offset_ref.near_ref, s32[1,1024]{1,0:T(1,128)} %bitcast_select_fusion.place_ref, bf16[512,7168]{1,0:T(8,128)(2,1)} %bitcast.190, ...), custom_call_target="tpu_custom_call" | custom-call | flops 5402263552 | bytes 12615680 | tf_op jit(solution)/shard_map/cond/branch_0_fun/pack_rows/pallas_call | solution.py:78
  176.7 26.4 %partial_products.16 = (bf16[192,3584]{1,0:T(8,128)(2,1)}, f32[192,3584]{1,0:T(8,128)}) custom-call(s32[1]{0:T(128)} %bitcast.9.offset_ref.near_ref, s32[1]{0:T(128)} %bitcast.10.near_ref, bf16[7168,2048]{1,0:T(8,128)(2,1)} %get-tuple-element.99.value.keep_ref, bf16[3584,2048]{1,0:T(8,128)(2,1)} %collective-permute-done.other_ref, ...), custom_call_target="tpu_custom_call" | custom-call | flops 11274289152 | bytes 34865152 | tf_op jit(solution)/shard_map/cond/branch_0_fun/partial_products/pallas_call | solution.py:194
  203.0 3.7 cut_columns.14
  206.8 1.5 collective-permute-start.8
  208.3 8.5 %fusion.5 = f32[512,64]{1,0:T(8,128)} fusion(bf16[64,7168]{1,0:T(8,128)(2,1)S(1)} %copy-done.63, bf16[512,7168]{1,0:T(8,128)(2,1)} %bitcast.182, bf16[512,7168]{1,0:T(8,128)(2,1)} %bitcast.191), kind=kOutput, calls=%fused_computation.7 | convolution fusion | flops 499122176 | bytes 15728640 | tf_op jit(solution)/shard_map/cond/branch_0_fun/dot_general | solution.py:19
  217.2 9.6 %collective-permute-done.8.refs_0_.refs_2_ = bf16[96,4096]{1,0:T(8,128)(2,1)} collective-permute-done((bf16[96,4096]{1,0:T(8,128)(2,1)}, bf16[96,4096]{1,0:T(8,128)(2,1)}, u32[]{:S(2)}, u32[]{:S(2)}) %collective-permute-start.8) | collective-permute-done | bytes 786464 | tf_op jit(solution)/shard_map/cond/branch_0_fun/ppermute | solution.py:47
  227.5 1.6 collective-permute-start.15
  229.1 5.3 %finish_chunk.12 = (f32[192,64]{1,0:T(8,128)}, f32[192,64]{1,0:T(8,128)}) custom-call(s32[1]{0:T(128)} %bitcast.13.near_ref, f32[192,3584]{1,0:T(8,128)} %get-tuple-element.113.own_ref, bf16[192,3584]{1,0:T(8,128)(2,1)} %collective-permute-done.11.came_ref, bf16[192,3584]{1,0:T(8,128)(2,1)} %get-tuple-element.108.refs_8_.gate_ref, ...), custom_call_target="tpu_custom_call" | custom-call | flops 176160768 | bytes 6881280 | tf_op jit(solution)/shard_map/cond/branch_0_fun/finish_chunk/pallas_call | solution.py:274
  234.4 1.7 pad_maximum_fusion.1.refs_8_
  237.9 26.3 %partial_products.17 = (bf16[192,3584]{1,0:T(8,128)(2,1)}, f32[192,3584]{1,0:T(8,128)}) custom-call(s32[1]{0:T(128)} %bitcast.9.offset_ref.near_ref, s32[1]{0:T(128)} %bitcast.10.near_ref, bf16[7168,2048]{1,0:T(8,128)(2,1)} %get-tuple-element.99.value.keep_ref, bf16[3584,2048]{1,0:T(8,128)(2,1)} %collective-permute-done.other_ref, ...), custom_call_target="tpu_custom_call" | custom-call | flops 11274289152 | bytes 34865152 | tf_op jit(solution)/shard_map/cond/branch_0_fun/partial_products/pallas_call | solution.py:194
  264.3 3.9 cut_columns.15
  269.7 15.8 %collective-permute-done.12.refs_0_.refs_2_ = bf16[80,4096]{1,0:T(8,128)(2,1)} collective-permute-done((bf16[80,4096]{1,0:T(8,128)(2,1)}, bf16[80,4096]{1,0:T(8,128)(2,1)}, u32[]{:S(2)}, u32[]{:S(2)}) %collective-permute-start.12) | collective-permute-done | bytes 655392 | tf_op jit(solution)/shard_map/cond/branch_0_fun/ppermute | solution.py:47
  287.9 5.3 %finish_chunk.13 = (f32[192,64]{1,0:T(8,128)}, f32[192,64]{1,0:T(8,128)}) custom-call(s32[1]{0:T(128)} %bitcast.13.near_ref, f32[192,3584]{1,0:T(8,128)} %get-tuple-element.121.own_ref, bf16[192,3584]{1,0:T(8,128)(2,1)} %collective-permute-done.15.came_ref, bf16[192,3584]{1,0:T(8,128)(2,1)} %get-tuple-element.122.gate_ref, ...), custom_call_target="tpu_custom_call" | custom-call | flops 176160768 | bytes 6881280 | tf_op jit(solution)/shard_map/cond/branch_0_fun/finish_chunk/pallas_call | solution.py:274
  293.2 1.7 pad_maximum_fusion.2.refs_8_
  296.6 26.2 %partial_products.18 = (bf16[160,3584]{1,0:T(8,128)(2,1)}, f32[192,3584]{1,0:T(8,128)}) custom-call(s32[1]{0:T(128)} %bitcast.9.offset_ref.near_ref, s32[1]{0:T(128)} %bitcast.10.near_ref, bf16[7168,2048]{1,0:T(8,128)(2,1)} %get-tuple-element.99.value.keep_ref, bf16[3584,2048]{1,0:T(8,128)(2,1)} %collective-permute-done.other_ref, ...), custom_call_target="tpu_custom_call" | custom-call | flops 10334765056 | bytes 34406400 | tf_op jit(solution)/shard_map/cond/branch_0_fun/partial_products/pallas_call | solution.py:194
  322.9 2.1 ordered_copy.3
  324.9 2.1 copy.33
  327.5 1.5 collective-permute-start.17
  329.0 2.5 collective-permute-start.18
  331.5 1.5 collective-permute-start.22
  333.0 18.2 %partial_products.19.refs_0_.own_ref = f32[160,3584]{1,0:T(8,128)} custom-call(s32[1]{0:T(128)} %bitcast.9.offset_ref.near_ref, s32[1]{0:T(128)} %bitcast.10.near_ref, bf16[7168,2048]{1,0:T(8,128)(2,1)} %get-tuple-element.99.value.keep_ref, bf16[3584,2048]{1,0:T(8,128)(2,1)} %collective-permute-done.other_ref, ...), custom_call_target="tpu_custom_call" | custom-call | flops 4697620480 | bytes 31653888 | tf_op jit(solution)/shard_map/cond/branch_0_fun/partial_products/pallas_call | solution.py:194
  351.2 5.3 %finish_chunk.14 = (f32[192,64]{1,0:T(8,128)}, f32[192,64]{1,0:T(8,128)}) custom-call(s32[1]{0:T(128)} %bitcast.13.near_ref, f32[192,3584]{1,0:T(8,128)} %get-tuple-element.127.own_ref, bf16[192,3584]{1,0:T(8,128)(2,1)} %collective-permute-done.20.came_ref, bf16[192,3584]{1,0:T(8,128)(2,1)} %get-tuple-element.128.gate_ref, ...), custom_call_target="tpu_custom_call" | custom-call | flops 176160768 | bytes 6881280 | tf_op jit(solution)/shard_map/cond/branch_0_fun/finish_chunk/pallas_call | solution.py:274
  356.5 1.7 pad_maximum_fusion.3.refs_0_
  358.2 2.2 copy.34
  360.4 2.2 copy.37
  362.5 2.2 copy.38
  364.7 2.0 add_add_fusion
  368.5 1.5 fusion.7
  370.1 5.0 %finish_chunk.15 = (f32[160,64]{1,0:T(8,128)}, f32[160,64]{1,0:T(8,128)}) custom-call(s32[1]{0:T(128)} %bitcast.13.near_ref, f32[160,3584]{1,0:T(8,128)} %partial_products.19.refs_0_.own_ref, bf16[160,3584]{1,0:T(8,128)(2,1)} %collective-permute-done.22.came_ref, bf16[160,3584]{1,0:T(8,128)(2,1)} %get-tuple-element.133.gate_ref, ...), custom_call_target="tpu_custom_call" | custom-call | flops 146800640 | bytes 5734400 | tf_op jit(solution)/shard_map/cond/branch_0_fun/finish_chunk/pallas_call | solution.py:274
  375.2 3.2 fusion.9
  390.4 3.2 collective-permute-start.74
  394.7 1.4 collective-permute-start.76
  396.3 5.6 %collective-permute-done.75 = f32[8,16,128]{2,1,0:T(8,128)S(1)} collective-permute-done((f32[8,16,128]{2,1,0:T(8,128)S(1)}, f32[8,16,128]{2,1,0:T(8,128)S(1)}, u32[]{:S(2)}, u32[]{:S(2)}) %collective-permute-start.75) | collective-permute-done | bytes 65568 | tf_op jit(solution)/shard_map/ppermute | solution.py:47
  403.7 1.6 collective-permute-start.78
  406.3 3.8 collective-permute-done.78
  410.1 1.9 collective-permute-done.79
  413.0 1.3 fusion.195
  415.2 1.5 collective-permute-start.81
  416.8 2.0 collective-permute-done.81
  419.7 1.6 collective-permute-start.83
  421.3 1.2 collective-permute-start.84
  422.5 1.6 collective-permute-start.85
  424.1 1.7 collective-permute-done.84
  425.8 2.1 collective-permute-done.85
  (157 shorter events, 30.0 us)
Async XLA Ops:
  6.5 406.5 %copy-start = (bf16[256,3072]{1,0:T(8,128)(2,1)S(1)}, bf16[256,3072]{1,0:T(8,128)(2,1)}, u32[]{:S(2)}) copy-start(bf16[256,3072]{1,0:T(8,128)(2,1)} %param.28) | copy-start | bytes 4718596
  6.5 15.8 %collective-permute-start.73 = (bf16[512,2048]{1,0:T(8,128)(2,1)}, bf16[512,2048]{1,0:T(8,128)(2,1)}, u32[]{:S(2)}, u32[]{:S(2)}) collective-permute-start(bf16[512,2048]{1,0:T(8,128)(2,1)} %bitcast.201), channel_id=1, source_target_pairs={{0,1},{1,0},{2,3},{3,2},{4,5},{5,4},{6,7},{7,6},{8,9},{9,8},{10,11... | collective-permute-start | bytes 6291464 | tf_op jit(solution)/shard_map/ppermute | solution.py:47
  7.0 4.4 %collective-permute-start.69 = (s32[4]{0:T(128)}, s32[4]{0:T(128)S(1)}, u32[]{:S(2)}, u32[]{:S(2)}) collective-permute-start(s32[4]{0:T(128)} %param.29), channel_id=1, source_target_pairs={{0,1},{1,0},{2,3},{3,2},{4,5},{5,4},{6,7},{7,6},{8,9},{9,8},{10,11... | collective-permute-start | bytes 56 | tf_op jit(solution)/shard_map/ppermute | solution.py:47
  7.0 6.2 %collective-permute-start.70 = (s32[4]{0:T(128)}, s32[4]{0:T(128)S(1)}, u32[]{:S(2)}, u32[]{:S(2)}) collective-permute-start(s32[4]{0:T(128)} %param.29), channel_id=1, source_target_pairs={{0,2},{1,3},{2,0},{3,1},{4,6},{5,7},{6,4},{7,5},{8,10},{9,11},{10,... | collective-permute-start | bytes 56 | tf_op jit(solution)/shard_map/ppermute | solution.py:47
  10.0 4.0 collective-permute-start.71
  15.9 3.8 collective-permute-start.72
  22.4 63.8 %all-gather.19.cloned.1.call-start = ((), (), s32[]{:S(2)}) async-start(), calls=%async_computation.3 | async-start | bytes 1966080 | tf_op jit(solution)/shard_map/cond/branch_0_fun/all_gather | solution.py:365
  47.1 64.5 %collective-permute-start = (bf16[3584,2048]{1,0:T(8,128)(2,1)}, bf16[3584,2048]{1,0:T(8,128)(2,1)}, u32[]{:S(2)}, u32[]{:S(2)}) collective-permute-start(bf16[3584,2048]{1,0:T(8,128)(2,1)} %copy_half.9.refs_0_), channel_id=1, source_target_pairs={{0,1},{1,0},{2,3},{3,2},{4,5},{5,4},{6,7},{7,6},{8,9},{9,8},{10,11... | collective-permute-start | bytes 44040200 | tf_op jit(solution)/shard_map/cond/branch_0_fun/ppermute | solution.py:47
  47.1 83.5 %all-gather.17.cloned.1.call-start = ((), (), s32[]{:S(2)}) async-start(), calls=%async_computation.2 | async-start | bytes 1966080 | tf_op jit(solution)/shard_map/cond/branch_0_fun/all_gather | solution.py:365
  47.8 155.2 %all-gather.15.cloned.1.call-start = ((), (), s32[]{:S(2)}) async-start(), calls=%async_computation.1 | async-start | bytes 1966080 | tf_op jit(solution)/shard_map/cond/branch_0_fun/all_gather | solution.py:365
  60.1 95.0 %collective-permute-start.7 = (bf16[512,3584]{1,0:T(8,128)(2,1)}, bf16[512,3584]{1,0:T(8,128)(2,1)}, u32[]{:S(2)}, u32[]{:S(2)}) collective-permute-start(bf16[512,3584]{1,0:T(8,128)(2,1)} %copy_half.11.refs_0_), channel_id=1, source_target_pairs={{0,1},{1,0},{2,3},{3,2},{4,5},{5,4},{6,7},{7,6},{8,9},{9,8},{10,11... | collective-permute-start | bytes 11010056 | tf_op jit(solution)/shard_map/cond/branch_0_fun/ppermute | solution.py:47
  60.6 104.8 %collective-permute-start.6 = (bf16[512,3584]{1,0:T(8,128)(2,1)}, bf16[512,3584]{1,0:T(8,128)(2,1)}, u32[]{:S(2)}, u32[]{:S(2)}) collective-permute-start(bf16[512,3584]{1,0:T(8,128)(2,1)} %copy_half.10.refs_0_), channel_id=1, source_target_pairs={{0,1},{1,0},{2,3},{3,2},{4,5},{5,4},{6,7},{7,6},{8,9},{9,8},{10,11... | collective-permute-start | bytes 11010056 | tf_op jit(solution)/shard_map/cond/branch_0_fun/ppermute | solution.py:47
  90.0 19.3 %collective-permute-start.1 = (bf16[96,4096]{1,0:T(8,128)(2,1)}, bf16[96,4096]{1,0:T(8,128)(2,1)S(1)}, u32[]{:S(2)}, u32[]{:S(2)}) collective-permute-start(bf16[96,4096]{1,0:T(8,128)(2,1)} %get-tuple-element.105), channel_id=1, source_target_pairs={{0,2},{1,3},{2,0},{3,1},{4,6},{5,7},{6,4},{7,5},{8,10},{9,11},{10,... | collective-permute-start | bytes 2359304 | tf_op jit(solution)/shard_map/cond/branch_0_fun/ppermute | solution.py:47
  91.4 172.8 %all-gather.13.cloned.1.call-start = ((), (), s32[]{:S(2)}) async-start(), calls=%async_computation | async-start | bytes 1638400 | tf_op jit(solution)/shard_map/cond/branch_0_fun/all_gather | solution.py:365
  109.3 2.3 copy-start.29
  109.3 2.3 collective-permute-start.2
  130.6 5.4 %copy-start.21 = (bf16[96,4096]{1,0:T(8,128)(2,1)S(1)}, bf16[96,4096]{1,0:T(8,128)(2,1)}, u32[]{:S(2)}) copy-start(bf16[96,4096]{1,0:T(8,128)(2,1)} %get-tuple-element.107.refs_4_.refs_6_) | copy-start | bytes 2359300 | tf_op jit(solution)/shard_map/cond
  134.5 20.6 %collective-permute-start.3 = (bf16[96,4096]{1,0:T(8,128)(2,1)}, bf16[96,4096]{1,0:T(8,128)(2,1)S(1)}, u32[]{:S(2)}, u32[]{:S(2)}) collective-permute-start(bf16[96,4096]{1,0:T(8,128)(2,1)} %get-tuple-element.106.refs_0_), channel_id=1, source_target_pairs={{0,2},{1,3},{2,0},{3,1},{4,6},{5,7},{6,4},{7,5},{8,10},{9,11},{10,... | collective-permute-start | bytes 2359304 | tf_op jit(solution)/shard_map/cond/branch_0_fun/ppermute | solution.py:47
  136.0 39.5 %collective-permute-start.5 = (bf16[96,4096]{1,0:T(8,128)(2,1)S(1)}, bf16[96,4096]{1,0:T(8,128)(2,1)S(1)}, u32[]{:S(2)}, u32[]{:S(2)}) collective-permute-start(bf16[96,4096]{1,0:T(8,128)(2,1)S(1)} %copy-done.21), channel_id=1, source_target_pairs={{0,1},{1,0},{2,3},{3,2},{4,5},{5,4},{6,7},{7,6},{8,9},{9,8},{10,11... | collective-permute-start | bytes 2359304 | tf_op jit(solution)/shard_map/cond/branch_0_fun/ppermute | solution.py:47
  136.1 93.0 %collective-permute-start.11 = (bf16[192,3584]{1,0:T(8,128)(2,1)}, bf16[192,3584]{1,0:T(8,128)(2,1)}, u32[]{:S(2)}, u32[]{:S(2)}) collective-permute-start(bf16[192,3584]{1,0:T(8,128)(2,1)} %partial_products.15.refs_0_), channel_id=1, source_target_pairs={{0,2},{1,3},{2,0},{3,1},{4,6},{5,7},{6,4},{7,5},{8,10},{9,11},{10,... | collective-permute-start | bytes 4128776 | tf_op jit(solution)/shard_map/cond/branch_0_fun/ppermute | solution.py:47
  155.1 10.3 %copy-start.22 = (bf16[96,4096]{1,0:T(8,128)(2,1)}, bf16[96,4096]{1,0:T(8,128)(2,1)S(1)}, u32[]{:S(2)}) copy-start(bf16[96,4096]{1,0:T(8,128)(2,1)S(1)} %collective-permute-done.3.refs_0_.refs_2_) | copy-start | bytes 2359300 | tf_op jit(solution)/shard_map/cond
  155.1 20.4 %collective-permute-start.4 = (bf16[96,4096]{1,0:T(8,128)(2,1)S(1)}, bf16[96,4096]{1,0:T(8,128)(2,1)S(1)}, u32[]{:S(2)}, u32[]{:S(2)}) collective-permute-start(bf16[96,4096]{1,0:T(8,128)(2,1)S(1)} %collective-permute-done.3.refs_0_.refs_2_), channel_id=1, source_target_pairs={{0,1},{1,0},{2,3},{3,2},{4,5},{5,4},{6,7},{7,6},{8,9},{9,8},{10,11... | collective-permute-start | bytes 2359304 | tf_op jit(solution)/shard_map/cond/branch_0_fun/ppermute | solution.py:47
  203.0 5.3 %copy-start.63 = (bf16[64,7168]{1,0:T(8,128)(2,1)S(1)}, bf16[64,7168]{1,0:T(8,128)(2,1)}, u32[]{:S(2)}) copy-start(bf16[64,7168]{1,0:T(8,128)(2,1)} %get-tuple-element.96) | copy-start | bytes 2752516 | tf_op jit(solution)/shard_map/cond
  206.8 20.0 %collective-permute-start.8 = (bf16[96,4096]{1,0:T(8,128)(2,1)}, bf16[96,4096]{1,0:T(8,128)(2,1)}, u32[]{:S(2)}, u32[]{:S(2)}) collective-permute-start(bf16[96,4096]{1,0:T(8,128)(2,1)} %get-tuple-element.111.refs_0_), channel_id=1, source_target_pairs={{0,2},{1,3},{2,0},{3,1},{4,6},{5,7},{6,4},{7,5},{8,10},{9,11},{10,... | collective-permute-start | bytes 2359304 | tf_op jit(solution)/shard_map/cond/branch_0_fun/ppermute | solution.py:47
  208.3 8.5 %copy-start.60 = (s32[16]{0:T(128)S(1)}, s32[16]{0:T(128)}, u32[]{:S(2)}) copy-start(s32[16]{0:T(128)} %get-tuple-element.91) | copy-start | bytes 196 | tf_op jit(solution)/shard_map/cond
  208.3 20.7 %copy-start.1 = (bf16[64,7168]{1,0:T(8,128)(2,1)S(1)}, bf16[64,7168]{1,0:T(8,128)(2,1)}, u32[]{:S(2)}) copy-start(bf16[64,7168]{1,0:T(8,128)(2,1)} %get-tuple-element.114.proj_gate_ref) | copy-start | bytes 2752516 | tf_op jit(solution)/shard_map/cond
  208.3 20.7 %copy-start.4 = (bf16[64,7168]{1,0:T(8,128)(2,1)S(1)}, bf16[64,7168]{1,0:T(8,128)(2,1)}, u32[]{:S(2)}) copy-start(bf16[64,7168]{1,0:T(8,128)(2,1)} %get-tuple-element.115.proj_up_ref) | copy-start | bytes 2752516 | tf_op jit(solution)/shard_map/cond
  217.2 18.9 %collective-permute-start.10 = (bf16[96,4096]{1,0:T(8,128)(2,1)}, bf16[96,4096]{1,0:T(8,128)(2,1)S(1)}, u32[]{:S(2)}, u32[]{:S(2)}) collective-permute-start(bf16[96,4096]{1,0:T(8,128)(2,1)} %get-tuple-element.112.refs_4_.refs_6_), channel_id=1, source_target_pairs={{0,1},{1,0},{2,3},{3,2},{4,5},{5,4},{6,7},{7,6},{8,9},{9,8},{10,11... | collective-permute-start | bytes 2359304 | tf_op jit(solution)/shard_map/cond/branch_0_fun/ppermute | solution.py:47
  226.8 9.3 %collective-permute-start.9 = (bf16[96,4096]{1,0:T(8,128)(2,1)}, bf16[96,4096]{1,0:T(8,128)(2,1)S(1)}, u32[]{:S(2)}, u32[]{:S(2)}) collective-permute-start(bf16[96,4096]{1,0:T(8,128)(2,1)} %collective-permute-done.8.refs_0_.refs_2_), channel_id=1, source_target_pairs={{0,1},{1,0},{2,3},{3,2},{4,5},{5,4},{6,7},{7,6},{8,9},{9,8},{10,11... | collective-permute-start | bytes 2359304 | tf_op jit(solution)/shard_map/cond/branch_0_fun/ppermute | solution.py:47
  227.5 60.4 %collective-permute-start.15 = (bf16[192,3584]{1,0:T(8,128)(2,1)}, bf16[192,3584]{1,0:T(8,128)(2,1)}, u32[]{:S(2)}, u32[]{:S(2)}) collective-permute-start(bf16[192,3584]{1,0:T(8,128)(2,1)} %get-tuple-element.110.refs_0_), channel_id=1, source_target_pairs={{0,2},{1,3},{2,0},{3,1},{4,6},{5,7},{6,4},{7,5},{8,10},{9,11},{10,... | collective-permute-start | bytes 4128776 | tf_op jit(solution)/shard_map/cond/branch_0_fun/ppermute | solution.py:47
  264.2 4.6 %copy-start.9 = (bf16[512,2048]{1,0:T(8,128)(2,1)S(1)}, bf16[512,2048]{1,0:T(8,128)(2,1)}, u32[]{:S(2)}) copy-start(bf16[512,2048]{1,0:T(8,128)(2,1)} %get-tuple-element.97.own_ref) | copy-start | bytes 6291460 | tf_op jit(solution)/shard_map/cond
  264.3 4.6 %copy-start.34 = (bf16[64,2048]{1,0:T(8,128)(2,1)S(1)}, bf16[64,2048]{1,0:T(8,128)(2,1)}, u32[]{:S(2)}) copy-start(bf16[64,2048]{1,0:T(8,128)(2,1)} %get-tuple-element.98) | copy-start | bytes 786436 | tf_op jit(solution)/shard_map/cond
  268.2 1.5 copy-start.57
  268.2 17.3 %copy-start.7 = (bf16[4,128,2048]{2,1,0:T(8,128)(2,1)S(1)}, bf16[4,128,2048]{2,1,0:T(8,128)(2,1)}, u32[]{:S(2)}) copy-start(bf16[4,128,2048]{2,1,0:T(8,128)(2,1)} %get-tuple-element.92) | copy-start | bytes 6291460 | tf_op jit(solution)/shard_map/cond
  268.2 17.3 %copy-start.32 = (bf16[64,2048]{1,0:T(8,128)(2,1)S(1)}, bf16[64,2048]{1,0:T(8,128)(2,1)}, u32[]{:S(2)}) copy-start(bf16[64,2048]{1,0:T(8,128)(2,1)} %get-tuple-element.93) | copy-start | bytes 786436 | tf_op jit(solution)/shard_map/cond
  268.2 17.3 %collective-permute-start.12 = (bf16[80,4096]{1,0:T(8,128)(2,1)}, bf16[80,4096]{1,0:T(8,128)(2,1)}, u32[]{:S(2)}, u32[]{:S(2)}) collective-permute-start(bf16[80,4096]{1,0:T(8,128)(2,1)} %get-tuple-element.119.refs_0_), channel_id=1, source_target_pairs={{0,2},{1,3},{2,0},{3,1},{4,6},{5,7},{6,4},{7,5},{8,10},{9,11},{10,... | collective-permute-start | bytes 1966088 | tf_op jit(solution)/shard_map/cond/branch_0_fun/ppermute | solution.py:47
  268.8 17.3 %copy-start.36 = (f32[512,64]{1,0:T(8,128)S(1)}, f32[512,64]{1,0:T(8,128)}, u32[]{:S(2)}) copy-start(f32[512,64]{1,0:T(8,128)} %fusion.5) | copy-start | bytes 393220 | tf_op jit(solution)/shard_map/cond
  269.5 25.4 %collective-permute-start.14 = (bf16[96,4096]{1,0:T(8,128)(2,1)}, bf16[96,4096]{1,0:T(8,128)(2,1)S(1)}, u32[]{:S(2)}, u32[]{:S(2)}) collective-permute-start(bf16[96,4096]{1,0:T(8,128)(2,1)} %get-tuple-element.120.refs_4_.refs_6_), channel_id=1, source_target_pairs={{0,1},{1,0},{2,3},{3,2},{4,5},{5,4},{6,7},{7,6},{8,9},{9,8},{10,11... | collective-permute-start | bytes 2359304 | tf_op jit(solution)/shard_map/cond/branch_0_fun/ppermute | solution.py:47
  285.5 9.4 %collective-permute-start.13 = (bf16[80,4096]{1,0:T(8,128)(2,1)}, bf16[80,4096]{1,0:T(8,128)(2,1)S(1)}, u32[]{:S(2)}, u32[]{:S(2)}) collective-permute-start(bf16[80,4096]{1,0:T(8,128)(2,1)} %collective-permute-done.12.refs_0_.refs_2_), channel_id=1, source_target_pairs={{0,1},{1,0},{2,3},{3,2},{4,5},{5,4},{6,7},{7,6},{8,9},{9,8},{10,11... | collective-permute-start | bytes 1966088 | tf_op jit(solution)/shard_map/cond/branch_0_fun/ppermute | solution.py:47
  287.2 64.0 %collective-permute-start.20 = (bf16[192,3584]{1,0:T(8,128)(2,1)}, bf16[192,3584]{1,0:T(8,128)(2,1)}, u32[]{:S(2)}, u32[]{:S(2)}) collective-permute-start(bf16[192,3584]{1,0:T(8,128)(2,1)} %get-tuple-element.118.refs_0_), channel_id=1, source_target_pairs={{0,2},{1,3},{2,0},{3,1},{4,6},{5,7},{6,4},{7,5},{8,10},{9,11},{10,... | collective-permute-start | bytes 4128776 | tf_op jit(solution)/shard_map/cond/branch_0_fun/ppermute | solution.py:47
  287.7 43.8 %collective-permute-start.21 = (bf16[80,4096]{1,0:T(8,128)(2,1)}, bf16[80,4096]{1,0:T(8,128)(2,1)}, u32[]{:S(2)}, u32[]{:S(2)}) collective-permute-start(bf16[80,4096]{1,0:T(8,128)(2,1)} %get-tuple-element.130.refs_0_.refs_2_), channel_id=1, source_target_pairs={{0,1},{1,0},{2,3},{3,2},{4,5},{5,4},{6,7},{7,6},{8,9},{9,8},{10,11... | collective-permute-start | bytes 1966088 | tf_op jit(solution)/shard_map/cond/branch_0_fun/ppermute | solution.py:47
  327.1 31.1 %collective-permute-start.16 = (f32[1536,64]{0,1:T(8,128)}, f32[1536,64]{0,1:T(8,128)}, u32[]{:S(2)}, u32[]{:S(2)}) collective-permute-start(f32[1536,64]{0,1:T(8,128)} %copy.33), channel_id=1, source_target_pairs={{0,4},{4,0},{8,12},{12,8},{1,5},{5,1},{9,13},{13,9},{2,6},{6,2},{1... | collective-permute-start | bytes 1179656 | tf_op jit(solution)/shard_map/cond/branch_0_fun/ppermute | solution.py:47
  327.5 32.9 %collective-permute-start.17 = (f32[1536,64]{0,1:T(8,128)}, f32[1536,64]{0,1:T(8,128)}, u32[]{:S(2)}, u32[]{:S(2)}) collective-permute-start(f32[1536,64]{0,1:T(8,128)} %copy.33), channel_id=1, source_target_pairs={{0,8},{4,12},{8,0},{12,4},{1,9},{5,13},{9,1},{13,5},{2,10},{6,14},... | collective-permute-start | bytes 1179656 | tf_op jit(solution)/shard_map/cond/branch_0_fun/ppermute | solution.py:47
  329.0 33.5 %collective-permute-start.18 = (f32[1536,64]{0,1:T(8,128)}, f32[1536,64]{0,1:T(8,128)}, u32[]{:S(2)}, u32[]{:S(2)}) collective-permute-start(f32[1536,64]{0,1:T(8,128)} %copy.33), channel_id=1, source_target_pairs={{0,12},{4,8},{8,4},{12,0},{1,13},{5,9},{9,5},{13,1},{2,14},{6,10},... | collective-permute-start | bytes 1179656 | tf_op jit(solution)/shard_map/cond/branch_0_fun/ppermute | solution.py:47
  331.5 38.6 %collective-permute-start.22 = (bf16[160,3584]{1,0:T(8,128)(2,1)}, bf16[160,3584]{1,0:T(8,128)(2,1)}, u32[]{:S(2)}, u32[]{:S(2)}) collective-permute-start(bf16[160,3584]{1,0:T(8,128)(2,1)} %get-tuple-element.126.refs_0_.refs_4_), channel_id=1, source_target_pairs={{0,2},{1,3},{2,0},{3,1},{4,6},{5,7},{6,4},{7,5},{8,10},{9,11},{10,... | collective-permute-start | bytes 3440648 | tf_op jit(solution)/shard_map/cond/branch_0_fun/ppermute | solution.py:47
  366.8 1.8 collective-permute-start.19
  370.1 5.1 %copy-start.49 = (f32[192,64]{1,0:T(8,128)S(1)}, f32[192,64]{1,0:T(8,128)}, u32[]{:S(2)}) copy-start(f32[192,64]{1,0:T(8,128)} %get-tuple-element.116) | copy-start | bytes 147460 | tf_op jit(solution)/shard_map/cond
  370.1 5.1 %copy-start.50 = (f32[192,64]{1,0:T(8,128)S(1)}, f32[192,64]{1,0:T(8,128)}, u32[]{:S(2)}) copy-start(f32[192,64]{1,0:T(8,128)} %get-tuple-element.117) | copy-start | bytes 147460 | tf_op jit(solution)/shard_map/cond
  370.1 5.1 %copy-start.51 = (f32[192,64]{1,0:T(8,128)S(1)}, f32[192,64]{1,0:T(8,128)}, u32[]{:S(2)}) copy-start(f32[192,64]{1,0:T(8,128)} %get-tuple-element.124) | copy-start | bytes 147460 | tf_op jit(solution)/shard_map/cond
  370.1 5.1 %copy-start.52 = (f32[192,64]{1,0:T(8,128)S(1)}, f32[192,64]{1,0:T(8,128)}, u32[]{:S(2)}) copy-start(f32[192,64]{1,0:T(8,128)} %get-tuple-element.125) | copy-start | bytes 147460 | tf_op jit(solution)/shard_map/cond
  370.1 5.1 %copy-start.53 = (f32[192,64]{1,0:T(8,128)S(1)}, f32[192,64]{1,0:T(8,128)}, u32[]{:S(2)}) copy-start(f32[192,64]{1,0:T(8,128)} %get-tuple-element.131) | copy-start | bytes 147460 | tf_op jit(solution)/shard_map/cond
  370.1 5.1 %copy-start.54 = (f32[192,64]{1,0:T(8,128)S(1)}, f32[192,64]{1,0:T(8,128)}, u32[]{:S(2)}) copy-start(f32[192,64]{1,0:T(8,128)} %get-tuple-element.132) | copy-start | bytes 147460 | tf_op jit(solution)/shard_map/cond
  390.4 5.9 %collective-permute-start.74 = (f32[8,16,128]{2,1,0:T(8,128)S(1)}, f32[8,16,128]{2,1,0:T(8,128)S(1)}, u32[]{:S(2)}, u32[]{:S(2)}) collective-permute-start(f32[8,16,128]{2,1,0:T(8,128)S(1)} %get-tuple-element.271), channel_id=1, source_target_pairs={{0,4},{4,0},{8,12},{12,8},{1,5},{5,1},{9,13},{13,9},{2,6},{6,2},{1... | collective-permute-start | bytes 196616 | tf_op jit(solution)/shard_map/ppermute | solution.py:47
  393.6 8.4 %collective-permute-start.75 = (f32[8,16,128]{2,1,0:T(8,128)S(1)}, f32[8,16,128]{2,1,0:T(8,128)S(1)}, u32[]{:S(2)}, u32[]{:S(2)}) collective-permute-start(f32[8,16,128]{2,1,0:T(8,128)S(1)} %get-tuple-element.273), channel_id=1, source_target_pairs={{0,8},{4,12},{8,0},{12,4},{1,9},{5,13},{9,1},{13,5},{2,10},{6,14},... | collective-permute-start | bytes 196616 | tf_op jit(solution)/shard_map/ppermute | solution.py:47
  394.7 7.3 %collective-permute-start.76 = (f32[8,16,128]{2,1,0:T(8,128)S(1)}, f32[8,16,128]{2,1,0:T(8,128)S(1)}, u32[]{:S(2)}, u32[]{:S(2)}) collective-permute-start(f32[8,16,128]{2,1,0:T(8,128)S(1)} %get-tuple-element.272), channel_id=1, source_target_pairs={{0,12},{4,8},{8,4},{12,0},{1,13},{5,9},{9,5},{13,1},{2,14},{6,10},... | collective-permute-start | bytes 196616 | tf_op jit(solution)/shard_map/ppermute | solution.py:47
  403.7 2.7 collective-permute-start.77
  403.7 6.4 %collective-permute-start.78 = (f32[8,16,192]{2,1,0:T(8,128)S(1)}, f32[8,16,192]{2,1,0:T(8,128)S(1)}, u32[]{:S(2)}, u32[]{:S(2)}) collective-permute-start(f32[8,16,192]{2,1,0:T(8,128)S(1)} %pad_maximum_fusion.12), channel_id=1, source_target_pairs={{0,2},{1,3},{2,0},{3,1},{4,6},{5,7},{6,4},{7,5},{8,10},{9,11},{10,... | collective-permute-start | bytes 294920 | tf_op jit(solution)/shard_map/ppermute | solution.py:47
  405.3 6.7 %collective-permute-start.79 = (f32[8,16,192]{2,1,0:T(8,128)S(1)}, f32[8,16,192]{2,1,0:T(8,128)S(1)}, u32[]{:S(2)}, u32[]{:S(2)}) collective-permute-start(f32[8,16,192]{2,1,0:T(8,128)S(1)} %pad_maximum_fusion.12), channel_id=1, source_target_pairs={{0,3},{1,2},{2,1},{3,0},{4,7},{5,6},{6,5},{7,4},{8,11},{9,10},{10,... | collective-permute-start | bytes 294920 | tf_op jit(solution)/shard_map/ppermute | solution.py:47
  414.9 1.9 collective-permute-start.80
  415.2 3.6 collective-permute-start.81
  416.7 3.0 collective-permute-start.82
  419.7 4.4 %collective-permute-start.83 = (f32[8,128]{1,0:T(8,128)S(1)}, f32[8,128]{1,0:T(8,128)S(1)}, u32[]{:S(2)}, u32[]{:S(2)}) collective-permute-start(f32[8,128]{1,0:T(8,128)S(1)} %add_add_fusion.5), channel_id=1, source_target_pairs={{0,4},{4,0},{8,12},{12,8},{1,5},{5,1},{9,13},{13,9},{2,6},{6,2},{1... | collective-permute-start | bytes 12296 | tf_op jit(solution)/shard_map/ppermute | solution.py:47
  421.3 4.5 %collective-permute-start.84 = (f32[8,128]{1,0:T(8,128)S(1)}, f32[8,128]{1,0:T(8,128)S(1)}, u32[]{:S(2)}, u32[]{:S(2)}) collective-permute-start(f32[8,128]{1,0:T(8,128)S(1)} %add_add_fusion.5), channel_id=1, source_target_pairs={{0,8},{4,12},{8,0},{12,4},{1,9},{5,13},{9,1},{13,5},{2,10},{6,14},... | collective-permute-start | bytes 12296 | tf_op jit(solution)/shard_map/ppermute | solution.py:47
  422.5 5.4 %collective-permute-start.85 = (f32[8,128]{1,0:T(8,128)S(1)}, f32[8,128]{1,0:T(8,128)S(1)}, u32[]{:S(2)}, u32[]{:S(2)}) collective-permute-start(f32[8,128]{1,0:T(8,128)S(1)} %add_add_fusion.5), channel_id=1, source_target_pairs={{0,12},{4,8},{8,4},{12,0},{1,13},{5,9},{9,5},{13,1},{2,14},{6,10},... | collective-permute-start | bytes 12296 | tf_op jit(solution)/shard_map/ppermute | solution.py:47
  (7 other events, 6.5 us)
Sparse Core Ops, SparseCore 0:
  47.2 38.9 all-gather.18
  87.8 35.9 all-gather.16
  125.4 35.9 all-gather.14
  162.8 31.6 all-gather.12
